TPU v7x, 32 devices: a whole 2x2x4 slice. The times are simulated.
32 devices in a mesh: batch: 4 (over z), ty: 2 (over y), tx: 4 (over x, core).
Axes of the slice: x: 2, y: 2, z: 4, core: 2. Of those that a mesh axis runs over, the one named last changes fastest.
Arguments:
- tokens: bfloat16 [96, 16, 16, 768], P('batch', 'ty', 'tx'), may hold values from -6 to 6
- skip_tokens: bfloat16 [96, 16, 16, 768], P('batch', 'ty', 'tx'), may hold values from -6 to 6
- extra_tokens: bfloat16 [96, 2, 768], P('batch'), may hold values from -6 to 6
- extra_skip: bfloat16 [96, 2, 768], P('batch'), may hold values from -6 to 6
- timesteps: int32 [96], P('batch'), may hold values from 0 to 999, as said below
- target: float32 [96, 32, 32, 4], P('batch', 'ty', 'tx'), may hold values from -6 to 6
- w_skip: bfloat16 [1536, 768], replicated, may hold values from -0.15625 to 0.15625
- b_skip: bfloat16 [768], replicated, may hold values from -3 to 3
- norm1_gain: bfloat16 [768], replicated, may hold values from 0.5 to 1.5
- norm1_shift: bfloat16 [768], replicated, may hold values from -2 to 2
- w_qkv: bfloat16 [768, 2304], replicated, may hold values from -0.3125 to 0.3125
- w_out: bfloat16 [768, 768], replicated, may hold values from -0.875 to 0.875
- b_out: bfloat16 [768], replicated, may hold values from -3 to 3
- norm2_gain: bfloat16 [768], replicated, may hold values from 0.5 to 1.5
- norm2_shift: bfloat16 [768], replicated, may hold values from -2 to 2
- w_up: bfloat16 [768, 3072], replicated, may hold values from -0.21875 to 0.21875
- b_up: bfloat16 [3072], replicated, may hold values from -3 to 3
- w_down: bfloat16 [3072, 768], replicated, may hold values from -0.109375 to 0.109375
- b_down: bfloat16 [768], replicated, may hold values from -3 to 3
- final_gain: bfloat16 [768], replicated, may hold values from 0.5 to 1.5
- final_shift: bfloat16 [768], replicated, may hold values from -2 to 2
- w_head: bfloat16 [768, 16], replicated, may hold values from -0.21875 to 0.21875
- b_head: bfloat16 [16], replicated, may hold values from -3 to 3
- w_conv: bfloat16 [3, 3, 4, 4], replicated, may hold values from -1 to 1
- b_conv: bfloat16 [4], replicated, may hold values from -3 to 3
Outputs:
- latent_out: bfloat16 [96, 32, 32, 4], P('batch', 'ty', 'tx')
- grad_tokens: bfloat16 [96, 16, 16, 768], P('batch', 'ty', 'tx')
- grad_skip_tokens: bfloat16 [96, 16, 16, 768], P('batch', 'ty', 'tx')
- grad_extra_tokens: bfloat16 [96, 2, 768], P('batch')
- grad_extra_skip: bfloat16 [96, 2, 768], P('batch')
- grad_w_skip: float32 [1536, 768], P(('batch', 'ty', 'tx'))
- grad_b_skip: float32 [768], P(('batch', 'ty', 'tx'))
- grad_norm1_gain: float32 [768], P(('batch', 'ty', 'tx'))
- grad_norm1_shift: float32 [768], P(('batch', 'ty', 'tx'))
- grad_w_qkv: float32 [768, 2304], P(('batch', 'ty', 'tx'))
- grad_w_out: float32 [768, 768], P(('batch', 'ty', 'tx'))
- grad_b_out: float32 [768], P(('batch', 'ty', 'tx'))
- grad_norm2_gain: float32 [768], P(('batch', 'ty', 'tx'))
- grad_norm2_shift: float32 [768], P(('batch', 'ty', 'tx'))
- grad_w_up: float32 [768, 3072], P(('batch', 'ty', 'tx'))
- grad_b_up: float32 [3072], P(('batch', 'ty', 'tx'))
- grad_w_down: float32 [3072, 768], P(('batch', 'ty', 'tx'))
- grad_b_down: float32 [768], P(('batch', 'ty', 'tx'))
- grad_final_gain: float32 [768], P(('batch', 'ty', 'tx'))
- grad_final_shift: float32 [768], P(('batch', 'ty', 'tx'))
- grad_w_head: float32 [768, 16], P(('batch', 'ty', 'tx'))
- grad_b_head: float32 [16], replicated
- grad_w_conv: float32 [3, 3, 4, 4], replicated
- grad_b_conv: float32 [4], replicated
Inputs may be any that keep to these rules, and one draw needn't show every extreme that they name: `timesteps`: diffusion steps lean toward high noise.
All inputs are finite; a program needn't handle non-finite values.
Results may differ from a plain program's by a relative error of at most 0.014.
Values may be sent and summed in bfloat16 or wider, within the bound.
No kernel may reach another device: no remote copies, remote signals or barrier semaphores. Data moves between devices by JAX's collectives and lax.ppermute only.
A program may use at most 192 MiB of HBM per device.

v0:
```python
import functools

import jax
import jax.numpy as jnp
import numpy as np
from jax import lax
from jax.experimental import pallas as pl
from jax.experimental.pallas import tpu as pltpu
from jax.sharding import PartitionSpec as P

HEADS = 12
PATCH = 2
EXTRA_PAD = 8
CHAIN_DOWN = True
EPS = 1e-05
BF = jnp.bfloat16
F32 = jnp.float32
PLANE = ("ty", "tx")
ALL = ("batch", "ty", "tx")
MIB = 1024 * 1024


def dot(left, right, left_dim, right_dim):
    return lax.dot_general(
        left, right, (((left_dim,), (right_dim,)), ((), ())), preferred_element_type=F32
    )


def norm_parts(values):
    center = values - jnp.mean(values, -1, keepdims=True)
    scaled = lax.rsqrt(jnp.mean(center * center, -1, keepdims=True) + EPS)
    return center * scaled, scaled


def norm_back(inner, normed, scaled):
    return scaled * (
        inner
        - jnp.mean(inner, -1, keepdims=True)
        - normed * jnp.mean(inner * normed, -1, keepdims=True)
    )


def flat(ref):
    return ref[...].astype(F32).reshape(1, -1)


def row_sum(values):
    return jnp.sum(values, 0, keepdims=True)


def gelu_parts(upper):
    spread = 0.5 + 0.5 * lax.erf(upper * np.float32(0.5**0.5))
    bell = jnp.exp(upper * upper * -0.5) * np.float32((2 * np.pi) ** -0.5)
    return upper * spread, spread + upper * bell


def noise_weight(timesteps):
    frac = (timesteps.astype(F32) / 1000.0 + 0.008) / 1.008
    kept = jnp.cos(frac * (0.5 * jnp.pi)) ** 2
    return jnp.minimum(1.0, 5.0 * (1.0 - kept) / kept)


def can_split(own):
    return own % 8 == 0


def store_split(value, own, lane_refs):
    if len(lane_refs) == 1:
        lane_refs[0][...] = value.astype(BF)
        return
    keep_ref, send_ref, core_ref = lane_refs
    pairs = value.reshape(value.shape[0] // (2 * own), 2, own, value.shape[1])
    first = core_ref[0] == 0
    keep = jnp.where(first, pairs[:, 0], pairs[:, 1])
    send = jnp.where(first, pairs[:, 1], pairs[:, 0])
    keep_ref[...] = keep.astype(BF)
    send_ref[...] = send.astype(BF)


def merge_kernel(tokens_ref, skip_ref, w_skip_ref, b_skip_ref, hidden_ref, joined_ref):
    width = w_skip_ref.shape[1]
    local = tokens_ref.shape[1] * tokens_ref.shape[2]
    body = tokens_ref[...].reshape(-1, width)
    body_skip = skip_ref[...].reshape(-1, width)
    hidden = (
        dot(body, w_skip_ref[:width], 1, 0)
        + dot(body_skip, w_skip_ref[width:], 1, 0)
        + b_skip_ref[...].astype(F32).reshape(1, width)
    )
    hidden_ref[...] = hidden.astype(BF).reshape(-1, local, width)
    joined_ref[:, :local] = body.reshape(-1, local, width)
    joined_ref[:, local : 2 * local] = body_skip.reshape(-1, local, width)


def attend_kernel(
    hidden_ref,
    key_extra_ref,
    value_extra_ref,
    gain_ref,
    shift_ref,
    b_out_ref,
    w_qkv_ref,
    w_out_ref,
    normed_ref,
    qkv_ref,
    probs_ref,
    probs_extra_ref,
    mixed_ref,
    hidden1_ref,
    scores_ref,
    scores_extra_ref,
):
    width = w_out_ref.shape[0]
    head_dim = width // HEADS
    scale = head_dim ** (-0.5)
    rows = hidden_ref.shape[0] * hidden_ref.shape[2]
    hidden = hidden_ref[...].reshape(rows, width).astype(F32)
    unit, _ = norm_parts(hidden)
    normed = (unit * flat(gain_ref) + flat(shift_ref)).astype(BF)
    normed_ref[0] = normed
    qkv_ref[0] = dot(w_qkv_ref[...], normed, 0, 1).astype(BF)
    live = lax.broadcasted_iota(jnp.int32, (EXTRA_PAD, rows), 0) < 2
    for head in range(HEADS):
        low = head * head_dim
        query = qkv_ref[0, low : low + head_dim, :]
        key = qkv_ref[0, width + low : width + low + head_dim, :]
        scores_ref[head] = dot(key, query, 0, 0) * scale
        scores_extra = dot(key_extra_ref[0, head], query, 1, 0) * scale
        scores_extra_ref[head] = jnp.where(live, scores_extra, -1e30)
    for head in range(HEADS):
        scores, scores_extra = scores_ref[head], scores_extra_ref[head]
        top = jnp.maximum(
            jnp.max(scores, 0, keepdims=True), jnp.max(scores_extra, 0, keepdims=True)
        )
        raised = jnp.exp(scores - top)
        raised_extra = jnp.exp(scores_extra - top)
        share = 1.0 / (row_sum(raised) + row_sum(raised_extra))
        probs_ref[0, head] = (raised * share).astype(BF)
        probs_extra_ref[0, head] = (raised_extra * share).astype(BF)
    for head in range(HEADS):
        low = head * head_dim
        value = qkv_ref[0, 2 * width + low : 2 * width + low + head_dim, :]
        mixed = dot(value, probs_ref[0, head], 1, 0) + dot(
            value_extra_ref[0, head], probs_extra_ref[0, head], 0, 0
        )
        mixed_ref[0, low : low + head_dim, :] = mixed.astype(BF)
    hidden1_ref[0] = hidden + (dot(mixed_ref[0], w_out_ref[...], 0, 0) + flat(b_out_ref))


def forward_kernel(
    hidden1_ref,
    gain2_ref,
    shift2_ref,
    b_up_ref,
    b_down_ref,
    w_up_ref,
    w_down_ref,
    active_ref,
    slope_ref,
    normed2_ref,
    total,
    up_rows,
):
    step = pl.program_id(0)

    @pl.when(step == 0)
    def _():
        unit, _ = norm_parts(hidden1_ref[...])
        b_up = flat(b_up_ref)
        width = up_rows.shape[1]
        for j in range(up_rows.shape[0]):
            up_rows[j : j + 1] = b_up[:, j * width : (j + 1) * width]
        normed2_ref[...] = (unit * flat(gain2_ref) + flat(shift2_ref)).astype(BF)

    count = normed2_ref.shape[0]
    blocks = 3 if count % 48 == 0 else 1
    size = count // blocks
    rows = [slice(i * size, (i + 1) * size) for i in range(blocks)]

    def raise_rows(i):
        return dot(normed2_ref[rows[i]], w_up_ref[...], 1, 0) + up_rows[pl.ds(step, 1)]

    def activate(upper, i):
        active, slope = gelu_parts(upper)
        active = active.astype(BF)
        active_ref[0, rows[i]] = active
        slope_ref[0, rows[i]] = slope.astype(BF)
        return active

    def lower(active, i):
        part = dot(active, w_down_ref[...], 1, 0)
        base = jnp.where(step == 0, hidden1_ref[rows[i]] + flat(b_down_ref), total[rows[i]])
        total[rows[i]] = base + part

    upper = raise_rows(0)
    for i in range(blocks):
        following = raise_rows(i + 1) if i + 1 < blocks else None
        active = activate(upper, i)
        upper = following
        lower(active, i)


def turn_kernel(
    tile_rows,
    tile_cols,
    tiles_x,
    hidden2_ref,
    gainf_ref,
    shiftf_ref,
    w_head_ref,
    w_conv_ref,
    lanes_ref,
    target_ref,
    after_ref,
    result_ref,
    grad_hidden2_ref,
    grad_down_ref,
    grad_head_ref,
    sums_ref,
    head_sum_ref,
    conv_sum_ref,
    conv_bias_ref,
    total,
):
    per_item, lanes = target_ref.shape
    patch_values, width = w_head_ref.shape
    items = lanes // patch_values

    def head_of(i):
        parts = [w_head_ref[...]]
        if i > 0:
            parts = [jnp.zeros((i * patch_values, width), BF)] + parts
        if i < items - 1:
            parts = parts + [jnp.zeros((lanes - (i + 1) * patch_values, width), BF)]
        return jnp.concatenate(parts, 0)

    heads = [head_of(i) for i in range(items)]
    unit, scaled = norm_parts(hidden2_ref[...])
    total[...] = unit
    normedf = (unit * flat(gainf_ref) + flat(shiftf_ref)).astype(BF)
    normed2_final = [normedf[i * per_item : (i + 1) * per_item] for i in range(items)]
    patches = lanes_ref[0:1]
    for i in range(items):
        patches = patches + dot(normed2_final[i], heads[i], 1, 1)
    patches = patches.astype(BF)

    def place(position):
        tile = position // (tile_rows * tile_cols)
        row = (tile // tiles_x) * tile_rows + (position // tile_cols) % tile_rows
        col = (tile % tiles_x) * tile_cols + position % tile_cols
        return row * 1024 + col

    own = place(lax.broadcasted_iota(jnp.int32, (per_item, 1), 0))
    other = place(lax.broadcasted_iota(jnp.int32, (1, per_item), 1))
    shifts = []
    for row_off in range(3):
        for col_off in range(3):
            wanted = own + ((row_off - 1) * 1024 + (col_off - 1))
            shifts.append(jnp.where(wanted == other, 1.0, 0.0).astype(BF))
    windows = [dot(shift, patches, 1, 0).astype(BF) for shift in shifts]
    result = lanes_ref[1:2]
    for k in range(9):
        result = result + dot(windows[k], w_conv_ref[k], 1, 0)
    result_ref[...] = result.astype(BF)
    grad_result = (lanes_ref[2:3] * (result - target_ref[...])).astype(BF)
    conv_bias_ref[...] = row_sum(grad_result.astype(F32))
    grad_patches = jnp.zeros(target_ref.shape, F32)
    for k in range(9):
        conv_sum_ref[k] = dot(windows[k], grad_result, 0, 0)
        moved = dot(shifts[8 - k], grad_result, 1, 0).astype(BF)
        grad_patches = grad_patches + dot(moved, w_conv_ref[k], 1, 1)
    grad_patches = grad_patches.astype(BF)
    grad_head_ref[...] = row_sum(grad_patches.astype(F32))
    sum_gain = jnp.zeros((1, unit.shape[1]), F32)
    sum_shift = sum_gain
    sum_down = sum_gain
    for i in range(items):
        rows = slice(i * per_item, (i + 1) * per_item)
        head_sum_ref[i] = dot(grad_patches, normed2_final[i], 0, 0)
        grad_normedf = dot(grad_patches, heads[i], 1, 0)
        unit_part = total[rows]
        sum_gain = sum_gain + row_sum(grad_normedf * unit_part)
        sum_shift = sum_shift + row_sum(grad_normedf)
        grad_hidden2 = norm_back(grad_normedf * flat(gainf_ref), unit_part, scaled[rows])
        grad_hidden2_ref[rows] = grad_hidden2
        grad_down = grad_hidden2.astype(BF)
        grad_down_ref[rows] = grad_down
        sum_down = sum_down + row_sum(grad_down.astype(F32))
    sums_ref[0:1] = sum_gain
    sums_ref[1:2] = sum_shift
    sums_ref[2:3] = sum_down


def down_kernel(own, split, active_ref, grad_down_ref, core_ref, *outs):
    total = dot(active_ref[0], grad_down_ref[...], 0, 0)
    if not split:
        outs[0][...] = total.astype(BF)
        return
    pairs = total.reshape(total.shape[0] // (8 * own), 2, 4, own, total.shape[1])
    first = core_ref[0] == 0
    half = total.shape[1] // 2
    for part in range(4):
        low, high = pairs[:, 0, part], pairs[:, 1, part]
        keep = jnp.where(first, low, high).astype(BF)
        send = jnp.where(first, high, low).astype(BF)
        for side in range(2):
            cols = slice(side * half, (side + 1) * half)
            outs[0][2 * part + side] = keep[:, :, cols]
            outs[1][2 * part + side] = send[:, :, cols]


def up_kernel(
    own,
    slope_ref,
    grad_down_ref,
    w_down_ref,
    w_up_ref,
    normed2_ref,
    hidden1_ref,
    gain2_ref,
    grad_hidden2_ref,
    mixed_ref,
    core_ref,
    *rest,
):
    total = rest[-1]
    rest = rest[-7 if can_split(own) else -6 : -1]
    grad_b_up_ref, grad_hidden1_ref, grad_branch_ref, sums_ref = rest[:4]
    rest = rest[4:]
    step = pl.program_id(0)
    steps = pl.num_programs(0)

    def store(value):
        half = value.shape[1] // 2
        for side in range(2):
            piece = value[:, side * half : (side + 1) * half]
            if can_split(own):
                store_split(piece, own, (rest[0].at[side], rest[1].at[side], core_ref))
            else:
                store_split(piece, own, (rest[0].at[side],))

    @pl.when(step < steps - 1)
    def _():
        grad_active = dot(grad_down_ref[...], w_down_ref[...], 1, 1)
        grad_upper = (grad_active * slope_ref[0].astype(F32)).astype(BF)
        grad_b_up_ref[0, 0:1] = row_sum(grad_upper.astype(F32))
        store(dot(normed2_ref[...], grad_upper, 0, 0))
        part = dot(grad_upper, w_up_ref[...], 1, 1)

        @pl.when(step == 0)
        def _():
            total[...] = part

        @pl.when(step > 0)
        def _():
            total[...] += part

    @pl.when(step == steps - 1)
    def _():
        unit, scaled = norm_parts(hidden1_ref[...])
        grad_normed2 = total[...]
        sums_ref[0:1] = row_sum(grad_normed2 * unit)
        sums_ref[1:2] = row_sum(grad_normed2)
        grad_hidden1 = grad_hidden2_ref[...] + norm_back(
            grad_normed2 * flat(gain2_ref), unit, scaled
        )
        grad_hidden1_ref[...] = grad_hidden1
        grad_branch = grad_hidden1.astype(BF)
        grad_branch_ref[...] = grad_branch
        sums_ref[2:3] = row_sum(grad_branch.astype(F32))
        items, _, per_item = mixed_ref.shape
        value = dot(mixed_ref[0], grad_branch[:per_item], 1, 0)
        for item in range(1, items):
            rows = slice(item * per_item, (item + 1) * per_item)
            value = value + dot(mixed_ref[item], grad_branch[rows], 1, 0)
        store(value)


def attend_back_kernel(
    hidden_ref,
    grad_hidden1_ref,
    grad_branch_ref,
    qkv_ref,
    probs_ref,
    probs_extra_ref,
    key_extra_ref,
    value_extra_ref,
    gain_ref,
    w_qkv_ref,
    w_out_ref,
    sums_in_ref,
    *rest,
):
    (
        grad_qkv_ref,
        grad_key_extra_ref,
        grad_value_extra_ref,
        grad_hidden0_ref,
        sums_ref,
        grad_mixed_ref,
        grad_probs_ref,
        grad_probs_extra_ref,
        grad_scores_ref,
        grad_scores_extra_ref,
    ) = rest[-10:]
    width = w_out_ref.shape[0]
    head_dim = width // HEADS
    scale = head_dim ** (-0.5)
    rows = hidden_ref.shape[0] * hidden_ref.shape[2]
    grad_mixed_ref[...] = dot(w_out_ref[...], grad_branch_ref[0], 1, 1).astype(BF)
    for head in range(HEADS):
        low = head * head_dim
        value = qkv_ref[0, 2 * width + low : 2 * width + low + head_dim, :]
        grad_mixed = grad_mixed_ref[low : low + head_dim, :]
        grad_probs_ref[head] = dot(value, grad_mixed, 0, 0)
        grad_probs_extra_ref[head] = dot(value_extra_ref[0, head], grad_mixed, 1, 0)
    for head in range(HEADS):
        probs = probs_ref[0, head].astype(F32)
        probs_extra = probs_extra_ref[0, head].astype(F32)
        grad_probs, grad_probs_extra = grad_probs_ref[head], grad_probs_extra_ref[head]
        common = row_sum(grad_probs * probs) + row_sum(grad_probs_extra * probs_extra)
        grad_scores_ref[head] = (probs * (grad_probs - common)).astype(BF)
        grad_scores_extra_ref[head] = (probs_extra * (grad_probs_extra - common)).astype(BF)
    for head in range(HEADS):
        low = head * head_dim
        query = qkv_ref[0, low : low + head_dim, :]
        key = qkv_ref[0, width + low : width + low + head_dim, :]
        grad_mixed = grad_mixed_ref[low : low + head_dim, :]
        grad_scores, grad_scores_extra = grad_scores_ref[head], grad_scores_extra_ref[head]
        grad_query = dot(key, grad_scores, 1, 0) + dot(
            key_extra_ref[0, head], grad_scores_extra, 0, 0
        )
        grad_key = dot(query, grad_scores, 1, 1)
        grad_value = dot(grad_mixed, probs_ref[0, head], 1, 1)
        grad_key_extra_ref[0, head] = dot(grad_scores_extra, query, 1, 1) * scale
        grad_value_extra_ref[0, head] = dot(probs_extra_ref[0, head], grad_mixed, 1, 1)
        grad_qkv_ref[0, low : low + head_dim, :] = (grad_query * scale).astype(BF)
        grad_qkv_ref[0, width + low : width + low + head_dim, :] = (grad_key * scale).astype(BF)
        grad_qkv_ref[0, 2 * width + low : 2 * width + low + head_dim, :] = grad_value.astype(BF)
    grad_normed = dot(grad_qkv_ref[0], w_qkv_ref[...], 0, 1)
    unit, scaled = norm_parts(hidden_ref[...].reshape(rows, width).astype(F32))

    @pl.when(pl.program_id(0) == 0)
    def _():
        sums_ref[...] = sums_in_ref[...]

    sums_ref[0:1] += row_sum(grad_normed * unit)
    sums_ref[1:2] += row_sum(grad_normed)
    grad_hidden0 = grad_hidden1_ref[0] + norm_back(grad_normed * flat(gain_ref), unit, scaled)
    grad_low = grad_hidden0.astype(BF)
    sums_ref[2:3] += row_sum(grad_low.astype(F32))
    grad_hidden0_ref[...] = grad_low.reshape(grad_hidden0_ref.shape)


def extra_back_kernel(
    share,
    hidden_ref,
    gain_ref,
    w_key_ref,
    w_value_ref,
    latent_ref,
    sums_in_ref,
    *rest,
):
    keys, values = rest[:share], rest[share : 2 * share]
    pairs_ref, grad_ref, sums_ref, back_ref = rest[-4:]
    width = hidden_ref.shape[1]

    def rows_of(refs):
        return jnp.concatenate(
            [jnp.concatenate([ref[0, head] for ref in refs], 0) for head in range(HEADS)], 1
        ).astype(BF)

    grad_key, grad_value = rows_of(keys), rows_of(values)
    pairs_ref[0] = grad_key
    pairs_ref[1] = grad_value
    grad_normed = dot(grad_key, w_key_ref[...], 1, 1) + dot(grad_value, w_value_ref[...], 1, 1)
    unit, scaled = norm_parts(hidden_ref[...])
    grad = norm_back(grad_normed * flat(gain_ref), unit, scaled).astype(BF)
    grad_ref[...] = grad
    wide = grad.astype(F32)
    sums_ref[0:1] = sums_in_ref[0:1] + row_sum(grad_normed * unit)
    sums_ref[1:2] = sums_in_ref[1:2] + row_sum(grad_normed)
    sums_ref[2:3] = sums_in_ref[2:3] + row_sum(wide)
    real = [wide[i * EXTRA_PAD : i * EXTRA_PAD + 2] for i in range(share)]
    fill = back_ref.shape[1] - 2 * share - latent_ref.shape[1]
    for group in range(back_ref.shape[0]):
        block = real + [latent_ref[group].astype(F32), jnp.zeros((fill, width), F32)]
        back_ref[group] = jnp.concatenate(block, 0).astype(BF)


def late_weight_kernel(
    own,
    normed_ref,
    normed_extra_ref,
    pairs_ref,
    joined_ref,
    grad_ref,
    joined_extra_ref,
    grad_extra_ref,
    grad_qkv_0_ref,
    grad_qkv_1_ref,
    grad_qkv_2_ref,
    core_ref,
    *rest,
):
    step = pl.program_id(0)
    split = can_split(own)
    groups, items, _, width = joined_ref.shape
    local = (grad_ref.shape[1] - 16) // items

    @pl.when(step < 3)
    def _():
        total = dot(normed_extra_ref[...], pairs_ref[0], 0, 0)
        total = total * jnp.where(step == 0, 0.0, 1.0)
        for item, ref in enumerate((grad_qkv_0_ref, grad_qkv_1_ref, grad_qkv_2_ref)):
            total = total + dot(normed_ref[item], ref[0], 0, 1)
        half = width // 2
        for side in range(2):
            piece = total[:, side * half : (side + 1) * half]
            if split:
                store_split(piece, own, (rest[-2].at[side], rest[-1].at[side], core_ref))
            else:
                store_split(piece, own, (rest[-1].at[side],))

    @pl.when(step >= 3)
    def _():
        grad = grad_ref[:, : items * local].reshape(groups * items * local, -1)
        for side in range(2):
            joined = joined_ref[:, :, side * local : (side + 1) * local]
            joined = joined.reshape(groups * items * local, width)
            extra = joined_extra_ref[:, side * width : (side + 1) * width]
            total = dot(joined, grad, 0, 0) + dot(extra, grad_extra_ref[...], 0, 0)
            if not split:
                rest[-1][side] = total.astype(BF)
                continue
            pairs = total.reshape(width // (4 * own), 2, 2, own, total.shape[1])
            first = core_ref[0] == 0
            count = pairs.shape[0]
            for part in range(2):
                low, high = pairs[:, 0, part], pairs[:, 1, part]
                where = pl.ds(side * count, count)
                rest[-2][part, where] = jnp.where(first, low, high).astype(BF)
                rest[-1][part, where] = jnp.where(first, high, low).astype(BF)


def token_kernel(back_ref, w_skip_ref, tokens_ref, skip_ref, extra_ref):
    width = w_skip_ref.shape[1]
    items = tokens_ref.shape[0]
    local = tokens_ref.shape[1] * tokens_ref.shape[2]
    body = items // back_ref.shape[0] * local
    grad = back_ref[:, :body].reshape(items * local, width)
    tokens_ref[...] = dot(grad, w_skip_ref[:width], 1, 1).astype(BF).reshape(tokens_ref.shape)
    skip_ref[...] = dot(grad, w_skip_ref[width:], 1, 1).astype(BF).reshape(skip_ref.shape)
    extra = back_ref[:, body:].reshape(-1, width)
    extra_ref[...] = dot(extra, w_skip_ref[...], 1, 1).astype(BF).reshape(extra_ref.shape)


def fold_matrix(shape, low, wide, period):
    row = lax.broadcasted_iota(jnp.int32, shape, 0)
    col = lax.broadcasted_iota(jnp.int32, shape, 1)
    return jnp.where((col >= low) & (col < low + wide) & (row % period == col - low), 1.0, 0.0)


def pack_kernel(
    sums_attend_ref,
    sums_up_ref,
    sums_final_ref,
    head_sum_ref,
    grad_head_ref,
    conv_sum_ref,
    conv_bias_ref,
    table_ref,
    *rest,
):
    stacked_ref, shared_ref = rest[-2:]
    items, lanes, _ = head_sum_ref.shape
    values = lanes // items
    exact = functools.partial(
        jnp.dot, precision=lax.Precision.HIGHEST, preferred_element_type=F32
    )
    stacked_ref[0:1] = sums_attend_ref[2:3]
    stacked_ref[1:2] = sums_attend_ref[0:1]
    stacked_ref[2:3] = sums_attend_ref[1:2]
    stacked_ref[3:4] = sums_up_ref[2:3]
    stacked_ref[4:6] = sums_up_ref[0:2]
    stacked_ref[6:7] = sums_final_ref[2:3]
    stacked_ref[7:9] = sums_final_ref[0:2]
    head = head_sum_ref[0, 0:values]
    for item in range(1, items):
        head = head + head_sum_ref[item, item * values : (item + 1) * values]
    stacked_ref[9 : 9 + values] = head
    row = lax.broadcasted_iota(jnp.int32, (8, lanes), 0)
    col = lax.broadcasted_iota(jnp.int32, (8, lanes), 1)
    left = jnp.where(col % 4 == row, 1.0, 0.0)
    shared = jnp.zeros((8, 128), F32)
    for tap in range(9):
        picked = conv_sum_ref[0] * table_ref[0, tap].astype(F32)
        for k in range(1, 9):
            picked = picked + conv_sum_ref[k] * table_ref[k, tap].astype(F32)
        shared = shared + exact(exact(left, picked), fold_matrix((lanes, 128), 4 * tap, 4, 4))
    bias = exact(grad_head_ref[...], fold_matrix((lanes, 128), 64, values, values))
    bias = bias + exact(conv_bias_ref[...], fold_matrix((lanes, 128), 96, 4, 4))
    first = lax.broadcasted_iota(jnp.int32, (8, 128), 0) == 0
    shared_ref[...] = shared + jnp.where(first, bias, 0.0)


def whole(shape):
    return pl.BlockSpec(shape, lambda *_: (0,) * len(shape), pipeline_mode=pl.Buffered(1))


def params():
    return pltpu.CompilerParams(vmem_limit_bytes=60 * MIB)


def cost(flops, moved, transcendentals=0):
    del flops, moved, transcendentals
    return pl.CostEstimate(flops=1024, bytes_accessed=1024, transcendentals=0)


def sds(shape, dtype):
    return jax.ShapeDtypeStruct(shape, dtype)


def swap(block, axis, gap):
    count = lax.axis_size(axis)
    return lax.ppermute(block, axis, [(i, i ^ gap) for i in range(count)])


def serve_kernel(tasks, places_ref, *refs):
    del places_ref
    inputs = sum(len(parts) for task in tasks for parts in task["sides"])
    outs = refs[len(refs) - sum(len(task["outs"]) for task in tasks) :]
    at, out_at = 0, 0
    del inputs
    for task in tasks:
        values = []
        for parts in task["sides"]:
            total = refs[at][...].astype(F32)
            for k in range(1, len(parts)):
                total = total + refs[at + k][...].astype(F32)
            at += len(parts)
            values.append(total)
        task["emit"](values, outs[out_at : out_at + len(task["outs"])])
        out_at += len(task["outs"])


def serve(tasks, after, name, places):
    arrays, specs = [], []
    for task in tasks:
        for parts in task["sides"]:
            for array, starts, sizes in parts:
                index = tuple(
                    start // size if isinstance(start, int) else start
                    for start, size in zip(starts, sizes, strict=True)
                )

                def where(_, ref, index=index):
                    return tuple(i if isinstance(i, int) else ref[i[0]] for i in index)

                arrays.append(array)
                specs.append(pl.BlockSpec(tuple(sizes), where))
    outs = [out for task in tasks for out in task["outs"]]
    moved = sum(2 * int(np.prod(spec.block_shape)) for spec in specs)
    return pl.pallas_call(
        functools.partial(serve_kernel, tasks),
        grid_spec=pltpu.PrefetchScalarGridSpec(
            num_scalar_prefetch=1,
            grid=(1,),
            in_specs=specs + [pl.BlockSpec(memory_space=pl.ANY)] * len(after),
            out_specs=[
                pl.BlockSpec(out.shape, lambda _, ref, n=len(out.shape): (0,) * n) for out in outs
            ],
        ),
        out_shape=outs,
        compiler_params=params(),
        cost_estimate=cost(moved, 2 * moved),
        name=name,
    )(places, *arrays, *after)


def emit_low(values, outs):
    for value, out in zip(values, outs, strict=True):
        out[...] = value.astype(BF)


def place_table():
    own = [lax.axis_index("ty"), lax.axis_index("tx") // 2]
    batch = lax.axis_size("batch")
    own += [(lax.axis_index("batch") >> bit) % 2 for bit in range(batch.bit_length() - 1)]
    return jnp.stack([v for place in own for v in (place, 1 - place)]).astype(jnp.int32)


class Sum:
    def __init__(self, grads, units, inner, columns, table):
        batch = lax.axis_size("batch")
        bits = batch.bit_length() - 1
        rows = sum(grad.size for grad in grads) // (units * columns)
        self.own = rows // lax.axis_size(ALL) // inner
        self.columns = columns
        self.table = table
        self.dims = [units] + [2] * bits + [2, 2, 2, inner, self.own, columns]
        self.moves = {"y": bits + 1, "x": bits + 2, "c": bits + 3}
        self.places = {"y": (0, 1), "x": (2, 3)}
        self.links = {"y": ("ty", 1), "x": ("tx", 2), "c": ("tx", 1)}
        for bit in range(bits):
            self.moves[bit] = bits - bit
            self.places[bit] = (4 + 2 * bit, 5 + 2 * bit)
            self.links[bit] = ("batch", 1 << bit)
        self.cut = 0 if units > 1 else len(self.dims) - 3
        self.half = self.dims[self.cut] // 2
        tail = list(range(bits))
        self.orders = [["x", "y"] + tail, ["y", "x"] + tail]
        at = self.moves["c"]
        if len(grads) == 1:
            grad = grads[0].reshape(self.dims)
            core = lax.axis_index("tx") % 2
            keep = lax.dynamic_slice_in_dim(grad, core, 1, at)
            send = lax.dynamic_slice_in_dim(grad, 1 - core, 1, at)
        else:
            halved = list(self.dims)
            halved[at] = 1
            keep, send = grads[0].reshape(halved), grads[1].reshape(halved)
        self.sent = [send]
        received = swap(send, *self.links["c"])
        self.parts = [[(keep, ("c",)), (received, ("c",))] for _ in range(2)]
        self.done = [["c"], ["c"]]

    def pick(self, part, chosen, side):
        array, fixed = part
        starts, sizes = [0] * array.ndim, list(array.shape)
        for move, where in chosen.items():
            if move not in fixed:
                starts[self.moves[move]] = where
                sizes[self.moves[move]] = 1
        if "side" not in fixed:
            starts[self.cut], sizes[self.cut] = side * self.half, self.half
        return array, starts, sizes

    def task(self):
        if self.orders[0][0] == self.orders[1][0]:
            return self.joint_task()
        sides, outs = [], []
        for side in range(2):
            move = self.orders[side][0]
            chosen = {m: self.places[m][:1] for m in self.done[side] if m != "c"}
            chosen[move] = self.places[move][1:]
            parts = [self.pick(part, chosen, side) for part in self.parts[side]]
            sides.append(parts)
            outs.append(sds(tuple(parts[0][2]), BF))
        return {"sides": sides, "outs": outs, "emit": emit_low}

    def joint_task(self):
        move = self.orders[0][0]
        sides = []
        for side in range(2):
            chosen = {m: self.places[m][:1] for m in self.done[side] if m != "c"}
            chosen[move] = self.places[move][1:]
            sides.append([self.pick(part, chosen, side) for part in self.parts[side]])
        shape = list(sides[0][0][2])
        shape[self.cut] = 2 * self.half
        cut, half = self.cut, self.half

        def emit(values, outs):
            for side in range(2):
                index = [slice(None)] * len(shape)
                index[cut] = slice(side * half, (side + 1) * half)
                outs[0][tuple(index)] = values[side].astype(BF)

        return {"sides": sides, "outs": [sds(tuple(shape), BF)], "emit": emit}

    def accept(self, sent):
        if len(sent) == 1:
            move = self.orders[0][0]
            received = swap(sent[0], *self.links[move])
            for side in range(2):
                self.orders[side].pop(0)
                self.done[side].append(move)
                self.parts[side].append((received, tuple(self.done[side])))
            return
        for side in range(2):
            move = self.orders[side].pop(0)
            self.done[side].append(move)
            received = swap(sent[side], *self.links[move])
            self.parts[side].append((received, ("side",) + tuple(self.done[side])))

    def last_task(self, layout):
        sides = []
        for side in range(2):
            chosen = {m: self.places[m][:1] for m in self.done[side] if m != "c"}
            sides.append([self.pick(part, chosen, side) for part in self.parts[side]])
        shapes, units = layout
        own, columns, half = self.own, self.columns, self.half

        def emit(values, outs):
            for side in range(2):
                value = values[side].reshape(half, own, columns)
                for k in range(half):
                    out, row, col = units[side * half + k]
                    outs[out][
                        row * own : (row + 1) * own, col * columns : (col + 1) * columns
                    ] = value[k]

        outs = [sds((r * own, c * columns), F32) for r, c in shapes]
        return {"sides": sides, "outs": outs, "emit": emit}


def run_tasks(sums, after, name):
    places = sums[0][0].table
    tasks = []
    for sum_, layout in sums:
        tasks.append(sum_.task() if sum_.orders[0] else sum_.last_task(layout))
    outs = serve(tasks, after, name, places)
    results, at = [], 0
    for (sum_, _), task in zip(sums, tasks, strict=True):
        got = outs[at : at + len(task["outs"])]
        at += len(task["outs"])
        if sum_.orders[0]:
            sum_.accept(got)
        else:
            results.append(got)
    return outs, results


def conv_map():
    table = np.zeros((9, 9, 4, 4), np.float32)
    for row_off in range(3):
        for col_off in range(3):
            for p in range(4):
                for q in range(4):
                    i = 2 * (row_off - 1) + p // 2 - q // 2 + 1
                    j = 2 * (col_off - 1) + p % 2 - q % 2 + 1
                    if 0 <= i < 3 and 0 <= j < 3:
                        table[i * 3 + j, row_off * 3 + col_off, p, q] = 1.0
    return table


def conv_lanes(share):
    table = conv_map().transpose(1, 0, 2, 3)
    wide = np.kron(np.eye(share, dtype=np.float32), np.ones((16, 16), np.float32))
    small = np.repeat(np.repeat(table, 4, 2), 4, 3)
    return np.tile(small, (1, 1, share, share)) * wide


def per_device(
    tokens,
    skip_tokens,
    extra_tokens,
    extra_skip,
    timesteps,
    target,
    w_skip,
    b_skip,
    norm1_gain,
    norm1_shift,
    w_qkv,
    w_out,
    b_out,
    norm2_gain,
    norm2_shift,
    w_up,
    b_up,
    w_down,
    b_down,
    final_gain,
    final_shift,
    w_head,
    b_head,
    w_conv,
    b_conv,
):
    items, rows, cols, width = tokens.shape
    hidden_units = w_up.shape[1]
    local = rows * cols
    patch_values = w_head.shape[1]
    chans = w_conv.shape[3]
    devices = lax.axis_size(ALL)
    groups = lax.axis_size(PLANE)
    place = lax.axis_index(PLANE)
    share = items // groups
    per_item = groups * local
    count = share * per_item
    head_dim = width // HEADS
    height, breadth = rows * PATCH, cols * PATCH

    def row(vector):
        return vector.astype(F32).reshape(1, -1)

    def to_items(array):
        return lax.all_to_all(array, PLANE, split_axis=0, concat_axis=0, tiled=True)

    some = 8
    joined_rows = 2 * local + 8
    tile_block = pl.BlockSpec((some, rows, cols, width), lambda i: (i, 0, 0, 0))
    flat_block = pl.BlockSpec((some, local, width), lambda i: (i, 0, 0))
    hidden0, joined = pl.pallas_call(
        merge_kernel,
        grid=(items // some,),
        in_specs=[tile_block, tile_block, whole((2 * width, width)), whole((width,))],
        out_specs=[flat_block, pl.BlockSpec((some, joined_rows, width), lambda i: (i, 0, 0))],
        out_shape=[sds((items, local, width), BF), sds((items, joined_rows, width), BF)],
        compiler_params=params(),
        cost_estimate=cost(items * local * 4 * width * width, 11e6),
        name="merge",
    )(tokens, skip_tokens, w_skip, b_skip)
    hidden0 = to_items(hidden0)
    hidden0 = hidden0.reshape(groups, share, local, width)
    target_patches = (
        target.reshape(items, rows, PATCH, cols, PATCH, chans)
        .transpose(0, 1, 3, 2, 4, 5)
        .reshape(items, local * patch_values)
    )
    high = lax.reduce_precision(target_patches, 8, 7)
    middle = lax.reduce_precision(target_patches - high, 8, 7)
    low = target_patches - high - middle
    thirds = jnp.concatenate([high, middle, low], 1).astype(BF).reshape(items, -1, width)
    joined = lax.dynamic_update_slice(joined, thirds, (0, 2 * local, 0))

    start = place * share
    joined_extra = jnp.concatenate(
        [
            lax.dynamic_slice_in_dim(extra_tokens, start, share, 0),
            lax.dynamic_slice_in_dim(extra_skip, start, share, 0),
        ],
        2,
    )
    extra_rows = share * EXTRA_PAD
    joined_extra = jnp.pad(joined_extra, ((0, 0), (0, EXTRA_PAD - 2), (0, 0)))
    joined_extra = joined_extra.reshape(extra_rows, 2 * width)
    hidden_extra = dot(joined_extra, w_skip, 1, 0) + row(b_skip)
    unit_extra, _ = norm_parts(hidden_extra)
    normed_extra = (unit_extra * row(norm1_gain) + row(norm1_shift)).astype(BF)
    pairs_extra = dot(normed_extra, w_qkv[:, width:], 1, 0).astype(BF)

    def by_head(block):
        return block.reshape(share, EXTRA_PAD, HEADS, head_dim).transpose(0, 2, 1, 3)

    key_extra = by_head(pairs_extra[:, :width])
    value_extra = by_head(pairs_extra[:, width:])

    weight = lax.dynamic_slice_in_dim(noise_weight(timesteps), start, share, 0)
    lanes = share * patch_values
    spread = jnp.tile(w_conv.reshape(9, chans, chans), (1, lanes // chans, lanes // chans))
    kernel = jnp.sum(jnp.asarray(conv_lanes(share)) * spread[None].astype(F32), 1).astype(BF)
    lane_rows = jnp.concatenate(
        [
            jnp.tile(b_head.astype(F32), share),
            jnp.tile(b_conv.astype(F32), lanes // chans),
            jnp.repeat(weight, patch_values),
        ]
    ).reshape(3, lanes)
    joined = lax.optimization_barrier(
        (joined, key_extra, value_extra, kernel, lane_rows, normed_extra)
    )[0]
    joined = to_items(joined).reshape(groups, share, joined_rows, width)
    thirds = joined[:, :, 2 * local : 2 * local + thirds.shape[1]].astype(F32)
    thirds = thirds.reshape(groups, share, 3, local, patch_values)
    target_own = (
        (thirds[:, :, 0] + thirds[:, :, 1] + thirds[:, :, 2])
        .transpose(0, 2, 1, 3)
        .reshape(per_item, share * patch_values)
    )

    vec = whole((width,))
    item_block = pl.BlockSpec((groups, 1, local, width), lambda i: (0, i, 0, 0))

    def per_share(*shape):
        return pl.BlockSpec((1,) + shape, lambda i: (i,) + (0,) * len(shape))

    normed1, qkv, probs, probs_extra, mixed, hidden1 = pl.pallas_call(
        attend_kernel,
        grid=(share,),
        in_specs=[
            item_block,
            per_share(HEADS, EXTRA_PAD, head_dim),
            per_share(HEADS, EXTRA_PAD, head_dim),
            vec,
            vec,
            vec,
            whole((width, 3 * width)),
            whole((width, width)),
        ],
        out_specs=[
            per_share(per_item, width),
            per_share(3 * width, per_item),
            per_share(HEADS, per_item, per_item),
            per_share(HEADS, EXTRA_PAD, per_item),
            per_share(width, per_item),
            per_share(per_item, width),
        ],
        out_shape=[
            sds((share, per_item, width), BF),
            sds((share, 3 * width, per_item), BF),
            sds((share, HEADS, per_item, per_item), BF),
            sds((share, HEADS, EXTRA_PAD, per_item), BF),
            sds((share, width, per_item), BF),
            sds((share, per_item, width), F32),
        ],
        scratch_shapes=[
            pltpu.VMEM((HEADS, per_item, per_item), F32),
            pltpu.VMEM((HEADS, EXTRA_PAD, per_item), F32),
        ],
        compiler_params=params(),
        cost_estimate=cost(count * (8 * width * width + 16 * per_item * width), 25e6, 3e6),
        name="attend",
    )(
        hidden0,
        key_extra,
        value_extra,
        norm1_gain,
        norm1_shift,
        b_out,
        w_qkv,
        w_out,
    )
    hidden1 = hidden1.reshape(count, width)

    chunk = width
    chunks = hidden_units // chunk
    by_col = pl.BlockSpec((1, count, chunk), lambda j: (j, 0, 0))
    active, slope, normed2, hidden2 = pl.pallas_call(
        forward_kernel,
        grid=(chunks,),
        in_specs=[
            whole((count, width)),
            vec,
            vec,
            whole((hidden_units,)),
            vec,
            pl.BlockSpec((width, chunk), lambda j: (0, j)),
            pl.BlockSpec((chunk, width), lambda j: (j, 0)),
        ],
        out_specs=[by_col, by_col, whole((count, width)), whole((count, width))],
        out_shape=[
            sds((chunks, count, chunk), BF),
            sds((chunks, count, chunk), BF),
            sds((count, width), BF),
            sds((count, width), F32),
        ],
        scratch_shapes=[pltpu.VMEM((chunks, chunk), F32)],
        compiler_params=params(),
        cost_estimate=cost(count * 4 * width * hidden_units, 25e6, 5e6),
        name="forward",
    )(hidden1, norm2_gain, norm2_shift, b_up, b_down, w_up, w_down)
    (
        result,
        grad_hidden2,
        grad_down,
        grad_head,
        sums_final,
        head_sum,
        conv_sum,
        conv_bias,
    ) = pl.pallas_call(
        functools.partial(turn_kernel, rows, cols, lax.axis_size("tx")),
        grid=(1,),
        in_specs=[
            whole((count, width)),
            vec,
            vec,
            whole((patch_values, width)),
            whole((9, lanes, lanes)),
            whole((3, lanes)),
            whole((per_item, lanes)),
            pl.BlockSpec(memory_space=pl.ANY),
        ],
        out_specs=[
            whole((per_item, lanes)),
            whole((count, width)),
            whole((count, width)),
            whole((1, lanes)),
            whole((8, width)),
            whole((share, lanes, width)),
            whole((9, lanes, lanes)),
            whole((1, lanes)),
        ],
        out_shape=[
            sds((per_item, lanes), BF),
            sds((count, width), F32),
            sds((count, width), BF),
            sds((1, lanes), F32),
            sds((8, width), F32),
            sds((share, lanes, width), F32),
            sds((9, lanes, lanes), F32),
            sds((1, lanes), F32),
        ],
        scratch_shapes=[pltpu.VMEM((count, width), F32)],
        compiler_params=params(),
        cost_estimate=cost(1e9, 10e6),
        name="turn",
    )(
        hidden2,
        final_gain,
        final_shift,
        w_head.T,
        kernel,
        lane_rows,
        target_own,
        joined,
    )

    any_place = pl.BlockSpec(memory_space=pl.ANY)
    table = place_table()
    core = lax.axis_index("tx") % 2
    core = core.astype(jnp.int32).reshape(1)
    core_spec = pl.BlockSpec(memory_space=pltpu.SMEM)

    def split_outs(units, rows, block_rows, own, cols, index):
        if can_split(own):
            spec = pl.BlockSpec(
                (units, block_rows // (2 * own), own, cols), lambda j: index(j) + (0, 0)
            )
            return spec, lambda n: sds((n, rows // (2 * own), own, cols), BF), 2
        spec = pl.BlockSpec((units, block_rows, cols), lambda j: index(j) + (0,))
        return spec, lambda n: sds((n, rows, cols), BF), 1

    own = width // devices
    half = width // 2
    units = 2 * chunks + 2
    chain_down = CHAIN_DOWN and can_split(own)
    if chain_down:
        down_specs = [
            pl.BlockSpec((8, chunk // (8 * own), own, half), lambda j: (0, j, 0, 0))
        ] * 2
        down_shapes = [sds((8, width // (2 * own), own, half), BF)] * 2
    else:
        down_specs = [pl.BlockSpec((chunk, width), lambda j: (j, 0))]
        down_shapes = [sds((hidden_units, width), BF)]
    grad_w_down = pl.pallas_call(
        functools.partial(down_kernel, own, chain_down),
        grid=(chunks,),
        in_specs=[by_col, whole((count, width)), core_spec],
        out_specs=down_specs,
        out_shape=down_shapes,
        compiler_params=params(),
        cost_estimate=cost(count * 2 * width * hidden_units, 11e6),
        name="down_weight",
    )(active, grad_down, core)
    if chain_down:
        sum_down = Sum(grad_w_down, 8, 1, half, table)
    else:
        out_down = lax.psum_scatter(
            grad_w_down[0], ALL, scatter_dimension=0, tiled=True
        ).astype(F32)

    up_spec, up_shape, up_outs = split_outs(2, width, width, own, half, lambda j: (j, 0))

    def held_col(j):
        return jnp.minimum(j, chunks - 1)

    grad_b_up, grad_hidden1, grad_branch, sums_up, *grad_w_up = pl.pallas_call(
        functools.partial(up_kernel, own),
        grid=(chunks + 1,),
        in_specs=[
            pl.BlockSpec((1, count, chunk), lambda j: (held_col(j), 0, 0)),
            whole((count, width)),
            pl.BlockSpec((chunk, width), lambda j: (held_col(j), 0)),
            pl.BlockSpec((width, chunk), lambda j: (0, held_col(j))),
            whole((count, width)),
            whole((count, width)),
            vec,
            whole((count, width)),
            whole((share, width, per_item)),
            core_spec,
        ]
        + [any_place] * len(grad_w_down),
        out_specs=[
            pl.BlockSpec((1, 8, chunk), lambda j: (held_col(j), 0, 0)),
            whole((count, width)),
            whole((count, width)),
            whole((8, width)),
        ]
        + [up_spec] * up_outs,
        out_shape=[
            sds((chunks, 8, chunk), F32),
            sds((count, width), F32),
            sds((count, width), BF),
            sds((8, width), F32),
        ]
        + [up_shape(units)] * up_outs,
        scratch_shapes=[pltpu.VMEM((count, width), F32)],
        compiler_params=params(),
        cost_estimate=cost(count * (6 * hidden_units + 2 * width) * width, 25e6),
        name="up_weight",
    )(
        slope,
        grad_down,
        w_down,
        w_up,
        normed2,
        hidden1,
        norm2_gain,
        grad_hidden2,
        mixed,
        core,
        *grad_w_down,
    )
    if can_split(own):
        sum_up = Sum(grad_w_up, units, 1, half, table)
    down_layout = ([(4, 2)], [(0, k // 2, k % 2) for k in range(8)])
    up_layout = (
        [(1, 2 * chunks), (1, 2)],
        [(0, 0, k) for k in range(2 * chunks)] + [(1, 0, 0), (1, 0, 1)],
    )
    late_layout = (
        [(1, 6), (2, 2)],
        [(0, 0, k) for k in range(6)] + [(1, 0, 0), (1, 1, 0), (1, 0, 1), (1, 1, 1)],
    )

    after = sum_up.sent if can_split(own) else []
    if chain_down:
        after, _ = run_tasks([(sum_down, None)], after, "serve_0")
        early = [(sum_down, None)]
    else:
        early = []
    grad_qkv, grad_key_extra, grad_value_extra = [], [], []
    sums_attend = jnp.zeros((8, width), F32)
    grad_hidden0 = None
    back_rows = share * local + 16
    for first, number in ((0, share - 1), (share - 1, 1)):

        def one(*shape, first=first):
            return pl.BlockSpec((1,) + shape, lambda i: (first + i,) + (0,) * len(shape))

        def own_item(*shape):
            return pl.BlockSpec((1,) + shape, lambda i: (i,) + (0,) * len(shape))

        held = [grad_hidden0] if first else []
        outs = pl.pallas_call(
            attend_back_kernel,
            grid=(number,),
            in_specs=[
                pl.BlockSpec(
                    (groups, 1, local, width), lambda i, first=first: (0, first + i, 0, 0)
                ),
                one(per_item, width),
                one(per_item, width),
                one(3 * width, per_item),
                one(HEADS, per_item, per_item),
                one(HEADS, EXTRA_PAD, per_item),
                one(HEADS, EXTRA_PAD, head_dim),
                one(HEADS, EXTRA_PAD, head_dim),
                vec,
                whole((width, 3 * width)),
                whole((width, width)),
                whole((8, width)),
            ]
            + [any_place] * (len(held) + len(after)),
            out_specs=[
                own_item(3 * width, per_item),
                own_item(HEADS, EXTRA_PAD, head_dim),
                own_item(HEADS, EXTRA_PAD, head_dim),
                pl.BlockSpec((groups, local, width), lambda i, first=first: (0, first + i, 0)),
                whole((8, width)),
            ],
            out_shape=[
                sds((number, 3 * width, per_item), BF),
                sds((number, HEADS, EXTRA_PAD, head_dim), F32),
                sds((number, HEADS, EXTRA_PAD, head_dim), F32),
                sds((groups, back_rows, width), BF),
                sds((8, width), F32),
            ],
            input_output_aliases={12: 3} if first else {},
            scratch_shapes=[
                pltpu.VMEM((width, per_item), BF),
                pltpu.VMEM((HEADS, per_item, per_item), F32),
                pltpu.VMEM((HEADS, EXTRA_PAD, per_item), F32),
                pltpu.VMEM((HEADS, per_item, per_item), BF),
                pltpu.VMEM((HEADS, EXTRA_PAD, per_item), BF),
            ],
            compiler_params=params(),
            cost_estimate=cost(
                per_item * (8 * width * width + 40 * per_item * width), 12e6
            ),
            name="attend_back",
        )(
            hidden0,
            grad_hidden1.reshape(share, per_item, width),
            grad_branch.reshape(share, per_item, width),
            qkv,
            probs,
            probs_extra,
            key_extra,
            value_extra,
            norm1_gain,
            w_qkv,
            w_out,
            sums_attend,
            *held,
            *after,
        )
        grad_qkv += [outs[0]] * number
        grad_key_extra += [outs[1]] * number
        grad_value_extra += [outs[2]] * number
        grad_hidden0, sums_attend = outs[3], outs[4]
        after = []
        if can_split(own) and not first:
            after, _ = run_tasks([(sum_up, None)] + early, [sums_attend], "serve_1")
    places_of = [i for number in (share - 1, 1) for i in range(number)]

    latent = result.reshape(groups, local * share * patch_values // width, width)
    pairs_extra, grad_extra, sums_attend, grad_back = pl.pallas_call(
        functools.partial(extra_back_kernel, share),
        grid=(1,),
        in_specs=[
            whole((extra_rows, width)),
            vec,
            pl.BlockSpec((width, width), lambda *_: (0, 1)),
            pl.BlockSpec((width, width), lambda *_: (0, 2)),
            whole(latent.shape),
            whole((8, width)),
        ]
        + [
            pl.BlockSpec((1, HEADS, EXTRA_PAD, head_dim), lambda *_, at=at: (at, 0, 0, 0))
            for at in places_of * 2
        ]
        + [any_place] * (1 + len(after)),
        out_specs=[
            whole((2, extra_rows, width)),
            whole((extra_rows, width)),
            whole((8, width)),
            pl.BlockSpec((groups, 16, width), lambda *_: (0, share * local // 16, 0)),
        ],
        out_shape=[
            sds((2, extra_rows, width), BF),
            sds((extra_rows, width), BF),
            sds((8, width), F32),
            sds((groups, back_rows, width), BF),
        ],
        input_output_aliases={6 + 2 * share: 3},
        compiler_params=params(),
        cost_estimate=cost(1e8, 5e6),
        name="extra_back",
    )(
        hidden_extra,
        norm1_gain,
        w_qkv,
        w_qkv,
        latent,
        sums_attend,
        *grad_key_extra,
        *grad_value_extra,
        grad_hidden0,
        *after,
    )

    late_spec, late_shape, late_outs = split_outs(
        2, width, width, own, width // 2, lambda j: (j, 0)
    )

    def skip_col(j):
        return jnp.maximum(j - 3, 0)

    def qkv_row(j):
        return jnp.minimum(j, 2)

    half = width // 2
    grad_late = pl.pallas_call(
        functools.partial(late_weight_kernel, own),
        grid=(5,),
        in_specs=[
            whole((share, per_item, width)),
            whole((extra_rows, width)),
            pl.BlockSpec(
                (1, extra_rows, width), lambda j: (jnp.clip(j - 1, 0, 1), 0, 0)
            ),
            whole(joined.shape),
            pl.BlockSpec((groups, back_rows, half), lambda j: (0, 0, skip_col(j))),
            whole((extra_rows, 2 * width)),
            pl.BlockSpec((extra_rows, half), lambda j: (0, skip_col(j))),
        ]
        + [
            pl.BlockSpec((1, width, per_item), lambda j, at=at: (at, qkv_row(j), 0))
            for at in places_of
        ]
        + [core_spec],
        out_specs=[late_spec] * late_outs,
        out_shape=[late_shape(10)] * late_outs,
        compiler_params=params(),
        cost_estimate=cost(count * 10 * width * width, 12e6),
        name="late_weight",
    )(
        normed1,
        normed_extra,
        pairs_extra,
        joined,
        grad_back,
        joined_extra,
        grad_extra,
        *grad_qkv,
        core,
    )

    def hold(values, *others):
        return lax.optimization_barrier((values, others))[0]

    if can_split(own):
        after, _ = run_tasks([(sum_up, None)] + early, [grad_late[0]], "serve_2")
        grad_late = [grad_late[0], hold(grad_late[1], after)]
        sum_late = Sum(grad_late, 10, 1, half, table)
    else:
        after = list(grad_late)

    stacked_count = 9 + patch_values
    stacked, shared = pl.pallas_call(
        pack_kernel,
        in_specs=[pl.BlockSpec(memory_space=pltpu.VMEM)] * 8 + [any_place] * len(after),
        out_specs=[pl.BlockSpec(memory_space=pltpu.VMEM)] * 2,
        out_shape=[sds((stacked_count, width), F32), sds((8, 128), F32)],
        compiler_params=params(),
        cost_estimate=cost(1e6, 1e6),
        name="pack",
    )(
        sums_attend,
        sums_up,
        sums_final,
        head_sum,
        grad_head,
        conv_sum,
        conv_bias,
        jnp.asarray(conv_lanes(share), BF),
        *after,
    )
    packed = jnp.concatenate(
        [
            stacked.reshape(stacked_count, devices, own).transpose(1, 0, 2).reshape(devices, -1),
            grad_b_up[:, 0].reshape(devices, -1),
            jnp.broadcast_to(shared[:4].reshape(1, -1), (devices, 512)),
        ],
        1,
    )
    packed_size = packed.shape[1]
    packed = jnp.pad(packed, ((0, 0), (0, (-packed.shape[1]) % 128)))
    if not can_split(own):
        wide = grad_w_up[0].transpose(1, 0, 2).reshape(width, -1)
        wide = lax.psum_scatter(wide, ALL, scatter_dimension=0, tiled=True).astype(F32)
        out_up, out_out = wide[:, :hidden_units], wide[:, hidden_units:]
        wide = grad_late[0][:6].transpose(1, 0, 2).reshape(width, -1)
        out_qkv = lax.psum_scatter(wide, ALL, scatter_dimension=0, tiled=True).astype(F32)
        tall = grad_late[0][6:].reshape(2, 2, width, half).transpose(1, 2, 0, 3)
        tall = tall.reshape(2 * width, width)
        out_skip = lax.psum_scatter(tall, ALL, scatter_dimension=0, tiled=True).astype(F32)
    else:
        after, _ = run_tasks([(sum_late, None), (sum_up, None)] + early, [packed], "serve_5")
    exchanged = lax.all_to_all(hold(packed, after), ALL, split_axis=0, concat_axis=0, tiled=True)
    if can_split(own):
        if chain_down:
            early = [(sum_down, down_layout)]
        after, results = run_tasks(
            [(sum_late, None), (sum_up, None)] + early, [exchanged], "serve_6"
        )
        if chain_down:
            out_down = results[0][0]
        after, results = run_tasks([(sum_late, None), (sum_up, up_layout)], after, "serve_7")
        out_up, out_out = results[0]
    back = to_items(hold(grad_back, after))
    if can_split(own):
        while sum_late.orders[0]:
            after, _ = run_tasks([(sum_late, None)], after, "serve_8")
    some_groups = max(groups // 2, 1)
    token_block = pl.BlockSpec(
        (some_groups * share, rows, cols, width), lambda i: (i, 0, 0, 0)
    )
    grad_tokens, grad_skip_tokens, grad_extra_all = pl.pallas_call(
        token_kernel,
        grid=(groups // some_groups,),
        in_specs=[
            pl.BlockSpec((some_groups, back_rows, width), lambda i: (i, 0, 0)),
            whole((2 * width, width)),
        ],
        out_specs=[
            token_block,
            token_block,
            pl.BlockSpec((some_groups, 16, 2 * width), lambda i: (i, 0, 0)),
        ],
        out_shape=[sds(tokens.shape, BF)] * 2 + [sds((groups, 16, 2 * width), BF)],
        compiler_params=params(),
        cost_estimate=cost(items * local * 4 * width * width, 8e6),
        name="tokens",
    )(hold(back, after), w_skip)
    summed = jnp.sum(hold(exchanged, after), 0)
    small = [summed[k * own : (k + 1) * own] for k in range(9)]
    own_head = summed[9 * own : stacked_count * own].reshape(patch_values, own).T
    up_low = stacked_count * own
    own_b_up = summed[up_low : up_low + hidden_units // devices]
    shared = summed[up_low + hidden_units // devices : packed_size].reshape(4, 128)

    latent_row = share * local + 2 * share
    latent = back[:, latent_row : latent_row + latent.shape[1]]
    latent_out = (
        hold(latent, after)
        .reshape(groups, rows, cols, share, PATCH, PATCH, chans)
        .transpose(0, 3, 1, 4, 2, 5, 6)
        .reshape(items, height, breadth, chans)
    )
    grad_joined_extra = grad_extra_all[:, : 2 * share].reshape(items, 2, 2 * width)
    if can_split(own):
        _, results = run_tasks([(sum_late, late_layout)], [grad_tokens, latent_out], "serve_9")
        out_qkv, out_skip = results[0]
    return (
        latent_out,
        grad_tokens,
        grad_skip_tokens,
        grad_joined_extra[..., :width],
        grad_joined_extra[..., width:],
        out_skip,
        small[0],
        small[1],
        small[2],
        out_qkv,
        out_out,
        small[3],
        small[4],
        small[5],
        out_up,
        own_b_up,
        out_down,
        small[6],
        small[7],
        small[8],
        own_head,
        shared[0, 64 : 64 + patch_values],
        shared[:, : 9 * chans].reshape(chans, 3, 3, chans).transpose(1, 2, 0, 3),
        shared[0, 96 : 96 + chans],
    )


def solution(mesh):
    tiles = P("batch", "ty", "tx", None)
    pairs = P("batch", None, None)
    matrix = P(ALL, None)
    vector = P(ALL)
    return jax.shard_map(
        per_device,
        mesh=mesh,
        in_specs=(tiles, tiles, pairs, pairs, P("batch"), tiles) + (P(),) * 19,
        out_specs=(
            tiles,
            tiles,
            tiles,
            pairs,
            pairs,
            matrix,
            vector,
            vector,
            vector,
            matrix,
            matrix,
            vector,
            vector,
            vector,
            matrix,
            vector,
            matrix,
            vector,
            vector,
            vector,
            matrix,
            P(),
            P(),
            P(),
        ),
        check_vma=False,
    )
```

profile of v0, /device:TPU:0, one launch (start us, length us, event | category | flops | bytes accessed | tf_op | source)
XLA Modules:
  0.0 275.9 jit_solution(402840350243318834)
XLA Ops:
  0.7 5.6 %merge.1 = (bf16[24,32,768]{2,1,0:T(8,128)(2,1)}, bf16[24,72,768]{2,1,0:T(8,128)(2,1)}) custom-call(bf16[24,8,4,768]{3,2,1,0:T(4,128)(2,1)} %tokens_ref.1, bf16[24,8,4,768]{3,2,1,0:T(4,128)(2,1)} %skip_ref.1, bf16[1536,768]{1,0:T(8,128)(2,1)} %w_skip_ref.3, bf16[768]{0:T(1024)(128)(2,1)} %b_skip_ref.1), custom_call_target="tpu_custom_call" | custom-call | flops 1024 | bytes 1024 | tf_op jit(solution)/shard_map/merge/pallas_call | solution.py:896
  6.3 5.4 %all-to-all-start = ((bf16[24,32,768]{2,1,0:T(8,128)(2,1)}), bf16[24,32,768]{2,1,0:T(8,128)(2,1)}, u32[]{:S(2)}, u32[]{:S(2)}) async-start(bf16[24,32,768]{2,1,0:T(8,128)(2,1)} %get-tuple-element.102), calls=%async_computation | async-start | bytes 2359296 | tf_op jit(solution)/shard_map/all_to_all | solution.py:890
  13.5 0.8 constant_dynamic-slice_fusion
  14.3 2.2 fusion.16
  22.1 1.0 copy.110
  24.0 0.9 multiply_reduce_fusion.w_conv_ref
  24.8 3.8 %all-to-all-done = bf16[24,32,768]{2,1,0:T(8,128)(2,1)} async-done(((bf16[24,32,768]{2,1,0:T(8,128)(2,1)}), bf16[24,32,768]{2,1,0:T(8,128)(2,1)}, u32[]{:S(2)}, u32[]{:S(2)}) %all-to-all-start) | async-done | bytes 1179680 | tf_op jit(solution)/shard_map/all_to_all | solution.py:890
  28.6 3.8 %all-to-all-start.1 = ((bf16[24,72,768]{2,1,0:T(8,128)(2,1)}), bf16[24,72,768]{2,1,0:T(8,128)(2,1)S(1)}, u32[]{:S(2)}, u32[]{:S(2)}) async-start(bf16[24,72,768]{2,1,0:T(8,128)(2,1)} %constant_dynamic-update-slice_fusion), calls=%async_computation.1 | async-start | bytes 5308416 | tf_op jit(solution)/shard_map/all_to_all | solution.py:890
  32.4 17.2 %attend.1 = (bf16[3,256,768]{2,1,0:T(8,128)(2,1)}, bf16[3,2304,256]{2,1,0:T(8,128)(2,1)}, bf16[3,12,256,256]{3,2,1,0:T(8,128)(2,1)}, bf16[3,12,8,256]{3,2,1,0:T(...) custom-call(bf16[8,3,32,768]{3,2,1,0:T(8,128)(2,1)} %bitcast.1.hidden_ref, ...), custom_call_target="tpu_custom_call" | custom-call | flops 1024 | bytes 1024 | tf_op jit(solution)/shard_map/attend/pallas_call | solution.py:970
  49.6 14.4 %forward.1 = (bf16[4,768,768]{2,1,0:T(8,128)(2,1)}, bf16[4,768,768]{2,1,0:T(8,128)(2,1)}, bf16[768,768]{1,0:T(8,128)(2,1)}, f32[768,768]{1,0:T(8,128)}) custom-call(f32[768,768]{1,0:T(8,128)} %bitcast.106, bf16[768]{0:T(1024)(128)(2,1)} %gain2_ref.3, bf16[768]{0:T(1024)(128)(2,1)} %shift2_ref.1, bf16[3072]{0:T(1024)(128)(2,1)} %b_up_ref.1, ...), custom_call_target="tpu_custom_call" | custom-call | flops 1024 | bytes 1024 | tf_op jit(solution)/shard_map/forward/pallas_call | solution.py:1021
  64.0 1.0 all-to-all-done.1
  65.0 1.8 reshape.221
  66.8 1.3 fusion.5
  68.4 0.8 copy.114.target_ref
  69.2 8.1 %turn.1 = (bf16[256,48]{1,0:T(8,128)(2,1)}, f32[768,768]{1,0:T(8,128)}, bf16[768,768]{1,0:T(8,128)(2,1)}, f32[1,48]{1,0:T(1,128)}, f32[8,768]{1,0:T(8,128)}, /*i...) custom-call(f32[768,768]{1,0:T(8,128)} %get-tuple-element.104.hidden2_ref, bf16[768]{0:T(1024)(128)(2,1)} %gainf_ref.1, ...), custom_call_target="tpu_custom_call" | custom-call | flops 1024 | bytes 1024 | tf_op jit(solution)/shard_map/turn/pallas_call | solution.py:1054
  77.3 8.1 %down_weight.1 = (bf16[8,16,24,384]{3,2,1,0:T(8,128)(2,1)}, bf16[8,16,24,384]{3,2,1,0:T(8,128)(2,1)}) custom-call(bf16[4,768,768]{2,1,0:T(8,128)(2,1)} %get-tuple-element.113.active_ref, bf16[768,768]{1,0:T(8,128)(2,1)} %get-tuple-element.109.grad_down_ref, s32[1]{0:T(128)} %bitcast.15.core_ref), custom_call_target="tpu_custom_call" | custom-call | flops 1024 | bytes 1024 | tf_op jit(solution)/shard_map/down_weight/pallas_call | solution.py:1129
  85.4 22.6 %up_weight.1 = (f32[4,8,768]{2,1,0:T(8,128)}, f32[768,768]{1,0:T(8,128)}, bf16[768,768]{1,0:T(8,128)(2,1)}, f32[8,768]{1,0:T(8,128)}, bf16[10,16,24,384]{3,2,1,0...) custom-call(bf16[4,768,768]{2,1,0:T(8,128)(2,1)} %get-tuple-element.108.slope_ref, ...), custom_call_target="tpu_custom_call" | custom-call | flops 1024 | bytes 1024 | tf_op jit(solution)/shard_map/up_weight/pallas_call | solution.py:1151
  109.1 3.4 %serve_0.1 = (bf16[4,2,2,2,1,1,1,24,384]{8,7,6,5,4,3,2,1,0:T(8,128)(2,1)}, bf16[4,2,2,1,2,1,1,24,384]{8,7,6,5,4,3,2,1,0:T(8,128)(2,1)}) custom-call(s32[8]{0:T(128)} %stack.35.places_ref, bf16[8,2,2,2,2,1,1,24,384]{8,7,6,5,4,3,2,1,0:T(8,128)(2,1)} %bitcast.91, ...), custom_call_target="tpu_custom_call" | custom-call | flops 1024 | bytes 1024 | tf_op jit(solution)/shard_map/serve_0/pallas_call | solution.py:665
  112.5 1.0 collective-permute-start.2
  113.5 1.5 collective-permute-start.3
  115.6 13.8 %attend_back.2 = (bf16[2,2304,256]{2,1,0:T(8,128)(2,1)}, f32[2,12,8,64]{3,2,1,0:T(8,128)}, f32[2,12,8,64]{3,2,1,0:T(8,128)}, bf16[8,112,768]{2,1,0:T(8,128)(2,1)}, f32[8,768]{1,0:T(8,128)}) custom-call(bf16[8,3,32,768]{3,2,1,0:T(8,128)(2,1)} %bitcast.1.hidden_ref, f32[3,256,768]{2,1,0:T(8,128)} %bitcast.104, bf16[3,256,768]{2,1,0:T(8,128)(2,1)} %bitcast.111, ...), custom_call_target="tpu_custom_call" | custom-call | flops 1024 | bytes 1024 | tf_op jit(solution)/shard_map/attend_back/pallas_call | solution.py:1229
  129.5 1.6 copy-done
  131.2 4.6 %serve_1.1 = (bf16[5,2,2,2,1,1,1,24,384]{8,7,6,5,4,3,2,1,0:T(8,128)(2,1)}, bf16[5,2,2,1,2,1,1,24,384]{8,7,6,5,4,3,2,1,0:T(8,128)(2,1)}, bf16[4,2,2,1,1,1,1,24,38...) custom-call(s32[8]{0:T(128)} %stack.35.places_ref, ...), custom_call_target="tpu_custom_call" | custom-call | flops 1024 | bytes 1024 | tf_op jit(solution)/shard_map/serve_1/pallas_call | solution.py:665
  136.3 1.0 collective-permute-start.5
  137.3 1.0 collective-permute-start.6
  138.4 1.5 collective-permute-start.7
  140.5 1.6 reshape.201.latent_ref
  142.1 8.6 %attend_back.3 = (bf16[1,2304,256]{2,1,0:T(8,128)(2,1)}, f32[1,12,8,64]{3,2,1,0:T(8,128)}, f32[1,12,8,64]{3,2,1,0:T(8,128)}, bf16[8,112,768]{2,1,0:T(8,128)(2,1)}, f32[8,768]{1,0:T(8,128)}) custom-call(bf16[8,3,32,768]{3,2,1,0:T(8,128)(2,1)} %bitcast.1.hidden_ref, f32[3,256,768]{2,1,0:T(8,128)} %bitcast.105, ...), custom_call_target="tpu_custom_call", output_to_operand_aliasing={{3}: (12, {})} | custom-call | flops 1024 | bytes 1024 | tf_op jit(solution)/shard_map/attend_back/pallas_call | solution.py:1229
  150.7 3.4 %extra_back.1 = (bf16[2,24,768]{2,1,0:T(8,128)(2,1)}, bf16[24,768]{1,0:T(8,128)(2,1)}, f32[8,768]{1,0:T(8,128)}, bf16[8,112,768]{2,1,0:T(8,128)(2,1)}) custom-call(f32[24,768]{1,0:T(8,128)} %copy-done.21, bf16[768]{0:T(1024)(128)(2,1)} %gain_ref.7, bf16[768,2304]{1,0:T(8,128)(2,1)} %w_value_ref.1, ...), custom_call_target="tpu_custom_call", output_to_operand_aliasing={{3}: (12, {})} | custom-call | flops 1024 | bytes 1024 | tf_op jit(solution)/shard_map/extra_back/pallas_call | solution.py:1302
  154.1 12.2 %late_weight.1 = (bf16[10,16,24,384]{3,2,1,0:T(8,128)(2,1)}, bf16[10,16,24,384]{3,2,1,0:T(8,128)(2,1)}) custom-call(bf16[3,256,768]{2,1,0:T(8,128)(2,1)} %get-tuple-element.138.normed_ref, bf16[24,768]{1,0:T(8,128)(2,1)} %copy-done.25, bf16[2,24,768]{2,1,0:T(8,128)(2,1)} %get-tuple-element.139.pairs_ref, bf16[8,3,72,768]{3,2,1,0:T(8,128)(2,1)} %bitcast.103, ...), custom_call_target="tpu_custom_call" | custom-call | flops 1024 | bytes 1024 | tf_op jit(solution)/shard_map/late_weight/pallas_call | solution.py:1358
  167.6 3.8 %serve_2.1 = (bf16[5,2,2,1,1,1,1,24,384]{8,7,6,5,4,3,2,1,0:T(8,128)(2,1)}, bf16[5,2,2,1,1,1,1,24,384]{8,7,6,5,4,3,2,1,0:T(8,128)(2,1)}, bf16[8,2,1,1,1,1,1,24,384]{8,7,6,5,4,3,2,1,0:T(8,128)(2,1)}) custom-call(s32[8]{0:T(128)} %stack.35.places_ref, bf16[10,2,2,2,2,1,1,24,384]{8,7,6,5,4,3,2,1,0:T(8,128)(2,1)} %bitcast.83, ...), custom_call_target="tpu_custom_call" | custom-call | flops 1024 | bytes 1024 | tf_op jit(solution)/shard_map/serve_2/pallas_call | solution.py:665
  171.9 1.0 collective-permute-start.10
  172.9 2.0 collective-permute-start.11
  175.0 0.9 slice_reduce_fusion
  176.6 3.0 %pack.1 = (f32[25,768]{1,0:T(8,128)}, f32[8,128]{1,0:T(8,128)}) custom-call(f32[8,768]{1,0:T(8,128)} %get-tuple-element.149.sums_attend_ref, f32[8,768]{1,0:T(8,128)} %get-tuple-element.150.sums_up_ref, f32[8,768]{1,0:T(8,128)} %get-tuple-element.151.sums_final_ref, f32[3,48,768]{2,1,0:T(8,128)} %get-tuple-element.152.head_sum_ref, ...), custom_call_target="tpu_custom_call" | custom-call | flops 1024 | bytes 1024 | tf_op jit(solution)/shard_map/pack/pallas_call | solution.py:1405
  179.5 1.9 reshape.211
  181.5 1.2 copy.115
  182.6 0.8 copy.116
  184.1 1.0 concatenate.16
  186.5 1.0 copy-done.1
  187.5 4.7 %serve_5.1 = (bf16[5,2,2,2,1,1,1,24,384]{8,7,6,5,4,3,2,1,0:T(8,128)(2,1)}, bf16[5,2,2,1,2,1,1,24,384]{8,7,6,5,4,3,2,1,0:T(8,128)(2,1)}, bf16[10,2,1,1,1,1,1,24,3...) custom-call(s32[8]{0:T(128)} %stack.35.places_ref, ...), custom_call_target="tpu_custom_call" | custom-call | flops 1024 | bytes 1024 | tf_op jit(solution)/shard_map/serve_5/pallas_call | solution.py:665
  192.2 1.1 collective-permute-start.12
  193.3 1.5 collective-permute-start.13
  194.9 0.8 copy.117
  195.7 4.9 %all-to-all-start.2 = ((f32[32,1,1280]{2,1,0:T(1,128)}), f32[32,1,1280]{2,1,0:T(1,128)S(1)}, u32[]{:S(2)}, u32[]{:S(2)}) async-start(f32[32,1,1280]{2,1,0:T(1,128)} %copy.117), calls=%async_computation.2 | async-start | bytes 327680 | tf_op jit(solution)/shard_map/all_to_all | solution.py:1445
  200.6 2.9 %collective-permute-start.15 = (bf16[8,1,1,1,1,1,1,24,384]{8,7,6,5,4,3,2,1,0:T(8,128)(2,1)}, bf16[8,1,1,1,1,1,1,24,384]{8,7,6,5,4,3,2,1,0:T(8,128)(2,1)S(1)}, u32[]{:S(2)}, u32[]{:S(2)}) collective-permute-start(bf16[8,1,1,1,1,1,1,24,384]{8,7,6,5,4,3,2,1,0:T(8,128)(2,1)} %get-tuple-element.162), channel_id=1, source_target_pairs={{0,16},{8,24},{16,0},{24,8},{1,17},{9,25},{17,1},{25,9},{2,18},{10... | collective-permute-start | bytes 442376 | tf_op jit(solution)/shard_map/ppermute | solution.py:627
  203.4 9.5 %all-to-all-done.2 = f32[32,1,1280]{2,1,0:T(1,128)S(1)} async-done(((f32[32,1,1280]{2,1,0:T(1,128)}), f32[32,1,1280]{2,1,0:T(1,128)S(1)}, u32[]{:S(2)}, u32[]{:S(2)}) %all-to-all-start.2) | async-done | bytes 163872 | tf_op jit(solution)/shard_map/all_to_all | solution.py:1445
  215.5 4.0 %serve_6.1 = (bf16[5,2,2,1,1,1,1,24,384]{8,7,6,5,4,3,2,1,0:T(8,128)(2,1)}, bf16[5,2,2,1,1,1,1,24,384]{8,7,6,5,4,3,2,1,0:T(8,128)(2,1)}, bf16[10,1,1,1,1,1,1,24,384]{8,7,6,5,4,3,2,1,0:T(8,128)(2,1)}, f32[96,768]{1,0:T(8,128)}) custom-call(s32[8]{0:T(128)} %stack.35.places_ref, bf16[10,2,2,2,2,1,1,24,384]{8,7,6,5,4,3,2,1,0:T(8,128)(2,1)} %bitcast.73, ...), custom_call_target="tpu_custom_call" | custom-call | flops 1024 | bytes 1024 | tf_op jit(solution)/shard_map/serve_6/pallas_call | solution.py:665
  219.5 1.5 collective-permute-start.16
  221.0 1.5 collective-permute-start.17
  222.5 1.1 collective-permute-start.18
  223.6 8.7 %collective-permute-done.18.refs_13_.refs_19_ = bf16[10,1,1,1,1,1,1,24,384]{8,7,6,5,4,3,2,1,0:T(8,128)(2,1)S(1)} collective-permute-done((bf16[10,1,1,1,1,1,1,24,384]{8,7,6,5,4,3,2,1,0:T(8,128)(2,1)}, bf16[10,1,1,1,1,1,1,24,384]{8,7,6,5,4,3,2,1,0:T(8,128)(2,1)S(1)}, u32[]{:S(2)}, u32[]{:S(2)}) %collective-permute-start.18) | collective-permute-done | bytes 184352 | tf_op jit(solution)/shard_map/ppermute | solution.py:627
  233.2 3.5 %serve_7.1 = (bf16[10,2,1,1,1,1,1,24,384]{8,7,6,5,4,3,2,1,0:T(8,128)(2,1)}, f32[24,3072]{1,0:T(8,128)}, f32[24,768]{1,0:T(8,128)}) custom-call(s32[8]{0:T(128)} %stack.35.places_ref, bf16[10,2,2,2,2,1,1,24,384]{8,7,6,5,4,3,2,1,0:T(8,128)(2,1)} %bitcast.75, bf16[10,2,2,2,2,1,1,24,384]{8,7,6,5,4,3,2,1,0:T(8,128)(2,1)} %copy-done.1, ...), custom_call_target="tpu_custom_call" | custom-call | flops 1024 | bytes 1024 | tf_op jit(solution)/shard_map/serve_7/pallas_call | solution.py:665
  236.8 3.6 %all-to-all-start.3 = ((bf16[8,112,768]{2,1,0:T(8,128)(2,1)}), bf16[8,112,768]{2,1,0:T(8,128)(2,1)S(1)}, u32[]{:S(2)}, u32[]{:S(2)}) async-start(bf16[8,112,768]{2,1,0:T(8,128)(2,1)} %get-tuple-element.171.grad_ref), calls=%async_computation.3 | async-start | bytes 2752512 | tf_op jit(solution)/shard_map/all_to_all | solution.py:890
  240.4 7.1 %collective-permute-done.19.refs_4_.refs_9_.refs_10_ = bf16[10,2,1,1,1,1,1,24,384]{8,7,6,5,4,3,2,1,0:T(8,128)(2,1)S(1)} collective-permute-done((bf16[10,2,1,1,1,1,1,24,384]{8,7,6,5,4,3,2,1,0:T(8,128)(2,1)}, bf16[10,2,1,1,1,1,1,24,384]{8,7,6,5,4,3,2,1,0:T(8,128)(2,1)S(1)}, u32[]{:S(2)}, u32[]{:S(2)}) %collective-permute-start.19) | collective-permute-done | bytes 368672 | tf_op jit(solution)/shard_map/ppermute | solution.py:627
  247.5 0.8 copy-done.11
  248.2 2.7 serve_8.1
  255.6 3.6 %all-to-all-done.3.back_ref = bf16[8,112,768]{2,1,0:T(8,128)(2,1)S(1)} async-done(((bf16[8,112,768]{2,1,0:T(8,128)(2,1)}), bf16[8,112,768]{2,1,0:T(8,128)(2,1)S(1)}, u32[]{:S(2)}, u32[]{:S(2)}) %all-to-all-start.3) | async-done | bytes 1376288 | tf_op jit(solution)/shard_map/all_to_all | solution.py:890
  259.5 3.0 %copy.119 = bf16[8,3,8,2,4,2,4]{6,5,4,3,2,1,0:T(2,128)(2,1)S(1)} copy(bf16[8,3,8,2,4,2,4]{0,6,5,3,1,4,2:T(4,128)(2,1)S(1)} %bitcast.117) | data formatting | bytes 49152 | tf_op jit(solution)/shard_map/transpose | solution.py:1493
  262.5 1.7 copy.120
  264.2 6.1 %tokens.1 = (bf16[24,8,4,768]{3,2,1,0:T(4,128)(2,1)}, bf16[24,8,4,768]{3,2,1,0:T(4,128)(2,1)}, bf16[8,16,1536]{2,1,0:T(8,128)(2,1)}) custom-call(bf16[8,112,768]{2,1,0:T(8,128)(2,1)} %copy-done.12, bf16[1536,768]{1,0:T(8,128)(2,1)} %w_skip_ref.3), custom_call_target="tpu_custom_call" | custom-call | flops 1024 | bytes 1024 | tf_op jit(solution)/shard_map/tokens/pallas_call | solution.py:1464
  270.4 0.9 slice.94
  271.5 0.8 fusion.13
  272.9 2.8 %serve_9.1 = (f32[24,2304]{1,0:T(8,128)}, f32[48,768]{1,0:T(8,128)}) custom-call(s32[8]{0:T(128)} %stack.35.places_ref, bf16[10,2,2,2,2,1,1,24,384]{8,7,6,5,4,3,2,1,0:T(8,128)(2,1)} %bitcast.79, bf16[10,2,2,2,2,1,1,24,384]{8,7,6,5,4,3,2,1,0:T(8,128)(2,1)} %copy-done.1, bf16[5,2,2,2,1,1,1,24,384]{8,7,6,5,4,3,2,1,0:T(8,128)(2,1)} %copy-done.6, ...), custom_call_target="tpu_custom_call" | custom-call | flops 1024 | bytes 1024 | tf_op jit(solution)/shard_map/serve_9/pallas_call | solution.py:665
  (152 shorter events, 25.3 us)
Async XLA Ops:
  6.2 5.5 %copy-start.31 = (bf16[768]{0:T(1024)(128)(2,1)S(1)}, bf16[768]{0:T(1024)(128)(2,1)}, u32[]{:S(2)}) copy-start(bf16[768]{0:T(1024)(128)(2,1)} %b_skip_ref.1) | copy-start | bytes 4612
  6.2 6.1 %copy-start.32 = (bf16[768]{0:T(1024)(128)(2,1)S(1)}, bf16[768]{0:T(1024)(128)(2,1)}, u32[]{:S(2)}) copy-start(bf16[768]{0:T(1024)(128)(2,1)} %shift_ref.1) | copy-start | bytes 4612
  6.2 6.7 %copy-start.28 = (bf16[768]{0:T(1024)(128)(2,1)S(1)}, bf16[768]{0:T(1024)(128)(2,1)}, u32[]{:S(2)}) copy-start(bf16[768]{0:T(1024)(128)(2,1)} %gain_ref.7) | copy-start | bytes 4612
  6.2 11.0 %copy-start.2 = (bf16[768,2304]{1,0:T(8,128)(2,1)S(1)}, bf16[768,2304]{1,0:T(8,128)(2,1)}, u32[]{:S(2)}) copy-start(bf16[768,2304]{1,0:T(8,128)(2,1)} %w_value_ref.1) | copy-start | bytes 10616836
  6.3 22.4 %all-to-all-start = ((bf16[24,32,768]{2,1,0:T(8,128)(2,1)}), bf16[24,32,768]{2,1,0:T(8,128)(2,1)}, u32[]{:S(2)}, u32[]{:S(2)}) async-start(bf16[24,32,768]{2,1,0:T(8,128)(2,1)} %get-tuple-element.102), calls=%async_computation | async-start | bytes 2359296 | tf_op jit(solution)/shard_map/all_to_all | solution.py:890
  13.5 3.6 %copy-start.29 = (f32[768]{0:T(1024)S(1)}, f32[768]{0:T(1024)}, u32[]{:S(2)}) copy-start(f32[768]{0:T(1024)} %convert_element_type.54) | copy-start | bytes 9220
  13.5 3.6 %copy-start.30 = (f32[768]{0:T(1024)S(1)}, f32[768]{0:T(1024)}, u32[]{:S(2)}) copy-start(f32[768]{0:T(1024)} %convert_element_type.53) | copy-start | bytes 9220
  14.2 2.5 copy-start.26
  16.5 0.6 copy-start.21
  17.2 0.6 copy-start.25
  17.2 3.9 %copy-start.33 = (bf16[4]{0:T(256)(128)(2,1)S(1)}, bf16[4]{0:T(256)(128)(2,1)}, u32[]{:S(2)}) copy-start(bf16[4]{0:T(256)(128)(2,1)} %param.51) | copy-start | bytes 28
  17.7 3.2 %copy-start.35 = (s32[24]{0:T(128)S(1)}, s32[24]{0:T(128)}, u32[]{:S(2)}) copy-start(s32[24]{0:T(128)} %param.31) | copy-start | bytes 292
  17.7 3.6 %copy-start.34 = (bf16[16]{0:T(256)(128)(2,1)S(1)}, bf16[16]{0:T(256)(128)(2,1)}, u32[]{:S(2)}) copy-start(bf16[16]{0:T(256)(128)(2,1)} %param.49) | copy-start | bytes 100
  17.8 6.1 %copy-start.18 = (f32[9,9,48,48]{3,2,1,0:T(8,128)S(1)}, f32[9,9,48,48]{3,2,1,0:T(8,128)}, u32[]{:S(2)}) copy-start(f32[9,9,48,48]{3,2,1,0:T(8,128)} %constant.84.clone) | copy-start | bytes 2239492
  28.6 36.3 %all-to-all-start.1 = ((bf16[24,72,768]{2,1,0:T(8,128)(2,1)}), bf16[24,72,768]{2,1,0:T(8,128)(2,1)S(1)}, u32[]{:S(2)}, u32[]{:S(2)}) async-start(bf16[24,72,768]{2,1,0:T(8,128)(2,1)} %constant_dynamic-update-slice_fusion), calls=%async_computation.1 | async-start | bytes 5308416 | tf_op jit(solution)/shard_map/all_to_all | solution.py:890
  65.0 4.2 %copy-start.3 = (bf16[24,72,768]{2,1,0:T(8,128)(2,1)}, bf16[24,72,768]{2,1,0:T(8,128)(2,1)S(1)}, u32[]{:S(2)}) copy-start(bf16[24,72,768]{2,1,0:T(8,128)(2,1)S(1)} %all-to-all-done.1) | copy-start | bytes 7962628
  85.4 23.7 %collective-permute-start = (bf16[8,2,2,2,2,1,1,24,384]{8,7,6,5,4,3,2,1,0:T(8,128)(2,1)}, bf16[8,2,2,2,2,1,1,24,384]{8,7,6,5,4,3,2,1,0:T(8,128)(2,1)}, u32[]{:S(2)}, u32[]{:S(2)}) collective-permute-start(bf16[8,2,2,2,2,1,1,24,384]{8,7,6,5,4,3,2,1,0:T(8,128)(2,1)} %bitcast.115), channel_id=1, source_target_pairs={{0,1},{1,0},{2,3},{3,2},{4,5},{5,4},{6,7},{7,6},{8,9},{9,8},{10,11... | collective-permute-start | bytes 7077896 | tf_op jit(solution)/shard_map/ppermute | solution.py:627
  108.0 21.5 %collective-permute-start.1 = (bf16[10,2,2,2,2,1,1,24,384]{8,7,6,5,4,3,2,1,0:T(8,128)(2,1)}, bf16[10,2,2,2,2,1,1,24,384]{8,7,6,5,4,3,2,1,0:T(8,128)(2,1)S(1)}, u32[]{:S(2)}, u32[]{:S(2)}) collective-permute-start(bf16[10,2,2,2,2,1,1,24,384]{8,7,6,5,4,3,2,1,0:T(8,128)(2,1)} %bitcast.113), channel_id=1, source_target_pairs={{0,1},{1,0},{2,3},{3,2},{4,5},{5,4},{6,7},{7,6},{8,9},{9,8},{10,11... | collective-permute-start | bytes 8847368 | tf_op jit(solution)/shard_map/ppermute | solution.py:627
  112.5 17.0 %collective-permute-start.2 = (bf16[4,2,2,2,1,1,1,24,384]{8,7,6,5,4,3,2,1,0:T(8,128)(2,1)}, bf16[4,2,2,2,1,1,1,24,384]{8,7,6,5,4,3,2,1,0:T(8,128)(2,1)S(1)}, u32[]{:S(2)}, u32[]{:S(2)}) collective-permute-start(bf16[4,2,2,2,1,1,1,24,384]{8,7,6,5,4,3,2,1,0:T(8,128)(2,1)} %get-tuple-element.122.rest_0_), channel_id=1, source_target_pairs={{0,2},{1,3},{2,0},{3,1},{4,6},{5,7},{6,4},{7,5},{8,10},{9,11},{10,... | collective-permute-start | bytes 1769480 | tf_op jit(solution)/shard_map/ppermute | solution.py:627
  113.5 16.0 %collective-permute-start.3 = (bf16[4,2,2,1,2,1,1,24,384]{8,7,6,5,4,3,2,1,0:T(8,128)(2,1)}, bf16[4,2,2,1,2,1,1,24,384]{8,7,6,5,4,3,2,1,0:T(8,128)(2,1)}, u32[]{:S(2)}, u32[]{:S(2)}) collective-permute-start(bf16[4,2,2,1,2,1,1,24,384]{8,7,6,5,4,3,2,1,0:T(8,128)(2,1)} %get-tuple-element.123.rest_1_), channel_id=1, source_target_pairs={{0,4},{4,0},{1,5},{5,1},{2,6},{6,2},{3,7},{7,3},{8,12},{12,8},{9,1... | collective-permute-start | bytes 1769480 | tf_op jit(solution)/shard_map/ppermute | solution.py:627
  129.4 1.6 copy-start
  129.5 1.7 copy-start.8
  131.2 8.6 %copy-start.27 = (bf16[3,2,768]{2,1,0:T(2,128)(2,1)S(1)}, bf16[3,2,768]{2,1,0:T(2,128)(2,1)}, u32[]{:S(2)}) copy-start(bf16[3,2,768]{2,1,0:T(2,128)(2,1)} %copy-done.26) | copy-start | bytes 27652
  135.8 30.5 %collective-permute-start.4 = (bf16[5,2,2,2,1,1,1,24,384]{8,7,6,5,4,3,2,1,0:T(8,128)(2,1)}, bf16[5,2,2,2,1,1,1,24,384]{8,7,6,5,4,3,2,1,0:T(8,128)(2,1)S(1)}, u32[]{:S(2)}, u32[]{:S(2)}) collective-permute-start(bf16[5,2,2,2,1,1,1,24,384]{8,7,6,5,4,3,2,1,0:T(8,128)(2,1)} %get-tuple-element.127.rest_1_), channel_id=1, source_target_pairs={{0,2},{1,3},{2,0},{3,1},{4,6},{5,7},{6,4},{7,5},{8,10},{9,11},{10,... | collective-permute-start | bytes 2211848 | tf_op jit(solution)/shard_map/ppermute | solution.py:627
  136.3 30.0 %collective-permute-start.5 = (bf16[5,2,2,1,2,1,1,24,384]{8,7,6,5,4,3,2,1,0:T(8,128)(2,1)}, bf16[5,2,2,1,2,1,1,24,384]{8,7,6,5,4,3,2,1,0:T(8,128)(2,1)S(1)}, u32[]{:S(2)}, u32[]{:S(2)}) collective-permute-start(bf16[5,2,2,1,2,1,1,24,384]{8,7,6,5,4,3,2,1,0:T(8,128)(2,1)} %get-tuple-element.128.rest_2_), channel_id=1, source_target_pairs={{0,4},{4,0},{1,5},{5,1},{2,6},{6,2},{3,7},{7,3},{8,12},{12,8},{9,1... | collective-permute-start | bytes 2211848 | tf_op jit(solution)/shard_map/ppermute | solution.py:627
  137.3 29.0 %collective-permute-start.6 = (bf16[4,2,2,1,1,1,1,24,384]{8,7,6,5,4,3,2,1,0:T(8,128)(2,1)}, bf16[4,2,2,1,1,1,1,24,384]{8,7,6,5,4,3,2,1,0:T(8,128)(2,1)S(1)}, u32[]{:S(2)}, u32[]{:S(2)}) collective-permute-start(bf16[4,2,2,1,1,1,1,24,384]{8,7,6,5,4,3,2,1,0:T(8,128)(2,1)} %get-tuple-element.129.rest_3_), channel_id=1, source_target_pairs={{0,4},{4,0},{1,5},{5,1},{2,6},{6,2},{3,7},{7,3},{8,12},{12,8},{9,1... | collective-permute-start | bytes 884744 | tf_op jit(solution)/shard_map/ppermute | solution.py:627
  138.4 27.9 %collective-permute-start.7 = (bf16[4,2,2,1,1,1,1,24,384]{8,7,6,5,4,3,2,1,0:T(8,128)(2,1)}, bf16[4,2,2,1,1,1,1,24,384]{8,7,6,5,4,3,2,1,0:T(8,128)(2,1)S(1)}, u32[]{:S(2)}, u32[]{:S(2)}) collective-permute-start(bf16[4,2,2,1,1,1,1,24,384]{8,7,6,5,4,3,2,1,0:T(8,128)(2,1)} %get-tuple-element.130.rest_4_), channel_id=1, source_target_pairs={{0,2},{1,3},{2,0},{3,1},{4,6},{5,7},{6,4},{7,5},{8,10},{9,11},{10,... | collective-permute-start | bytes 884744 | tf_op jit(solution)/shard_map/ppermute | solution.py:627
  166.3 0.7 copy-start.16
  166.3 0.8 copy-start.17
  166.3 1.0 copy-start.4
  166.4 1.2 copy-start.5
  171.3 14.5 %collective-permute-start.8 = (bf16[10,2,2,2,2,1,1,24,384]{8,7,6,5,4,3,2,1,0:T(8,128)(2,1)}, bf16[10,2,2,2,2,1,1,24,384]{8,7,6,5,4,3,2,1,0:T(8,128)(2,1)S(1)}, u32[]{:S(2)}, u32[]{:S(2)}) collective-permute-start(bf16[10,2,2,2,2,1,1,24,384]{8,7,6,5,4,3,2,1,0:T(8,128)(2,1)} %bitcast.134), channel_id=1, source_target_pairs={{0,1},{1,0},{2,3},{3,2},{4,5},{5,4},{6,7},{7,6},{8,9},{9,8},{10,11... | collective-permute-start | bytes 8847368 | tf_op jit(solution)/shard_map/ppermute | solution.py:627
  171.3 14.5 %collective-permute-start.9 = (bf16[5,2,2,1,1,1,1,24,384]{8,7,6,5,4,3,2,1,0:T(8,128)(2,1)}, bf16[5,2,2,1,1,1,1,24,384]{8,7,6,5,4,3,2,1,0:T(8,128)(2,1)}, u32[]{:S(2)}, u32[]{:S(2)}) collective-permute-start(bf16[5,2,2,1,1,1,1,24,384]{8,7,6,5,4,3,2,1,0:T(8,128)(2,1)} %get-tuple-element.145.rest_0_), channel_id=1, source_target_pairs={{0,4},{4,0},{1,5},{5,1},{2,6},{6,2},{3,7},{7,3},{8,12},{12,8},{9,1... | collective-permute-start | bytes 1105928 | tf_op jit(solution)/shard_map/ppermute | solution.py:627
  171.9 13.9 %collective-permute-start.10 = (bf16[5,2,2,1,1,1,1,24,384]{8,7,6,5,4,3,2,1,0:T(8,128)(2,1)}, bf16[5,2,2,1,1,1,1,24,384]{8,7,6,5,4,3,2,1,0:T(8,128)(2,1)}, u32[]{:S(2)}, u32[]{:S(2)}) collective-permute-start(bf16[5,2,2,1,1,1,1,24,384]{8,7,6,5,4,3,2,1,0:T(8,128)(2,1)} %get-tuple-element.146.rest_1_), channel_id=1, source_target_pairs={{0,2},{1,3},{2,0},{3,1},{4,6},{5,7},{6,4},{7,5},{8,10},{9,11},{10,... | collective-permute-start | bytes 1105928 | tf_op jit(solution)/shard_map/ppermute | solution.py:627
  172.9 12.9 %collective-permute-start.11 = (bf16[8,2,1,1,1,1,1,24,384]{8,7,6,5,4,3,2,1,0:T(8,128)(2,1)}, bf16[8,2,1,1,1,1,1,24,384]{8,7,6,5,4,3,2,1,0:T(8,128)(2,1)S(1)}, u32[]{:S(2)}, u32[]{:S(2)}) collective-permute-start(bf16[8,2,1,1,1,1,1,24,384]{8,7,6,5,4,3,2,1,0:T(8,128)(2,1)} %get-tuple-element.147.rest_2_), channel_id=1, source_target_pairs={{0,8},{8,0},{16,24},{24,16},{1,9},{9,1},{17,25},{25,17},{2,10},{10... | collective-permute-start | bytes 884744 | tf_op jit(solution)/shard_map/ppermute | solution.py:627
  185.8 0.7 copy-start.13
  185.8 1.6 copy-start.1
  187.5 7.4 %copy-start.20 = (f32[32,1280]{1,0:T(8,128)S(1)}, f32[32,1280]{1,0:T(8,128)}, u32[]{:S(2)}) copy-start(f32[32,1280]{1,0:T(8,128)} %pad.9.refs_22_) | copy-start | bytes 491524
  192.2 22.0 %collective-permute-start.12 = (bf16[5,2,2,2,1,1,1,24,384]{8,7,6,5,4,3,2,1,0:T(8,128)(2,1)}, bf16[5,2,2,2,1,1,1,24,384]{8,7,6,5,4,3,2,1,0:T(8,128)(2,1)S(1)}, u32[]{:S(2)}, u32[]{:S(2)}) collective-permute-start(bf16[5,2,2,2,1,1,1,24,384]{8,7,6,5,4,3,2,1,0:T(8,128)(2,1)} %get-tuple-element.159), channel_id=1, source_target_pairs={{0,2},{1,3},{2,0},{3,1},{4,6},{5,7},{6,4},{7,5},{8,10},{9,11},{10,... | collective-permute-start | bytes 2211848 | tf_op jit(solution)/shard_map/ppermute | solution.py:627
  193.3 20.9 %collective-permute-start.13 = (bf16[5,2,2,1,2,1,1,24,384]{8,7,6,5,4,3,2,1,0:T(8,128)(2,1)}, bf16[5,2,2,1,2,1,1,24,384]{8,7,6,5,4,3,2,1,0:T(8,128)(2,1)S(1)}, u32[]{:S(2)}, u32[]{:S(2)}) collective-permute-start(bf16[5,2,2,1,2,1,1,24,384]{8,7,6,5,4,3,2,1,0:T(8,128)(2,1)} %get-tuple-element.160), channel_id=1, source_target_pairs={{0,4},{4,0},{1,5},{5,1},{2,6},{6,2},{3,7},{7,3},{8,12},{12,8},{9,1... | collective-permute-start | bytes 2211848 | tf_op jit(solution)/shard_map/ppermute | solution.py:627
  194.8 19.4 %collective-permute-start.14 = (bf16[10,2,1,1,1,1,1,24,384]{8,7,6,5,4,3,2,1,0:T(8,128)(2,1)}, bf16[10,2,1,1,1,1,1,24,384]{8,7,6,5,4,3,2,1,0:T(8,128)(2,1)S(1)}, u32[]{:S(2)}, u32[]{:S(2)}) collective-permute-start(bf16[10,2,1,1,1,1,1,24,384]{8,7,6,5,4,3,2,1,0:T(8,128)(2,1)} %get-tuple-element.161), channel_id=1, source_target_pairs={{0,8},{8,0},{16,24},{24,16},{1,9},{9,1},{17,25},{25,17},{2,10},{10... | collective-permute-start | bytes 1105928 | tf_op jit(solution)/shard_map/ppermute | solution.py:627
  195.7 17.3 %all-to-all-start.2 = ((f32[32,1,1280]{2,1,0:T(1,128)}), f32[32,1,1280]{2,1,0:T(1,128)S(1)}, u32[]{:S(2)}, u32[]{:S(2)}) async-start(f32[32,1,1280]{2,1,0:T(1,128)} %copy.117), calls=%async_computation.2 | async-start | bytes 327680 | tf_op jit(solution)/shard_map/all_to_all | solution.py:1445
  200.6 13.6 %collective-permute-start.15 = (bf16[8,1,1,1,1,1,1,24,384]{8,7,6,5,4,3,2,1,0:T(8,128)(2,1)}, bf16[8,1,1,1,1,1,1,24,384]{8,7,6,5,4,3,2,1,0:T(8,128)(2,1)S(1)}, u32[]{:S(2)}, u32[]{:S(2)}) collective-permute-start(bf16[8,1,1,1,1,1,1,24,384]{8,7,6,5,4,3,2,1,0:T(8,128)(2,1)} %get-tuple-element.162), channel_id=1, source_target_pairs={{0,16},{8,24},{16,0},{24,8},{1,17},{9,25},{17,1},{25,9},{2,18},{10... | collective-permute-start | bytes 442376 | tf_op jit(solution)/shard_map/ppermute | solution.py:627
  214.2 0.7 copy-start.24
  214.2 0.8 copy-start.10
  214.2 1.0 copy-start.6
  214.2 1.3 copy-start.7
  219.5 12.8 %collective-permute-start.16 = (bf16[5,2,2,1,1,1,1,24,384]{8,7,6,5,4,3,2,1,0:T(8,128)(2,1)}, bf16[5,2,2,1,1,1,1,24,384]{8,7,6,5,4,3,2,1,0:T(8,128)(2,1)S(1)}, u32[]{:S(2)}, u32[]{:S(2)}) collective-permute-start(bf16[5,2,2,1,1,1,1,24,384]{8,7,6,5,4,3,2,1,0:T(8,128)(2,1)} %get-tuple-element.164.refs_20_), channel_id=1, source_target_pairs={{0,4},{4,0},{1,5},{5,1},{2,6},{6,2},{3,7},{7,3},{8,12},{12,8},{9,1... | collective-permute-start | bytes 1105928 | tf_op jit(solution)/shard_map/ppermute | solution.py:627
  221.0 11.3 %collective-permute-start.17 = (bf16[5,2,2,1,1,1,1,24,384]{8,7,6,5,4,3,2,1,0:T(8,128)(2,1)}, bf16[5,2,2,1,1,1,1,24,384]{8,7,6,5,4,3,2,1,0:T(8,128)(2,1)S(1)}, u32[]{:S(2)}, u32[]{:S(2)}) collective-permute-start(bf16[5,2,2,1,1,1,1,24,384]{8,7,6,5,4,3,2,1,0:T(8,128)(2,1)} %get-tuple-element.165.refs_21_), channel_id=1, source_target_pairs={{0,2},{1,3},{2,0},{3,1},{4,6},{5,7},{6,4},{7,5},{8,10},{9,11},{10,... | collective-permute-start | bytes 1105928 | tf_op jit(solution)/shard_map/ppermute | solution.py:627
  222.5 9.8 %collective-permute-start.18 = (bf16[10,1,1,1,1,1,1,24,384]{8,7,6,5,4,3,2,1,0:T(8,128)(2,1)}, bf16[10,1,1,1,1,1,1,24,384]{8,7,6,5,4,3,2,1,0:T(8,128)(2,1)S(1)}, u32[]{:S(2)}, u32[]{:S(2)}) collective-permute-start(bf16[10,1,1,1,1,1,1,24,384]{8,7,6,5,4,3,2,1,0:T(8,128)(2,1)} %get-tuple-element.166.refs_22_), channel_id=1, source_target_pairs={{0,16},{8,24},{16,0},{24,8},{1,17},{9,25},{17,1},{25,9},{2,18},{10... | collective-permute-start | bytes 552968 | tf_op jit(solution)/shard_map/ppermute | solution.py:627
  232.3 0.7 copy-start.23
  232.3 0.8 copy-start.14
  232.3 0.9 copy-start.15
  236.8 10.7 %collective-permute-start.19 = (bf16[10,2,1,1,1,1,1,24,384]{8,7,6,5,4,3,2,1,0:T(8,128)(2,1)}, bf16[10,2,1,1,1,1,1,24,384]{8,7,6,5,4,3,2,1,0:T(8,128)(2,1)S(1)}, u32[]{:S(2)}, u32[]{:S(2)}) collective-permute-start(bf16[10,2,1,1,1,1,1,24,384]{8,7,6,5,4,3,2,1,0:T(8,128)(2,1)} %get-tuple-element.168.refs_10_), channel_id=1, source_target_pairs={{0,8},{8,0},{16,24},{24,16},{1,9},{9,1},{17,25},{25,17},{2,10},{10... | collective-permute-start | bytes 1105928 | tf_op jit(solution)/shard_map/ppermute | solution.py:627
  236.8 22.4 %all-to-all-start.3 = ((bf16[8,112,768]{2,1,0:T(8,128)(2,1)}), bf16[8,112,768]{2,1,0:T(8,128)(2,1)S(1)}, u32[]{:S(2)}, u32[]{:S(2)}) async-start(bf16[8,112,768]{2,1,0:T(8,128)(2,1)} %get-tuple-element.171.grad_ref), calls=%async_computation.3 | async-start | bytes 2752512 | tf_op jit(solution)/shard_map/all_to_all | solution.py:890
  240.4 11.3 %copy-start.19 = (f32[32,1,1280]{2,0,1:T(8,128)S(1)}, f32[32,1,1280]{2,0,1:T(8,128)}, u32[]{:S(2)}) copy-start(f32[32,1,1280]{2,0,1:T(8,128)} %copy.126) | copy-start | bytes 491524
  247.5 0.8 copy-start.11
  251.0 21.3 %collective-permute-start.20 = (bf16[10,1,1,1,1,1,1,24,384]{8,7,6,5,4,3,2,1,0:T(8,128)(2,1)}, bf16[10,1,1,1,1,1,1,24,384]{8,7,6,5,4,3,2,1,0:T(8,128)(2,1)S(1)}, u32[]{:S(2)}, u32[]{:S(2)}) collective-permute-start(bf16[10,1,1,1,1,1,1,24,384]{8,7,6,5,4,3,2,1,0:T(8,128)(2,1)} %serve_8.1), channel_id=1, source_target_pairs={{0,16},{8,24},{16,0},{24,8},{1,17},{9,25},{17,1},{25,9},{2,18},{10... | collective-permute-start | bytes 552968 | tf_op jit(solution)/shard_map/ppermute | solution.py:627
  259.2 5.0 %copy-start.12 = (bf16[8,112,768]{2,1,0:T(8,128)(2,1)}, bf16[8,112,768]{2,1,0:T(8,128)(2,1)S(1)}, u32[]{:S(2)}) copy-start(bf16[8,112,768]{2,1,0:T(8,128)(2,1)S(1)} %all-to-all-done.3.back_ref) | copy-start | bytes 4128772
  262.5 8.8 %copy-start.9 = (bf16[8,3,8,2,4,2,4]{6,5,4,3,2,1,0:T(2,128)(2,1)}, bf16[8,3,8,2,4,2,4]{6,5,4,3,2,1,0:T(2,128)(2,1)S(1)}, u32[]{:S(2)}) copy-start(bf16[8,3,8,2,4,2,4]{6,5,4,3,2,1,0:T(2,128)(2,1)S(1)} %copy.119) | copy-start | bytes 73732
  272.2 0.7 copy-start.22
where the time goes:
time: 280 us; the launch traced here: 276 us
  Pallas kernels  153 us (55%)
  local copies, waits for them, and re-layouts  40.4 us (14%)
  starting transfers between devices  38.7 us (14%)
  waiting for transfers between devices  34.3 us (12%)
  other arithmetic  5.83 us (2%)
    pallas_call x8, Pallas kernels, serve(): pl.pallas_call(functools.partial(serve_kernel, tasks), grid_spec=pltpu.Pr...  29.6 us
    pallas_call x1, Pallas kernels, per_device(): pl.pallas_call(functools.partial(up_kernel, own), grid=(chunks + 1,), in_...  22.6 us
    pallas_call x2, Pallas kernels, per_device(): pl.pallas_call(attend_back_kernel, grid=(number,), in_specs=[pl.BlockSpec...  22.5 us
    ppermute x21, starting transfers between devices, swap(): return lax.ppermute(block, axis, [(i, i ^ gap) for i in range(count)])  21 us
    pallas_call x1, Pallas kernels, per_device(): pl.pallas_call(attend_kernel, grid=(share,), in_specs=[item_block, per_sh...  17.2 us
    ppermute x21, waiting for transfers between devices, swap(): return lax.ppermute(block, axis, [(i, i ^ gap) for i in range(count)])  16.4 us
    pallas_call x1, Pallas kernels, per_device(): pl.pallas_call(forward_kernel, grid=(chunks,), in_specs=[whole((count, wi...  14.4 us
    all_to_all x3, starting transfers between devices, to_items(): return lax.all_to_all(array, PLANE, split_axis=0, concat_axis=0, tiled=True)  12.8 us
  transfers between devices with their start and end apart: 25, of which 7 were waited for; matrix products, arithmetic and copies ran while one was open for 13% of the time, Pallas kernels for 39%

commit v1 on v0

--- a/solution.py
+++ b/solution.py
@@ -209,7 +209,9 @@
     shiftf_ref,
     w_head_ref,
     w_conv_ref,
-    lanes_ref,
+    b_head_ref,
+    b_conv_ref,
+    weight_ref,
     target_ref,
     after_ref,
     result_ref,
@@ -226,6 +228,11 @@
     patch_values, width = w_head_ref.shape
     items = lanes // patch_values
 
+    weight = flat(weight_ref)
+    weight_lanes = jnp.concatenate(
+        [jnp.broadcast_to(weight[:, i : i + 1], (1, patch_values)) for i in range(items)], 1
+    )
+
     def head_of(i):
         parts = [w_head_ref[...]]
         if i > 0:
@@ -239,7 +246,7 @@
     total[...] = unit
     normedf = (unit * flat(gainf_ref) + flat(shiftf_ref)).astype(BF)
     normed2_final = [normedf[i * per_item : (i + 1) * per_item] for i in range(items)]
-    patches = lanes_ref[0:1]
+    patches = jnp.concatenate([flat(b_head_ref)] * items, 1)
     for i in range(items):
         patches = patches + dot(normed2_final[i], heads[i], 1, 1)
     patches = patches.astype(BF)
@@ -258,11 +265,11 @@
             wanted = own + ((row_off - 1) * 1024 + (col_off - 1))
             shifts.append(jnp.where(wanted == other, 1.0, 0.0).astype(BF))
     windows = [dot(shift, patches, 1, 0).astype(BF) for shift in shifts]
-    result = lanes_ref[1:2]
+    result = jnp.concatenate([flat(b_conv_ref)] * (lanes // b_conv_ref.shape[0]), 1)
     for k in range(9):
         result = result + dot(windows[k], w_conv_ref[k], 1, 0)
     result_ref[...] = result.astype(BF)
-    grad_result = (lanes_ref[2:3] * (result - target_ref[...])).astype(BF)
+    grad_result = (weight_lanes * (result - target_ref[...])).astype(BF)
     conv_bias_ref[...] = row_sum(grad_result.astype(F32))
     grad_patches = jnp.zeros(target_ref.shape, F32)
     for k in range(9):
@@ -316,15 +323,26 @@
     w_down_ref,
     w_up_ref,
     normed2_ref,
-    hidden1_ref,
+    hidden1_hbm,
     gain2_ref,
-    grad_hidden2_ref,
-    mixed_ref,
+    grad_hidden2_hbm,
+    mixed_hbm,
     core_ref,
     *rest,
 ):
-    total = rest[-1]
-    rest = rest[-7 if can_split(own) else -6 : -1]
+    total, hidden1_ref, grad_hidden2_ref, mixed_ref, sems = rest[-5:]
+    rest = rest[-11 if can_split(own) else -10 : -5]
+    late_copies = [
+        pltpu.make_async_copy(hidden1_hbm, hidden1_ref, sems.at[0]),
+        pltpu.make_async_copy(grad_hidden2_hbm, grad_hidden2_ref, sems.at[1]),
+        pltpu.make_async_copy(mixed_hbm, mixed_ref, sems.at[2]),
+    ]
+
+    @pl.when(pl.program_id(0) == 0)
+    def _():
+        for copy in late_copies:
+            copy.start()
+
     grad_b_up_ref, grad_hidden1_ref, grad_branch_ref, sums_ref = rest[:4]
     rest = rest[4:]
     step = pl.program_id(0)
@@ -357,6 +375,8 @@
 
     @pl.when(step == steps - 1)
     def _():
+        for copy in late_copies:
+            copy.wait()
         unit, scaled = norm_parts(hidden1_ref[...])
         grad_normed2 = total[...]
         sums_ref[0:1] = row_sum(grad_normed2 * unit)
@@ -377,6 +397,7 @@
 
 
 def attend_back_kernel(
+    opening,
     hidden_ref,
     grad_hidden1_ref,
     grad_branch_ref,
@@ -386,7 +407,7 @@
     key_extra_ref,
     value_extra_ref,
     gain_ref,
-    w_qkv_ref,
+    w_qkv_hbm,
     w_out_ref,
     sums_in_ref,
     *rest,
@@ -402,7 +423,16 @@
         grad_probs_extra_ref,
         grad_scores_ref,
         grad_scores_extra_ref,
-    ) = rest[-10:]
+        w_qkv_ref,
+        sem,
+    ) = rest[-12:]
+    step = pl.program_id(0)
+    late_copy = pltpu.make_async_copy(w_qkv_hbm, w_qkv_ref, sem)
+
+    @pl.when(step == 0)
+    def _():
+        late_copy.start()
+
     width = w_out_ref.shape[0]
     head_dim = width // HEADS
     scale = head_dim ** (-0.5)
@@ -437,12 +467,17 @@
         grad_qkv_ref[0, low : low + head_dim, :] = (grad_query * scale).astype(BF)
         grad_qkv_ref[0, width + low : width + low + head_dim, :] = (grad_key * scale).astype(BF)
         grad_qkv_ref[0, 2 * width + low : 2 * width + low + head_dim, :] = grad_value.astype(BF)
+
+    @pl.when(step == 0)
+    def _():
+        late_copy.wait()
+
     grad_normed = dot(grad_qkv_ref[0], w_qkv_ref[...], 0, 1)
     unit, scaled = norm_parts(hidden_ref[...].reshape(rows, width).astype(F32))
 
     @pl.when(pl.program_id(0) == 0)
     def _():
-        sums_ref[...] = sums_in_ref[...]
+        sums_ref[...] = jnp.zeros_like(sums_ref) if opening else sums_in_ref[...]
 
     sums_ref[0:1] += row_sum(grad_normed * unit)
     sums_ref[1:2] += row_sum(grad_normed)
@@ -494,7 +529,7 @@
     normed_ref,
     normed_extra_ref,
     pairs_ref,
-    joined_ref,
+    joined_hbm,
     grad_ref,
     joined_extra_ref,
     grad_extra_ref,
@@ -504,8 +539,20 @@
     core_ref,
     *rest,
 ):
+    joined_ref, sem = rest[-2:]
+    rest = rest[:-2]
     step = pl.program_id(0)
     split = can_split(own)
+    late_copy = pltpu.make_async_copy(joined_hbm, joined_ref, sem)
+
+    @pl.when(step == 0)
+    def _():
+        late_copy.start()
+
+    @pl.when(step == 3)
+    def _():
+        late_copy.wait()
+
     groups, items, _, width = joined_ref.shape
     local = (grad_ref.shape[1] - 16) // items
 
@@ -942,16 +989,10 @@
     lanes = share * patch_values
     spread = jnp.tile(w_conv.reshape(9, chans, chans), (1, lanes // chans, lanes // chans))
     kernel = jnp.sum(jnp.asarray(conv_lanes(share)) * spread[None].astype(F32), 1).astype(BF)
-    lane_rows = jnp.concatenate(
-        [
-            jnp.tile(b_head.astype(F32), share),
-            jnp.tile(b_conv.astype(F32), lanes // chans),
-            jnp.repeat(weight, patch_values),
-        ]
-    ).reshape(3, lanes)
-    joined = lax.optimization_barrier(
-        (joined, key_extra, value_extra, kernel, lane_rows, normed_extra)
-    )[0]
+    table = place_table()
+    joined, table, joined_extra = lax.optimization_barrier(
+        (joined, table, joined_extra, key_extra, value_extra, kernel, weight, normed_extra)
+    )[:3]
     joined = to_items(joined).reshape(groups, share, joined_rows, width)
     thirds = joined[:, :, 2 * local : 2 * local + thirds.shape[1]].astype(F32)
     thirds = thirds.reshape(groups, share, 3, local, patch_values)
@@ -1060,7 +1101,9 @@
             vec,
             whole((patch_values, width)),
             whole((9, lanes, lanes)),
-            whole((3, lanes)),
+            whole((patch_values,)),
+            whole((chans,)),
+            whole((share,)),
             whole((per_item, lanes)),
             pl.BlockSpec(memory_space=pl.ANY),
         ],
@@ -1094,13 +1137,14 @@
         final_shift,
         w_head.T,
         kernel,
-        lane_rows,
+        b_head,
+        b_conv,
+        weight,
         target_own,
         joined,
     )
 
     any_place = pl.BlockSpec(memory_space=pl.ANY)
-    table = place_table()
     core = lax.axis_index("tx") % 2
     core = core.astype(jnp.int32).reshape(1)
     core_spec = pl.BlockSpec(memory_space=pltpu.SMEM)
@@ -1157,10 +1201,10 @@
             pl.BlockSpec((chunk, width), lambda j: (held_col(j), 0)),
             pl.BlockSpec((width, chunk), lambda j: (0, held_col(j))),
             whole((count, width)),
-            whole((count, width)),
+            any_place,
             vec,
-            whole((count, width)),
-            whole((share, width, per_item)),
+            any_place,
+            any_place,
             core_spec,
         ]
         + [any_place] * len(grad_w_down),
@@ -1178,7 +1222,13 @@
             sds((8, width), F32),
         ]
         + [up_shape(units)] * up_outs,
-        scratch_shapes=[pltpu.VMEM((count, width), F32)],
+        scratch_shapes=[
+            pltpu.VMEM((count, width), F32),
+            pltpu.VMEM((count, width), F32),
+            pltpu.VMEM((count, width), F32),
+            pltpu.VMEM((share, width, per_item), BF),
+            pltpu.SemaphoreType.DMA((3,)),
+        ],
         compiler_params=params(),
         cost_estimate=cost(count * (6 * hidden_units + 2 * width) * width, 25e6),
         name="up_weight",
@@ -1214,7 +1264,7 @@
     else:
         early = []
     grad_qkv, grad_key_extra, grad_value_extra = [], [], []
-    sums_attend = jnp.zeros((8, width), F32)
+    sums_attend = sums_up
     grad_hidden0 = None
     back_rows = share * local + 16
     for first, number in ((0, share - 1), (share - 1, 1)):
@@ -1227,7 +1277,7 @@
 
         held = [grad_hidden0] if first else []
         outs = pl.pallas_call(
-            attend_back_kernel,
+            functools.partial(attend_back_kernel, first == 0),
             grid=(number,),
             in_specs=[
                 pl.BlockSpec(
@@ -1241,7 +1291,7 @@
                 one(HEADS, EXTRA_PAD, head_dim),
                 one(HEADS, EXTRA_PAD, head_dim),
                 vec,
-                whole((width, 3 * width)),
+                any_place,
                 whole((width, width)),
                 whole((8, width)),
             ]
@@ -1267,6 +1317,8 @@
                 pltpu.VMEM((HEADS, EXTRA_PAD, per_item), F32),
                 pltpu.VMEM((HEADS, per_item, per_item), BF),
                 pltpu.VMEM((HEADS, EXTRA_PAD, per_item), BF),
+                pltpu.VMEM((width, 3 * width), BF),
+                pltpu.SemaphoreType.DMA,
             ],
             compiler_params=params(),
             cost_estimate=cost(
@@ -1364,7 +1416,7 @@
             pl.BlockSpec(
                 (1, extra_rows, width), lambda j: (jnp.clip(j - 1, 0, 1), 0, 0)
             ),
-            whole(joined.shape),
+            any_place,
             pl.BlockSpec((groups, back_rows, half), lambda j: (0, 0, skip_col(j))),
             whole((extra_rows, 2 * width)),
             pl.BlockSpec((extra_rows, half), lambda j: (0, skip_col(j))),
@@ -1376,6 +1428,7 @@
         + [core_spec],
         out_specs=[late_spec] * late_outs,
         out_shape=[late_shape(10)] * late_outs,
+        scratch_shapes=[pltpu.VMEM(joined.shape, BF), pltpu.SemaphoreType.DMA],
         compiler_params=params(),
         cost_estimate=cost(count * 10 * width * width, 12e6),
         name="late_weight",

time: 280 us -> 275 us (0.982)
  Pallas kernels: 153 us -> 149 us
    unnamed x75 -> x71, local copies, waits for them, and re-layouts: 11.7 us -> 11.8 us
  transfers between devices with their start and end apart: 25 -> 25, of which waited for: 7 -> 8; matrix products, arithmetic and copies ran while one was open for 13% -> 13% of each run, Pallas kernels for 39% -> 38%
where the time goes in v1:
time: 275 us; the launch traced here: 271 us
  Pallas kernels  149 us (54%)
  local copies, waits for them, and re-layouts  39.2 us (14%)
  starting transfers between devices  39.2 us (14%)
  waiting for transfers between devices  32 us (12%)
  other arithmetic  7.02 us (3%)
    pallas_call x8, Pallas kernels, serve(): pl.pallas_call(functools.partial(serve_kernel, tasks), grid_spec=pltpu.Pr...  29.6 us
    pallas_call x2, Pallas kernels, per_device(): pl.pallas_call(functools.partial(attend_back_kernel, first == 0), grid=(n...  21.5 us
    ppermute x21, starting transfers between devices, swap(): return lax.ppermute(block, axis, [(i, i ^ gap) for i in range(count)])  20.9 us
    pallas_call x1, Pallas kernels, per_device(): pl.pallas_call(functools.partial(up_kernel, own), grid=(chunks + 1,), in_...  20.8 us
    pallas_call x1, Pallas kernels, per_device(): pl.pallas_call(attend_kernel, grid=(share,), in_specs=[item_block, per_sh...  17.1 us
    ppermute x21, waiting for transfers between devices, swap(): return lax.ppermute(block, axis, [(i, i ^ gap) for i in range(count)])  16.4 us
    pallas_call x1, Pallas kernels, per_device(): pl.pallas_call(forward_kernel, grid=(chunks,), in_specs=[whole((count, wi...  14.4 us
    all_to_all x3, starting transfers between devices, to_items(): return lax.all_to_all(array, PLANE, split_axis=0, concat_axis=0, tiled=True)  12.8 us
  transfers between devices with their start and end apart: 25, of which 8 were waited for; matrix products, arithmetic and copies ran while one was open for 13% of the time, Pallas kernels for 38%

profile of v1, /device:TPU:0, one launch (start us, length us, event | category | flops | bytes accessed | tf_op | source)
XLA Modules:
  0.0 270.7 jit_solution(12144811635221929764)
XLA Ops:
  0.7 5.6 %merge.1 = (bf16[24,32,768]{2,1,0:T(8,128)(2,1)}, bf16[24,72,768]{2,1,0:T(8,128)(2,1)}) custom-call(bf16[24,8,4,768]{3,2,1,0:T(4,128)(2,1)} %tokens_ref.1, bf16[24,8,4,768]{3,2,1,0:T(4,128)(2,1)} %skip_ref.1, bf16[1536,768]{1,0:T(8,128)(2,1)} %w_skip_ref.3, bf16[768]{0:T(1024)(128)(2,1)} %b_skip_ref.1), custom_call_target="tpu_custom_call" | custom-call | flops 1024 | bytes 1024 | tf_op jit(solution)/shard_map/merge/pallas_call | solution.py:943
  6.2 5.4 %all-to-all-start = ((bf16[24,32,768]{2,1,0:T(8,128)(2,1)}), bf16[24,32,768]{2,1,0:T(8,128)(2,1)}, u32[]{:S(2)}, u32[]{:S(2)}) async-start(bf16[24,32,768]{2,1,0:T(8,128)(2,1)} %get-tuple-element.104), calls=%async_computation | async-start | bytes 2359296 | tf_op jit(solution)/shard_map/all_to_all | solution.py:937
  11.7 1.3 convert_element_type.46
  13.0 1.3 convert_element_type.48
  16.2 2.2 fusion.16
  20.5 0.8 copy.108
  22.9 1.0 copy.110
  26.0 0.9 multiply_reduce_fusion.w_conv_ref
  27.5 1.1 all-to-all-done
  28.6 3.8 %all-to-all-start.1 = ((bf16[24,72,768]{2,1,0:T(8,128)(2,1)}), bf16[24,72,768]{2,1,0:T(8,128)(2,1)S(1)}, u32[]{:S(2)}, u32[]{:S(2)}) async-start(bf16[24,72,768]{2,1,0:T(8,128)(2,1)} %constant_dynamic-update-slice_fusion), calls=%async_computation.1 | async-start | bytes 5308416 | tf_op jit(solution)/shard_map/all_to_all | solution.py:937
  32.4 17.1 %attend.1 = (bf16[3,256,768]{2,1,0:T(8,128)(2,1)}, bf16[3,2304,256]{2,1,0:T(8,128)(2,1)}, bf16[3,12,256,256]{3,2,1,0:T(8,128)(2,1)}, bf16[3,12,8,256]{3,2,1,0:T(...) custom-call(bf16[8,3,32,768]{3,2,1,0:T(8,128)(2,1)} %bitcast.1.hidden_ref, ...), custom_call_target="tpu_custom_call" | custom-call | flops 1024 | bytes 1024 | tf_op jit(solution)/shard_map/attend/pallas_call | solution.py:1011
  49.6 14.4 %forward.1 = (bf16[4,768,768]{2,1,0:T(8,128)(2,1)}, bf16[4,768,768]{2,1,0:T(8,128)(2,1)}, bf16[768,768]{1,0:T(8,128)(2,1)}, f32[768,768]{1,0:T(8,128)}) custom-call(f32[768,768]{1,0:T(8,128)} %bitcast.106, bf16[768]{0:T(1024)(128)(2,1)} %gain2_ref.3, bf16[768]{0:T(1024)(128)(2,1)} %shift2_ref.1, bf16[3072]{0:T(1024)(128)(2,1)} %b_up_ref.1, ...), custom_call_target="tpu_custom_call" | custom-call | flops 1024 | bytes 1024 | tf_op jit(solution)/shard_map/forward/pallas_call | solution.py:1062
  63.9 1.0 all-to-all-done.1
  65.0 1.8 reshape.211
  66.8 1.3 fusion.5
  68.4 0.8 copy.114.target_ref
  69.2 8.2 %turn.1 = (bf16[256,48]{1,0:T(8,128)(2,1)}, f32[768,768]{1,0:T(8,128)}, bf16[768,768]{1,0:T(8,128)(2,1)}, f32[1,48]{1,0:T(1,128)}, f32[8,768]{1,0:T(8,128)}, /*i...) custom-call(f32[768,768]{1,0:T(8,128)} %get-tuple-element.106.hidden2_ref, bf16[768]{0:T(1024)(128)(2,1)} %gainf_ref.1, ...), custom_call_target="tpu_custom_call" | custom-call | flops 1024 | bytes 1024 | tf_op jit(solution)/shard_map/turn/pallas_call | solution.py:1095
  77.4 8.1 %down_weight.1 = (bf16[8,16,24,384]{3,2,1,0:T(8,128)(2,1)}, bf16[8,16,24,384]{3,2,1,0:T(8,128)(2,1)}) custom-call(bf16[4,768,768]{2,1,0:T(8,128)(2,1)} %get-tuple-element.115.active_ref, bf16[768,768]{1,0:T(8,128)(2,1)} %get-tuple-element.111.grad_down_ref, s32[1]{0:T(128)} %bitcast.23.core_ref), custom_call_target="tpu_custom_call" | custom-call | flops 1024 | bytes 1024 | tf_op jit(solution)/shard_map/down_weight/pallas_call | solution.py:1173
  85.5 20.8 %up_weight.1 = (f32[4,8,768]{2,1,0:T(8,128)}, f32[768,768]{1,0:T(8,128)}, bf16[768,768]{1,0:T(8,128)(2,1)}, f32[8,768]{1,0:T(8,128)}, bf16[10,16,24,384]{3,2,1,0...) custom-call(bf16[4,768,768]{2,1,0:T(8,128)(2,1)} %get-tuple-element.110.slope_ref, ...), custom_call_target="tpu_custom_call" | custom-call | flops 1024 | bytes 1024 | tf_op jit(solution)/shard_map/up_weight/pallas_call | solution.py:1195
  106.9 3.4 %serve_0.1 = (bf16[4,2,2,2,1,1,1,24,384]{8,7,6,5,4,3,2,1,0:T(8,128)(2,1)}, bf16[4,2,2,1,2,1,1,24,384]{8,7,6,5,4,3,2,1,0:T(8,128)(2,1)}) custom-call(s32[8]{0:T(128)} %stack.35.places_ref, bf16[8,2,2,2,2,1,1,24,384]{8,7,6,5,4,3,2,1,0:T(8,128)(2,1)} %bitcast.91, ...), custom_call_target="tpu_custom_call" | custom-call | flops 1024 | bytes 1024 | tf_op jit(solution)/shard_map/serve_0/pallas_call | solution.py:712
  110.3 1.0 collective-permute-start.2
  111.3 1.5 collective-permute-start.3
  112.8 13.5 %attend_back.2 = (bf16[2,2304,256]{2,1,0:T(8,128)(2,1)}, f32[2,12,8,64]{3,2,1,0:T(8,128)}, f32[2,12,8,64]{3,2,1,0:T(8,128)}, bf16[8,112,768]{2,1,0:T(8,128)(2,1)}, f32[8,768]{1,0:T(8,128)}) custom-call(bf16[8,3,32,768]{3,2,1,0:T(8,128)(2,1)} %bitcast.1.hidden_ref, f32[3,256,768]{2,1,0:T(8,128)} %bitcast.104, bf16[3,256,768]{2,1,0:T(8,128)(2,1)} %bitcast.111, ...), custom_call_target="tpu_custom_call" | custom-call | flops 1024 | bytes 1024 | tf_op jit(solution)/shard_map/attend_back/pallas_call | solution.py:1279
  127.1 1.3 copy-done
  128.4 4.6 %serve_1.1 = (bf16[5,2,2,2,1,1,1,24,384]{8,7,6,5,4,3,2,1,0:T(8,128)(2,1)}, bf16[5,2,2,1,2,1,1,24,384]{8,7,6,5,4,3,2,1,0:T(8,128)(2,1)}, bf16[4,2,2,1,1,1,1,24,38...) custom-call(s32[8]{0:T(128)} %stack.35.places_ref, ...), custom_call_target="tpu_custom_call" | custom-call | flops 1024 | bytes 1024 | tf_op jit(solution)/shard_map/serve_1/pallas_call | solution.py:712
  133.0 0.9 collective-permute-start.4
  133.9 1.1 collective-permute-start.5
  135.0 0.9 collective-permute-start.6
  135.9 1.1 collective-permute-start.7
  137.8 8.0 %attend_back.3 = (bf16[1,2304,256]{2,1,0:T(8,128)(2,1)}, f32[1,12,8,64]{3,2,1,0:T(8,128)}, f32[1,12,8,64]{3,2,1,0:T(8,128)}, bf16[8,112,768]{2,1,0:T(8,128)(2,1)}, f32[8,768]{1,0:T(8,128)}) custom-call(bf16[8,3,32,768]{3,2,1,0:T(8,128)(2,1)} %bitcast.1.hidden_ref, f32[3,256,768]{2,1,0:T(8,128)} %bitcast.105, ...), custom_call_target="tpu_custom_call", output_to_operand_aliasing={{3}: (12, {})} | custom-call | flops 1024 | bytes 1024 | tf_op jit(solution)/shard_map/attend_back/pallas_call | solution.py:1279
  145.8 3.3 %extra_back.1 = (bf16[2,24,768]{2,1,0:T(8,128)(2,1)}, bf16[24,768]{1,0:T(8,128)(2,1)}, f32[8,768]{1,0:T(8,128)}, bf16[8,112,768]{2,1,0:T(8,128)(2,1)}) custom-call(f32[24,768]{1,0:T(8,128)} %copy-done.21, bf16[768]{0:T(1024)(128)(2,1)} %gain_ref.7, bf16[768,2304]{1,0:T(8,128)(2,1)} %w_value_ref.1, ...), custom_call_target="tpu_custom_call", output_to_operand_aliasing={{3}: (12, {})} | custom-call | flops 1024 | bytes 1024 | tf_op jit(solution)/shard_map/extra_back/pallas_call | solution.py:1354
  149.1 11.4 %late_weight.1 = (bf16[10,16,24,384]{3,2,1,0:T(8,128)(2,1)}, bf16[10,16,24,384]{3,2,1,0:T(8,128)(2,1)}) custom-call(bf16[3,256,768]{2,1,0:T(8,128)(2,1)} %get-tuple-element.142.normed_ref, bf16[24,768]{1,0:T(8,128)(2,1)} %copy-done.25, bf16[2,24,768]{2,1,0:T(8,128)(2,1)} %get-tuple-element.143.pairs_ref, bf16[8,3,72,768]{3,2,1,0:T(8,128)(2,1)} %bitcast.103, ...), custom_call_target="tpu_custom_call" | custom-call | flops 1024 | bytes 1024 | tf_op jit(solution)/shard_map/late_weight/pallas_call | solution.py:1410
  161.9 3.7 %serve_2.1 = (bf16[5,2,2,1,1,1,1,24,384]{8,7,6,5,4,3,2,1,0:T(8,128)(2,1)}, bf16[5,2,2,1,1,1,1,24,384]{8,7,6,5,4,3,2,1,0:T(8,128)(2,1)}, bf16[8,2,1,1,1,1,1,24,384]{8,7,6,5,4,3,2,1,0:T(8,128)(2,1)}) custom-call(s32[8]{0:T(128)} %stack.35.places_ref, bf16[10,2,2,2,2,1,1,24,384]{8,7,6,5,4,3,2,1,0:T(8,128)(2,1)} %bitcast.83, ...), custom_call_target="tpu_custom_call" | custom-call | flops 1024 | bytes 1024 | tf_op jit(solution)/shard_map/serve_2/pallas_call | solution.py:712
  165.6 1.6 collective-permute-start.9
  167.7 2.0 collective-permute-start.11
  169.8 0.9 slice_reduce_fusion
  171.4 3.0 %pack.1 = (f32[25,768]{1,0:T(8,128)}, f32[8,128]{1,0:T(8,128)}) custom-call(f32[8,768]{1,0:T(8,128)} %get-tuple-element.154.sums_attend_ref, f32[8,768]{1,0:T(8,128)} %get-tuple-element.123.sums_in_ref.sums_up_ref, f32[8,768]{1,0:T(8,128)} %get-tuple-element.155.sums_final_ref, f32[3,48,768]{2,1,0:T(8,128)} %get-tuple-element.156.head_sum_ref, ...), custom_call_target="tpu_custom_call" | custom-call | flops 1024 | bytes 1024 | tf_op jit(solution)/shard_map/pack/pallas_call | solution.py:1458
  174.3 1.9 reshape.201
  176.3 1.2 copy.115
  177.5 0.8 copy.116
  178.9 1.0 concatenate.12
  181.4 0.9 copy-done.1
  182.3 4.7 %serve_5.1 = (bf16[5,2,2,2,1,1,1,24,384]{8,7,6,5,4,3,2,1,0:T(8,128)(2,1)}, bf16[5,2,2,1,2,1,1,24,384]{8,7,6,5,4,3,2,1,0:T(8,128)(2,1)}, bf16[10,2,1,1,1,1,1,24,3...) custom-call(s32[8]{0:T(128)} %stack.35.places_ref, ...), custom_call_target="tpu_custom_call" | custom-call | flops 1024 | bytes 1024 | tf_op jit(solution)/shard_map/serve_5/pallas_call | solution.py:712
  187.0 1.5 collective-permute-start.12
  189.1 0.8 copy.117
  189.9 5.5 %all-to-all-start.2 = ((f32[32,1,1280]{2,1,0:T(1,128)}), f32[32,1,1280]{2,1,0:T(1,128)S(1)}, u32[]{:S(2)}, u32[]{:S(2)}) async-start(f32[32,1,1280]{2,1,0:T(1,128)} %copy.117), calls=%async_computation.2 | async-start | bytes 327680 | tf_op jit(solution)/shard_map/all_to_all | solution.py:1498
  195.4 2.9 %collective-permute-start.15 = (bf16[8,1,1,1,1,1,1,24,384]{8,7,6,5,4,3,2,1,0:T(8,128)(2,1)}, bf16[8,1,1,1,1,1,1,24,384]{8,7,6,5,4,3,2,1,0:T(8,128)(2,1)S(1)}, u32[]{:S(2)}, u32[]{:S(2)}) collective-permute-start(bf16[8,1,1,1,1,1,1,24,384]{8,7,6,5,4,3,2,1,0:T(8,128)(2,1)} %get-tuple-element.166), channel_id=1, source_target_pairs={{0,16},{8,24},{16,0},{24,8},{1,17},{9,25},{17,1},{25,9},{2,18},{10... | collective-permute-start | bytes 442376 | tf_op jit(solution)/shard_map/ppermute | solution.py:674
  198.3 9.9 %all-to-all-done.2 = f32[32,1,1280]{2,1,0:T(1,128)S(1)} async-done(((f32[32,1,1280]{2,1,0:T(1,128)}), f32[32,1,1280]{2,1,0:T(1,128)S(1)}, u32[]{:S(2)}, u32[]{:S(2)}) %all-to-all-start.2) | async-done | bytes 163872 | tf_op jit(solution)/shard_map/all_to_all | solution.py:1498
  210.3 4.0 %serve_6.1 = (bf16[5,2,2,1,1,1,1,24,384]{8,7,6,5,4,3,2,1,0:T(8,128)(2,1)}, bf16[5,2,2,1,1,1,1,24,384]{8,7,6,5,4,3,2,1,0:T(8,128)(2,1)}, bf16[10,1,1,1,1,1,1,24,384]{8,7,6,5,4,3,2,1,0:T(8,128)(2,1)}, f32[96,768]{1,0:T(8,128)}) custom-call(s32[8]{0:T(128)} %stack.35.places_ref, bf16[10,2,2,2,2,1,1,24,384]{8,7,6,5,4,3,2,1,0:T(8,128)(2,1)} %bitcast.73, ...), custom_call_target="tpu_custom_call" | custom-call | flops 1024 | bytes 1024 | tf_op jit(solution)/shard_map/serve_6/pallas_call | solution.py:712
  214.3 1.5 collective-permute-start.16
  215.9 1.5 collective-permute-start.17
  217.3 1.1 collective-permute-start.18
  218.4 8.7 %collective-permute-done.18.refs_13_.refs_19_ = bf16[10,1,1,1,1,1,1,24,384]{8,7,6,5,4,3,2,1,0:T(8,128)(2,1)S(1)} collective-permute-done((bf16[10,1,1,1,1,1,1,24,384]{8,7,6,5,4,3,2,1,0:T(8,128)(2,1)}, bf16[10,1,1,1,1,1,1,24,384]{8,7,6,5,4,3,2,1,0:T(8,128)(2,1)S(1)}, u32[]{:S(2)}, u32[]{:S(2)}) %collective-permute-start.18) | collective-permute-done | bytes 184352 | tf_op jit(solution)/shard_map/ppermute | solution.py:674
  228.1 3.5 %serve_7.1 = (bf16[10,2,1,1,1,1,1,24,384]{8,7,6,5,4,3,2,1,0:T(8,128)(2,1)}, f32[24,3072]{1,0:T(8,128)}, f32[24,768]{1,0:T(8,128)}) custom-call(s32[8]{0:T(128)} %stack.35.places_ref, bf16[10,2,2,2,2,1,1,24,384]{8,7,6,5,4,3,2,1,0:T(8,128)(2,1)} %bitcast.75, bf16[10,2,2,2,2,1,1,24,384]{8,7,6,5,4,3,2,1,0:T(8,128)(2,1)} %copy-done.1, ...), custom_call_target="tpu_custom_call" | custom-call | flops 1024 | bytes 1024 | tf_op jit(solution)/shard_map/serve_7/pallas_call | solution.py:712
  231.6 3.6 %all-to-all-start.3 = ((bf16[8,112,768]{2,1,0:T(8,128)(2,1)}), bf16[8,112,768]{2,1,0:T(8,128)(2,1)S(1)}, u32[]{:S(2)}, u32[]{:S(2)}) async-start(bf16[8,112,768]{2,1,0:T(8,128)(2,1)} %get-tuple-element.175.grad_ref), calls=%async_computation.3 | async-start | bytes 2752512 | tf_op jit(solution)/shard_map/all_to_all | solution.py:937
  235.2 7.1 %collective-permute-done.19.refs_4_.refs_9_.refs_10_ = bf16[10,2,1,1,1,1,1,24,384]{8,7,6,5,4,3,2,1,0:T(8,128)(2,1)S(1)} collective-permute-done((bf16[10,2,1,1,1,1,1,24,384]{8,7,6,5,4,3,2,1,0:T(8,128)(2,1)}, bf16[10,2,1,1,1,1,1,24,384]{8,7,6,5,4,3,2,1,0:T(8,128)(2,1)S(1)}, u32[]{:S(2)}, u32[]{:S(2)}) %collective-permute-start.19) | collective-permute-done | bytes 368672 | tf_op jit(solution)/shard_map/ppermute | solution.py:674
  243.1 2.7 %serve_8.1 = bf16[10,1,1,1,1,1,1,24,384]{8,7,6,5,4,3,2,1,0:T(8,128)(2,1)} custom-call(s32[8]{0:T(128)} %stack.35.places_ref, bf16[10,2,2,2,2,1,1,24,384]{8,7,6,5,4,3,2,1,0:T(8,128)(2,1)} %bitcast.77, bf16[10,2,2,2,2,1,1,24,384]{8,7,6,5,4,3,2,1,0:T(8,128)(2,1)} %copy-done.1, bf16[5,2,2,2,1,1,1,24,384]{8,7,6,5,4,3,2,1,0:T(8,128)(2,1)} %copy-done.6, ...), custom_call_target="tpu_custom_call" | custom-call | flops 1024 | bytes 1024 | tf_op jit(solution)/shard_map/serve_8/pallas_call | solution.py:712
  250.4 3.6 %all-to-all-done.3.back_ref = bf16[8,112,768]{2,1,0:T(8,128)(2,1)S(1)} async-done(((bf16[8,112,768]{2,1,0:T(8,128)(2,1)}), bf16[8,112,768]{2,1,0:T(8,128)(2,1)S(1)}, u32[]{:S(2)}, u32[]{:S(2)}) %all-to-all-start.3) | async-done | bytes 1376288 | tf_op jit(solution)/shard_map/all_to_all | solution.py:937
  254.3 3.0 %copy.119 = bf16[8,3,8,2,4,2,4]{6,5,4,3,2,1,0:T(2,128)(2,1)S(1)} copy(bf16[8,3,8,2,4,2,4]{0,6,5,3,1,4,2:T(4,128)(2,1)S(1)} %bitcast.117) | data formatting | bytes 49152 | tf_op jit(solution)/shard_map/transpose | solution.py:1546
  257.4 1.7 copy.120
  259.1 6.2 %tokens.1 = (bf16[24,8,4,768]{3,2,1,0:T(4,128)(2,1)}, bf16[24,8,4,768]{3,2,1,0:T(4,128)(2,1)}, bf16[8,16,1536]{2,1,0:T(8,128)(2,1)}) custom-call(bf16[8,112,768]{2,1,0:T(8,128)(2,1)} %copy-done.12, bf16[1536,768]{1,0:T(8,128)(2,1)} %w_skip_ref.3), custom_call_target="tpu_custom_call" | custom-call | flops 1024 | bytes 1024 | tf_op jit(solution)/shard_map/tokens/pallas_call | solution.py:1517
  265.2 0.9 slice.94
  266.3 0.8 fusion.13
  267.7 2.8 %serve_9.1 = (f32[24,2304]{1,0:T(8,128)}, f32[48,768]{1,0:T(8,128)}) custom-call(s32[8]{0:T(128)} %stack.35.places_ref, bf16[10,2,2,2,2,1,1,24,384]{8,7,6,5,4,3,2,1,0:T(8,128)(2,1)} %bitcast.79, bf16[10,2,2,2,2,1,1,24,384]{8,7,6,5,4,3,2,1,0:T(8,128)(2,1)} %copy-done.1, bf16[5,2,2,2,1,1,1,24,384]{8,7,6,5,4,3,2,1,0:T(8,128)(2,1)} %copy-done.6, ...), custom_call_target="tpu_custom_call" | custom-call | flops 1024 | bytes 1024 | tf_op jit(solution)/shard_map/serve_9/pallas_call | solution.py:712
  (139 shorter events, 25.3 us)
Async XLA Ops:
  6.2 8.0 %copy-start.29 = (bf16[768]{0:T(1024)(128)(2,1)S(1)}, bf16[768]{0:T(1024)(128)(2,1)}, u32[]{:S(2)}) copy-start(bf16[768]{0:T(1024)(128)(2,1)} %gain_ref.7) | copy-start | bytes 4612
  6.2 8.6 %copy-start.32 = (bf16[3,3,4,4]{3,2,1,0:T(4,128)(2,1)S(1)}, bf16[3,3,4,4]{3,2,1,0:T(4,128)(2,1)}, u32[]{:S(2)}) copy-start(bf16[3,3,4,4]{3,2,1,0:T(4,128)(2,1)} %param.50) | copy-start | bytes 868
  6.2 12.9 %copy-start.2 = (bf16[768,2304]{1,0:T(8,128)(2,1)S(1)}, bf16[768,2304]{1,0:T(8,128)(2,1)}, u32[]{:S(2)}) copy-start(bf16[768,2304]{1,0:T(8,128)(2,1)} %w_value_ref.1) | copy-start | bytes 10616836
  6.2 22.4 %all-to-all-start = ((bf16[24,32,768]{2,1,0:T(8,128)(2,1)}), bf16[24,32,768]{2,1,0:T(8,128)(2,1)}, u32[]{:S(2)}, u32[]{:S(2)}) async-start(bf16[24,32,768]{2,1,0:T(8,128)(2,1)} %get-tuple-element.104), calls=%async_computation | async-start | bytes 2359296 | tf_op jit(solution)/shard_map/all_to_all | solution.py:937
  14.8 4.3 %copy-start.30 = (f32[768]{0:T(1024)S(1)}, f32[768]{0:T(1024)}, u32[]{:S(2)}) copy-start(f32[768]{0:T(1024)} %convert_element_type.48) | copy-start | bytes 9220
  15.4 3.6 %copy-start.31 = (f32[768]{0:T(1024)S(1)}, f32[768]{0:T(1024)}, u32[]{:S(2)}) copy-start(f32[768]{0:T(1024)} %convert_element_type.47) | copy-start | bytes 9220
  16.2 2.5 copy-start.26
  16.2 3.6 %copy-start.33 = (s32[24]{0:T(128)S(1)}, s32[24]{0:T(128)}, u32[]{:S(2)}) copy-start(s32[24]{0:T(128)} %param.31) | copy-start | bytes 292
  18.4 0.6 copy-start.21
  19.2 0.6 copy-start.25
  19.9 6.2 %copy-start.18 = (f32[9,9,48,48]{3,2,1,0:T(8,128)S(1)}, f32[9,9,48,48]{3,2,1,0:T(8,128)}, u32[]{:S(2)}) copy-start(f32[9,9,48,48]{3,2,1,0:T(8,128)} %constant.83.clone) | copy-start | bytes 2239492
  24.0 2.9 %copy-start.27 = (bf16[3,2,768]{2,1,0:T(2,128)(2,1)S(1)}, bf16[3,2,768]{2,1,0:T(2,128)(2,1)}, u32[]{:S(2)}) copy-start(bf16[3,2,768]{2,1,0:T(2,128)(2,1)} %copy-done.26) | copy-start | bytes 27652
  28.6 36.3 %all-to-all-start.1 = ((bf16[24,72,768]{2,1,0:T(8,128)(2,1)}), bf16[24,72,768]{2,1,0:T(8,128)(2,1)S(1)}, u32[]{:S(2)}, u32[]{:S(2)}) async-start(bf16[24,72,768]{2,1,0:T(8,128)(2,1)} %constant_dynamic-update-slice_fusion), calls=%async_computation.1 | async-start | bytes 5308416 | tf_op jit(solution)/shard_map/all_to_all | solution.py:937
  64.9 4.2 %copy-start.3 = (bf16[24,72,768]{2,1,0:T(8,128)(2,1)}, bf16[24,72,768]{2,1,0:T(8,128)(2,1)S(1)}, u32[]{:S(2)}) copy-start(bf16[24,72,768]{2,1,0:T(8,128)(2,1)S(1)} %all-to-all-done.1) | copy-start | bytes 7962628
  85.5 21.4 %collective-permute-start = (bf16[8,2,2,2,2,1,1,24,384]{8,7,6,5,4,3,2,1,0:T(8,128)(2,1)}, bf16[8,2,2,2,2,1,1,24,384]{8,7,6,5,4,3,2,1,0:T(8,128)(2,1)}, u32[]{:S(2)}, u32[]{:S(2)}) collective-permute-start(bf16[8,2,2,2,2,1,1,24,384]{8,7,6,5,4,3,2,1,0:T(8,128)(2,1)} %bitcast.115), channel_id=1, source_target_pairs={{0,1},{1,0},{2,3},{3,2},{4,5},{5,4},{6,7},{7,6},{8,9},{9,8},{10,11... | collective-permute-start | bytes 7077896 | tf_op jit(solution)/shard_map/ppermute | solution.py:674
  106.3 20.4 %collective-permute-start.1 = (bf16[10,2,2,2,2,1,1,24,384]{8,7,6,5,4,3,2,1,0:T(8,128)(2,1)}, bf16[10,2,2,2,2,1,1,24,384]{8,7,6,5,4,3,2,1,0:T(8,128)(2,1)S(1)}, u32[]{:S(2)}, u32[]{:S(2)}) collective-permute-start(bf16[10,2,2,2,2,1,1,24,384]{8,7,6,5,4,3,2,1,0:T(8,128)(2,1)} %bitcast.113), channel_id=1, source_target_pairs={{0,1},{1,0},{2,3},{3,2},{4,5},{5,4},{6,7},{7,6},{8,9},{9,8},{10,11... | collective-permute-start | bytes 8847368 | tf_op jit(solution)/shard_map/ppermute | solution.py:674
  110.3 16.0 %collective-permute-start.2 = (bf16[4,2,2,2,1,1,1,24,384]{8,7,6,5,4,3,2,1,0:T(8,128)(2,1)}, bf16[4,2,2,2,1,1,1,24,384]{8,7,6,5,4,3,2,1,0:T(8,128)(2,1)S(1)}, u32[]{:S(2)}, u32[]{:S(2)}) collective-permute-start(bf16[4,2,2,2,1,1,1,24,384]{8,7,6,5,4,3,2,1,0:T(8,128)(2,1)} %get-tuple-element.126.rest_0_), channel_id=1, source_target_pairs={{0,2},{1,3},{2,0},{3,1},{4,6},{5,7},{6,4},{7,5},{8,10},{9,11},{10,... | collective-permute-start | bytes 1769480 | tf_op jit(solution)/shard_map/ppermute | solution.py:674
  111.3 15.4 %collective-permute-start.3 = (bf16[4,2,2,1,2,1,1,24,384]{8,7,6,5,4,3,2,1,0:T(8,128)(2,1)}, bf16[4,2,2,1,2,1,1,24,384]{8,7,6,5,4,3,2,1,0:T(8,128)(2,1)}, u32[]{:S(2)}, u32[]{:S(2)}) collective-permute-start(bf16[4,2,2,1,2,1,1,24,384]{8,7,6,5,4,3,2,1,0:T(8,128)(2,1)} %get-tuple-element.127.rest_1_), channel_id=1, source_target_pairs={{0,4},{4,0},{1,5},{5,1},{2,6},{6,2},{3,7},{7,3},{8,12},{12,8},{9,1... | collective-permute-start | bytes 1769480 | tf_op jit(solution)/shard_map/ppermute | solution.py:674
  126.3 0.8 copy-start.8
  126.7 1.7 copy-start
  128.4 8.6 %copy-start.28 = (bf16[256,48]{1,0:T(8,128)(2,1)S(1)}, bf16[256,48]{1,0:T(8,128)(2,1)}, u32[]{:S(2)}) copy-start(bf16[256,48]{1,0:T(8,128)(2,1)} %get-tuple-element.109) | copy-start | bytes 73732
  133.0 27.6 %collective-permute-start.4 = (bf16[5,2,2,2,1,1,1,24,384]{8,7,6,5,4,3,2,1,0:T(8,128)(2,1)}, bf16[5,2,2,2,1,1,1,24,384]{8,7,6,5,4,3,2,1,0:T(8,128)(2,1)S(1)}, u32[]{:S(2)}, u32[]{:S(2)}) collective-permute-start(bf16[5,2,2,2,1,1,1,24,384]{8,7,6,5,4,3,2,1,0:T(8,128)(2,1)} %get-tuple-element.131.rest_1_), channel_id=1, source_target_pairs={{0,2},{1,3},{2,0},{3,1},{4,6},{5,7},{6,4},{7,5},{8,10},{9,11},{10,... | collective-permute-start | bytes 2211848 | tf_op jit(solution)/shard_map/ppermute | solution.py:674
  133.9 26.7 %collective-permute-start.5 = (bf16[5,2,2,1,2,1,1,24,384]{8,7,6,5,4,3,2,1,0:T(8,128)(2,1)}, bf16[5,2,2,1,2,1,1,24,384]{8,7,6,5,4,3,2,1,0:T(8,128)(2,1)S(1)}, u32[]{:S(2)}, u32[]{:S(2)}) collective-permute-start(bf16[5,2,2,1,2,1,1,24,384]{8,7,6,5,4,3,2,1,0:T(8,128)(2,1)} %get-tuple-element.132.rest_2_), channel_id=1, source_target_pairs={{0,4},{4,0},{1,5},{5,1},{2,6},{6,2},{3,7},{7,3},{8,12},{12,8},{9,1... | collective-permute-start | bytes 2211848 | tf_op jit(solution)/shard_map/ppermute | solution.py:674
  135.0 25.5 %collective-permute-start.6 = (bf16[4,2,2,1,1,1,1,24,384]{8,7,6,5,4,3,2,1,0:T(8,128)(2,1)}, bf16[4,2,2,1,1,1,1,24,384]{8,7,6,5,4,3,2,1,0:T(8,128)(2,1)S(1)}, u32[]{:S(2)}, u32[]{:S(2)}) collective-permute-start(bf16[4,2,2,1,1,1,1,24,384]{8,7,6,5,4,3,2,1,0:T(8,128)(2,1)} %get-tuple-element.133.rest_3_), channel_id=1, source_target_pairs={{0,4},{4,0},{1,5},{5,1},{2,6},{6,2},{3,7},{7,3},{8,12},{12,8},{9,1... | collective-permute-start | bytes 884744 | tf_op jit(solution)/shard_map/ppermute | solution.py:674
  135.9 24.6 %collective-permute-start.7 = (bf16[4,2,2,1,1,1,1,24,384]{8,7,6,5,4,3,2,1,0:T(8,128)(2,1)}, bf16[4,2,2,1,1,1,1,24,384]{8,7,6,5,4,3,2,1,0:T(8,128)(2,1)S(1)}, u32[]{:S(2)}, u32[]{:S(2)}) collective-permute-start(bf16[4,2,2,1,1,1,1,24,384]{8,7,6,5,4,3,2,1,0:T(8,128)(2,1)} %get-tuple-element.134.rest_4_), channel_id=1, source_target_pairs={{0,2},{1,3},{2,0},{3,1},{4,6},{5,7},{6,4},{7,5},{8,10},{9,11},{10,... | collective-permute-start | bytes 884744 | tf_op jit(solution)/shard_map/ppermute | solution.py:674
  160.6 0.7 copy-start.16
  160.6 0.8 copy-start.17
  160.6 1.0 copy-start.4
  160.6 1.2 copy-start.5
  165.6 15.1 %collective-permute-start.8 = (bf16[10,2,2,2,2,1,1,24,384]{8,7,6,5,4,3,2,1,0:T(8,128)(2,1)}, bf16[10,2,2,2,2,1,1,24,384]{8,7,6,5,4,3,2,1,0:T(8,128)(2,1)S(1)}, u32[]{:S(2)}, u32[]{:S(2)}) collective-permute-start(bf16[10,2,2,2,2,1,1,24,384]{8,7,6,5,4,3,2,1,0:T(8,128)(2,1)} %bitcast.134), channel_id=1, source_target_pairs={{0,1},{1,0},{2,3},{3,2},{4,5},{5,4},{6,7},{7,6},{8,9},{9,8},{10,11... | collective-permute-start | bytes 8847368 | tf_op jit(solution)/shard_map/ppermute | solution.py:674
  165.6 15.0 %collective-permute-start.9 = (bf16[5,2,2,1,1,1,1,24,384]{8,7,6,5,4,3,2,1,0:T(8,128)(2,1)}, bf16[5,2,2,1,1,1,1,24,384]{8,7,6,5,4,3,2,1,0:T(8,128)(2,1)}, u32[]{:S(2)}, u32[]{:S(2)}) collective-permute-start(bf16[5,2,2,1,1,1,1,24,384]{8,7,6,5,4,3,2,1,0:T(8,128)(2,1)} %get-tuple-element.150.rest_0_), channel_id=1, source_target_pairs={{0,4},{4,0},{1,5},{5,1},{2,6},{6,2},{3,7},{7,3},{8,12},{12,8},{9,1... | collective-permute-start | bytes 1105928 | tf_op jit(solution)/shard_map/ppermute | solution.py:674
  167.1 13.5 %collective-permute-start.10 = (bf16[5,2,2,1,1,1,1,24,384]{8,7,6,5,4,3,2,1,0:T(8,128)(2,1)}, bf16[5,2,2,1,1,1,1,24,384]{8,7,6,5,4,3,2,1,0:T(8,128)(2,1)}, u32[]{:S(2)}, u32[]{:S(2)}) collective-permute-start(bf16[5,2,2,1,1,1,1,24,384]{8,7,6,5,4,3,2,1,0:T(8,128)(2,1)} %get-tuple-element.151.rest_1_), channel_id=1, source_target_pairs={{0,2},{1,3},{2,0},{3,1},{4,6},{5,7},{6,4},{7,5},{8,10},{9,11},{10,... | collective-permute-start | bytes 1105928 | tf_op jit(solution)/shard_map/ppermute | solution.py:674
  167.7 12.9 %collective-permute-start.11 = (bf16[8,2,1,1,1,1,1,24,384]{8,7,6,5,4,3,2,1,0:T(8,128)(2,1)}, bf16[8,2,1,1,1,1,1,24,384]{8,7,6,5,4,3,2,1,0:T(8,128)(2,1)S(1)}, u32[]{:S(2)}, u32[]{:S(2)}) collective-permute-start(bf16[8,2,1,1,1,1,1,24,384]{8,7,6,5,4,3,2,1,0:T(8,128)(2,1)} %get-tuple-element.152.rest_2_), channel_id=1, source_target_pairs={{0,8},{8,0},{16,24},{24,16},{1,9},{9,1},{17,25},{25,17},{2,10},{10... | collective-permute-start | bytes 884744 | tf_op jit(solution)/shard_map/ppermute | solution.py:674
  180.6 0.7 copy-start.13
  180.7 1.6 copy-start.1
  182.3 6.8 %copy-start.20 = (f32[32,1280]{1,0:T(8,128)S(1)}, f32[32,1280]{1,0:T(8,128)}, u32[]{:S(2)}) copy-start(f32[32,1280]{1,0:T(8,128)} %pad.9.refs_22_) | copy-start | bytes 491524
  187.0 22.0 %collective-permute-start.12 = (bf16[5,2,2,2,1,1,1,24,384]{8,7,6,5,4,3,2,1,0:T(8,128)(2,1)}, bf16[5,2,2,2,1,1,1,24,384]{8,7,6,5,4,3,2,1,0:T(8,128)(2,1)S(1)}, u32[]{:S(2)}, u32[]{:S(2)}) collective-permute-start(bf16[5,2,2,2,1,1,1,24,384]{8,7,6,5,4,3,2,1,0:T(8,128)(2,1)} %get-tuple-element.163), channel_id=1, source_target_pairs={{0,2},{1,3},{2,0},{3,1},{4,6},{5,7},{6,4},{7,5},{8,10},{9,11},{10,... | collective-permute-start | bytes 2211848 | tf_op jit(solution)/shard_map/ppermute | solution.py:674
  188.5 20.5 %collective-permute-start.13 = (bf16[5,2,2,1,2,1,1,24,384]{8,7,6,5,4,3,2,1,0:T(8,128)(2,1)}, bf16[5,2,2,1,2,1,1,24,384]{8,7,6,5,4,3,2,1,0:T(8,128)(2,1)S(1)}, u32[]{:S(2)}, u32[]{:S(2)}) collective-permute-start(bf16[5,2,2,1,2,1,1,24,384]{8,7,6,5,4,3,2,1,0:T(8,128)(2,1)} %get-tuple-element.164), channel_id=1, source_target_pairs={{0,4},{4,0},{1,5},{5,1},{2,6},{6,2},{3,7},{7,3},{8,12},{12,8},{9,1... | collective-permute-start | bytes 2211848 | tf_op jit(solution)/shard_map/ppermute | solution.py:674
  189.1 19.9 %collective-permute-start.14 = (bf16[10,2,1,1,1,1,1,24,384]{8,7,6,5,4,3,2,1,0:T(8,128)(2,1)}, bf16[10,2,1,1,1,1,1,24,384]{8,7,6,5,4,3,2,1,0:T(8,128)(2,1)S(1)}, u32[]{:S(2)}, u32[]{:S(2)}) collective-permute-start(bf16[10,2,1,1,1,1,1,24,384]{8,7,6,5,4,3,2,1,0:T(8,128)(2,1)} %get-tuple-element.165), channel_id=1, source_target_pairs={{0,8},{8,0},{16,24},{24,16},{1,9},{9,1},{17,25},{25,17},{2,10},{10... | collective-permute-start | bytes 1105928 | tf_op jit(solution)/shard_map/ppermute | solution.py:674
  189.9 18.3 %all-to-all-start.2 = ((f32[32,1,1280]{2,1,0:T(1,128)}), f32[32,1,1280]{2,1,0:T(1,128)S(1)}, u32[]{:S(2)}, u32[]{:S(2)}) async-start(f32[32,1,1280]{2,1,0:T(1,128)} %copy.117), calls=%async_computation.2 | async-start | bytes 327680 | tf_op jit(solution)/shard_map/all_to_all | solution.py:1498
  195.4 13.6 %collective-permute-start.15 = (bf16[8,1,1,1,1,1,1,24,384]{8,7,6,5,4,3,2,1,0:T(8,128)(2,1)}, bf16[8,1,1,1,1,1,1,24,384]{8,7,6,5,4,3,2,1,0:T(8,128)(2,1)S(1)}, u32[]{:S(2)}, u32[]{:S(2)}) collective-permute-start(bf16[8,1,1,1,1,1,1,24,384]{8,7,6,5,4,3,2,1,0:T(8,128)(2,1)} %get-tuple-element.166), channel_id=1, source_target_pairs={{0,16},{8,24},{16,0},{24,8},{1,17},{9,25},{17,1},{25,9},{2,18},{10... | collective-permute-start | bytes 442376 | tf_op jit(solution)/shard_map/ppermute | solution.py:674
  209.0 0.7 copy-start.24
  209.0 0.8 copy-start.10
  209.0 1.1 copy-start.6
  209.0 1.2 copy-start.7
  214.3 12.8 %collective-permute-start.16 = (bf16[5,2,2,1,1,1,1,24,384]{8,7,6,5,4,3,2,1,0:T(8,128)(2,1)}, bf16[5,2,2,1,1,1,1,24,384]{8,7,6,5,4,3,2,1,0:T(8,128)(2,1)S(1)}, u32[]{:S(2)}, u32[]{:S(2)}) collective-permute-start(bf16[5,2,2,1,1,1,1,24,384]{8,7,6,5,4,3,2,1,0:T(8,128)(2,1)} %get-tuple-element.168.refs_20_), channel_id=1, source_target_pairs={{0,4},{4,0},{1,5},{5,1},{2,6},{6,2},{3,7},{7,3},{8,12},{12,8},{9,1... | collective-permute-start | bytes 1105928 | tf_op jit(solution)/shard_map/ppermute | solution.py:674
  215.9 11.3 %collective-permute-start.17 = (bf16[5,2,2,1,1,1,1,24,384]{8,7,6,5,4,3,2,1,0:T(8,128)(2,1)}, bf16[5,2,2,1,1,1,1,24,384]{8,7,6,5,4,3,2,1,0:T(8,128)(2,1)S(1)}, u32[]{:S(2)}, u32[]{:S(2)}) collective-permute-start(bf16[5,2,2,1,1,1,1,24,384]{8,7,6,5,4,3,2,1,0:T(8,128)(2,1)} %get-tuple-element.169.refs_21_), channel_id=1, source_target_pairs={{0,2},{1,3},{2,0},{3,1},{4,6},{5,7},{6,4},{7,5},{8,10},{9,11},{10,... | collective-permute-start | bytes 1105928 | tf_op jit(solution)/shard_map/ppermute | solution.py:674
  217.3 9.8 %collective-permute-start.18 = (bf16[10,1,1,1,1,1,1,24,384]{8,7,6,5,4,3,2,1,0:T(8,128)(2,1)}, bf16[10,1,1,1,1,1,1,24,384]{8,7,6,5,4,3,2,1,0:T(8,128)(2,1)S(1)}, u32[]{:S(2)}, u32[]{:S(2)}) collective-permute-start(bf16[10,1,1,1,1,1,1,24,384]{8,7,6,5,4,3,2,1,0:T(8,128)(2,1)} %get-tuple-element.170.refs_22_), channel_id=1, source_target_pairs={{0,16},{8,24},{16,0},{24,8},{1,17},{9,25},{17,1},{25,9},{2,18},{10... | collective-permute-start | bytes 552968 | tf_op jit(solution)/shard_map/ppermute | solution.py:674
  227.1 0.7 copy-start.23
  227.1 0.8 copy-start.14
  227.1 1.0 copy-start.15
  231.6 10.7 %collective-permute-start.19 = (bf16[10,2,1,1,1,1,1,24,384]{8,7,6,5,4,3,2,1,0:T(8,128)(2,1)}, bf16[10,2,1,1,1,1,1,24,384]{8,7,6,5,4,3,2,1,0:T(8,128)(2,1)S(1)}, u32[]{:S(2)}, u32[]{:S(2)}) collective-permute-start(bf16[10,2,1,1,1,1,1,24,384]{8,7,6,5,4,3,2,1,0:T(8,128)(2,1)} %get-tuple-element.172.refs_10_), channel_id=1, source_target_pairs={{0,8},{8,0},{16,24},{24,16},{1,9},{9,1},{17,25},{25,17},{2,10},{10... | collective-permute-start | bytes 1105928 | tf_op jit(solution)/shard_map/ppermute | solution.py:674
  231.6 22.4 %all-to-all-start.3 = ((bf16[8,112,768]{2,1,0:T(8,128)(2,1)}), bf16[8,112,768]{2,1,0:T(8,128)(2,1)S(1)}, u32[]{:S(2)}, u32[]{:S(2)}) async-start(bf16[8,112,768]{2,1,0:T(8,128)(2,1)} %get-tuple-element.175.grad_ref), calls=%async_computation.3 | async-start | bytes 2752512 | tf_op jit(solution)/shard_map/all_to_all | solution.py:937
  235.2 10.6 %copy-start.19 = (f32[32,1,1280]{2,0,1:T(8,128)S(1)}, f32[32,1,1280]{2,0,1:T(8,128)}, u32[]{:S(2)}) copy-start(f32[32,1,1280]{2,0,1:T(8,128)} %copy.126) | copy-start | bytes 491524
  242.3 0.7 copy-start.11
  246.5 20.6 %collective-permute-start.20 = (bf16[10,1,1,1,1,1,1,24,384]{8,7,6,5,4,3,2,1,0:T(8,128)(2,1)}, bf16[10,1,1,1,1,1,1,24,384]{8,7,6,5,4,3,2,1,0:T(8,128)(2,1)S(1)}, u32[]{:S(2)}, u32[]{:S(2)}) collective-permute-start(bf16[10,1,1,1,1,1,1,24,384]{8,7,6,5,4,3,2,1,0:T(8,128)(2,1)} %serve_8.1), channel_id=1, source_target_pairs={{0,16},{8,24},{16,0},{24,8},{1,17},{9,25},{17,1},{25,9},{2,18},{10... | collective-permute-start | bytes 552968 | tf_op jit(solution)/shard_map/ppermute | solution.py:674
  254.0 5.0 %copy-start.12 = (bf16[8,112,768]{2,1,0:T(8,128)(2,1)}, bf16[8,112,768]{2,1,0:T(8,128)(2,1)S(1)}, u32[]{:S(2)}) copy-start(bf16[8,112,768]{2,1,0:T(8,128)(2,1)S(1)} %all-to-all-done.3.back_ref) | copy-start | bytes 4128772
  257.4 8.8 %copy-start.9 = (bf16[8,3,8,2,4,2,4]{6,5,4,3,2,1,0:T(2,128)(2,1)}, bf16[8,3,8,2,4,2,4]{6,5,4,3,2,1,0:T(2,128)(2,1)S(1)}, u32[]{:S(2)}) copy-start(bf16[8,3,8,2,4,2,4]{6,5,4,3,2,1,0:T(2,128)(2,1)S(1)} %copy.119) | copy-start | bytes 73732
  267.1 0.7 copy-start.22

commit v2 on v1

--- a/solution.py
+++ b/solution.py
@@ -58,6 +58,14 @@
     frac = (timesteps.astype(F32) / 1000.0 + 0.008) / 1.008
     kept = jnp.cos(frac * (0.5 * jnp.pi)) ** 2
     return jnp.minimum(1.0, 5.0 * (1.0 - kept) / kept)
+
+
+def staggered(stages, groups):
+    for step in range(len(stages) + len(groups) - 1):
+        for index in reversed(range(len(stages))):
+            if 0 <= step - index < len(groups):
+                for member in groups[step - index]:
+                    stages[index](member)
 
 
 def can_split(own):
@@ -120,14 +128,15 @@
     normed_ref[0] = normed
     qkv_ref[0] = dot(w_qkv_ref[...], normed, 0, 1).astype(BF)
     live = lax.broadcasted_iota(jnp.int32, (EXTRA_PAD, rows), 0) < 2
-    for head in range(HEADS):
+    def score(head):
         low = head * head_dim
         query = qkv_ref[0, low : low + head_dim, :]
         key = qkv_ref[0, width + low : width + low + head_dim, :]
         scores_ref[head] = dot(key, query, 0, 0) * scale
         scores_extra = dot(key_extra_ref[0, head], query, 1, 0) * scale
         scores_extra_ref[head] = jnp.where(live, scores_extra, -1e30)
-    for head in range(HEADS):
+
+    def weigh(head):
         scores, scores_extra = scores_ref[head], scores_extra_ref[head]
         top = jnp.maximum(
             jnp.max(scores, 0, keepdims=True), jnp.max(scores_extra, 0, keepdims=True)
@@ -137,13 +146,16 @@
         share = 1.0 / (row_sum(raised) + row_sum(raised_extra))
         probs_ref[0, head] = (raised * share).astype(BF)
         probs_extra_ref[0, head] = (raised_extra * share).astype(BF)
-    for head in range(HEADS):
+
+    def mix(head):
         low = head * head_dim
         value = qkv_ref[0, 2 * width + low : 2 * width + low + head_dim, :]
         mixed = dot(value, probs_ref[0, head], 1, 0) + dot(
             value_extra_ref[0, head], probs_extra_ref[0, head], 0, 0
         )
         mixed_ref[0, low : low + head_dim, :] = mixed.astype(BF)
+
+    staggered([score, weigh, mix], [range(low, low + 4) for low in range(0, HEADS, 4)])
     hidden1_ref[0] = hidden + (dot(mixed_ref[0], w_out_ref[...], 0, 0) + flat(b_out_ref))
 
 
@@ -936,7 +948,7 @@
     def to_items(array):
         return lax.all_to_all(array, PLANE, split_axis=0, concat_axis=0, tiled=True)
 
-    some = 8
+    some = 12
     joined_rows = 2 * local + 8
     tile_block = pl.BlockSpec((some, rows, cols, width), lambda i: (i, 0, 0, 0))
     flat_block = pl.BlockSpec((some, local, width), lambda i: (i, 0, 0))
@@ -1510,7 +1522,7 @@
     if can_split(own):
         while sum_late.orders[0]:
             after, _ = run_tasks([(sum_late, None)], after, "serve_8")
-    some_groups = max(groups // 2, 1)
+    some_groups = groups
     token_block = pl.BlockSpec(
         (some_groups * share, rows, cols, width), lambda i: (i, 0, 0, 0)
     )

time: 275 us -> 274 us (level)
  no operation moved by 1% of the time
where the time goes in v2:
time: 274 us; the launch traced here: 269 us
  Pallas kernels  148 us (54%)
  local copies, waits for them, and re-layouts  39.2 us (14%)
  starting transfers between devices  39.1 us (14%)
  waiting for transfers between devices  32.2 us (12%)
  other arithmetic  7.02 us (3%)
    pallas_call x8, Pallas kernels, serve(): pl.pallas_call(functools.partial(serve_kernel, tasks), grid_spec=pltpu.Pr...  29.6 us
    pallas_call x2, Pallas kernels, per_device(): pl.pallas_call(functools.partial(attend_back_kernel, first == 0), grid=(n...  21.5 us
    pallas_call x1, Pallas kernels, per_device(): pl.pallas_call(functools.partial(up_kernel, own), grid=(chunks + 1,), in_...  20.8 us
    ppermute x21, starting transfers between devices, swap(): return lax.ppermute(block, axis, [(i, i ^ gap) for i in range(count)])  20.7 us
    pallas_call x1, Pallas kernels, per_device(): pl.pallas_call(attend_kernel, grid=(share,), in_specs=[item_block, per_sh...  16.9 us
    ppermute x21, waiting for transfers between devices, swap(): return lax.ppermute(block, axis, [(i, i ^ gap) for i in range(count)])  16.3 us
    pallas_call x1, Pallas kernels, per_device(): pl.pallas_call(forward_kernel, grid=(chunks,), in_specs=[whole((count, wi...  14.4 us
    all_to_all x3, starting transfers between devices, to_items(): return lax.all_to_all(array, PLANE, split_axis=0, concat_axis=0, tiled=True)  12.8 us
  transfers between devices with their start and end apart: 25, of which 8 were waited for; matrix products, arithmetic and copies ran while one was open for 13% of the time, Pallas kernels for 38%

profile of v2, /device:TPU:0, one launch (start us, length us, event | category | flops | bytes accessed | tf_op | source)
XLA Modules:
  0.0 269.4 jit_solution(11025546000386403482)
XLA Ops:
  0.7 5.1 %merge.1 = (bf16[24,32,768]{2,1,0:T(8,128)(2,1)}, bf16[24,72,768]{2,1,0:T(8,128)(2,1)}) custom-call(bf16[24,8,4,768]{3,2,1,0:T(4,128)(2,1)} %tokens_ref.1, bf16[24,8,4,768]{3,2,1,0:T(4,128)(2,1)} %skip_ref.1, bf16[1536,768]{1,0:T(8,128)(2,1)} %w_skip_ref.3, bf16[768]{0:T(1024)(128)(2,1)} %b_skip_ref.1), custom_call_target="tpu_custom_call" | custom-call | flops 1024 | bytes 1024 | tf_op jit(solution)/shard_map/merge/pallas_call | solution.py:955
  5.8 5.4 %all-to-all-start = ((bf16[24,32,768]{2,1,0:T(8,128)(2,1)}), bf16[24,32,768]{2,1,0:T(8,128)(2,1)}, u32[]{:S(2)}, u32[]{:S(2)}) async-start(bf16[24,32,768]{2,1,0:T(8,128)(2,1)} %get-tuple-element.104), calls=%async_computation | async-start | bytes 2359296 | tf_op jit(solution)/shard_map/all_to_all | solution.py:949
  11.2 1.3 convert_element_type.46
  12.5 1.3 convert_element_type.48
  15.8 2.2 fusion.16
  20.0 0.8 copy.108
  22.4 1.0 copy.110
  25.6 0.9 multiply_reduce_fusion.w_conv_ref
  27.1 1.1 all-to-all-done
  28.1 3.8 %all-to-all-start.1 = ((bf16[24,72,768]{2,1,0:T(8,128)(2,1)}), bf16[24,72,768]{2,1,0:T(8,128)(2,1)S(1)}, u32[]{:S(2)}, u32[]{:S(2)}) async-start(bf16[24,72,768]{2,1,0:T(8,128)(2,1)} %constant_dynamic-update-slice_fusion), calls=%async_computation.1 | async-start | bytes 5308416 | tf_op jit(solution)/shard_map/all_to_all | solution.py:949
  32.0 16.9 %attend.1 = (bf16[3,256,768]{2,1,0:T(8,128)(2,1)}, bf16[3,2304,256]{2,1,0:T(8,128)(2,1)}, bf16[3,12,256,256]{3,2,1,0:T(8,128)(2,1)}, bf16[3,12,8,256]{3,2,1,0:T(...) custom-call(bf16[8,3,32,768]{3,2,1,0:T(8,128)(2,1)} %bitcast.1.hidden_ref, ...), custom_call_target="tpu_custom_call" | custom-call | flops 1024 | bytes 1024 | tf_op jit(solution)/shard_map/attend/pallas_call | solution.py:1023
  48.8 14.4 %forward.1 = (bf16[4,768,768]{2,1,0:T(8,128)(2,1)}, bf16[4,768,768]{2,1,0:T(8,128)(2,1)}, bf16[768,768]{1,0:T(8,128)(2,1)}, f32[768,768]{1,0:T(8,128)}) custom-call(f32[768,768]{1,0:T(8,128)} %bitcast.106, bf16[768]{0:T(1024)(128)(2,1)} %gain2_ref.3, bf16[768]{0:T(1024)(128)(2,1)} %shift2_ref.1, bf16[3072]{0:T(1024)(128)(2,1)} %b_up_ref.1, ...), custom_call_target="tpu_custom_call" | custom-call | flops 1024 | bytes 1024 | tf_op jit(solution)/shard_map/forward/pallas_call | solution.py:1074
  63.2 1.3 all-to-all-done.1
  64.5 1.8 reshape.211
  66.3 1.3 fusion.5
  68.0 0.8 copy.114.target_ref
  68.7 8.2 %turn.1 = (bf16[256,48]{1,0:T(8,128)(2,1)}, f32[768,768]{1,0:T(8,128)}, bf16[768,768]{1,0:T(8,128)(2,1)}, f32[1,48]{1,0:T(1,128)}, f32[8,768]{1,0:T(8,128)}, /*i...) custom-call(f32[768,768]{1,0:T(8,128)} %get-tuple-element.106.hidden2_ref, bf16[768]{0:T(1024)(128)(2,1)} %gainf_ref.1, ...), custom_call_target="tpu_custom_call" | custom-call | flops 1024 | bytes 1024 | tf_op jit(solution)/shard_map/turn/pallas_call | solution.py:1107
  76.9 8.1 %down_weight.1 = (bf16[8,16,24,384]{3,2,1,0:T(8,128)(2,1)}, bf16[8,16,24,384]{3,2,1,0:T(8,128)(2,1)}) custom-call(bf16[4,768,768]{2,1,0:T(8,128)(2,1)} %get-tuple-element.115.active_ref, bf16[768,768]{1,0:T(8,128)(2,1)} %get-tuple-element.111.grad_down_ref, s32[1]{0:T(128)} %bitcast.23.core_ref), custom_call_target="tpu_custom_call" | custom-call | flops 1024 | bytes 1024 | tf_op jit(solution)/shard_map/down_weight/pallas_call | solution.py:1185
  85.0 20.8 %up_weight.1 = (f32[4,8,768]{2,1,0:T(8,128)}, f32[768,768]{1,0:T(8,128)}, bf16[768,768]{1,0:T(8,128)(2,1)}, f32[8,768]{1,0:T(8,128)}, bf16[10,16,24,384]{3,2,1,0...) custom-call(bf16[4,768,768]{2,1,0:T(8,128)(2,1)} %get-tuple-element.110.slope_ref, ...), custom_call_target="tpu_custom_call" | custom-call | flops 1024 | bytes 1024 | tf_op jit(solution)/shard_map/up_weight/pallas_call | solution.py:1207
  106.4 3.4 %serve_0.1 = (bf16[4,2,2,2,1,1,1,24,384]{8,7,6,5,4,3,2,1,0:T(8,128)(2,1)}, bf16[4,2,2,1,2,1,1,24,384]{8,7,6,5,4,3,2,1,0:T(8,128)(2,1)}) custom-call(s32[8]{0:T(128)} %stack.35.places_ref, bf16[8,2,2,2,2,1,1,24,384]{8,7,6,5,4,3,2,1,0:T(8,128)(2,1)} %bitcast.91, ...), custom_call_target="tpu_custom_call" | custom-call | flops 1024 | bytes 1024 | tf_op jit(solution)/shard_map/serve_0/pallas_call | solution.py:724
  110.6 1.5 collective-permute-start.3
  112.1 13.5 %attend_back.2 = (bf16[2,2304,256]{2,1,0:T(8,128)(2,1)}, f32[2,12,8,64]{3,2,1,0:T(8,128)}, f32[2,12,8,64]{3,2,1,0:T(8,128)}, bf16[8,112,768]{2,1,0:T(8,128)(2,1)}, f32[8,768]{1,0:T(8,128)}) custom-call(bf16[8,3,32,768]{3,2,1,0:T(8,128)(2,1)} %bitcast.1.hidden_ref, f32[3,256,768]{2,1,0:T(8,128)} %bitcast.104, bf16[3,256,768]{2,1,0:T(8,128)(2,1)} %bitcast.111, ...), custom_call_target="tpu_custom_call" | custom-call | flops 1024 | bytes 1024 | tf_op jit(solution)/shard_map/attend_back/pallas_call | solution.py:1291
  126.4 1.3 copy-done
  127.7 4.6 %serve_1.1 = (bf16[5,2,2,2,1,1,1,24,384]{8,7,6,5,4,3,2,1,0:T(8,128)(2,1)}, bf16[5,2,2,1,2,1,1,24,384]{8,7,6,5,4,3,2,1,0:T(8,128)(2,1)}, bf16[4,2,2,1,1,1,1,24,38...) custom-call(s32[8]{0:T(128)} %stack.35.places_ref, ...), custom_call_target="tpu_custom_call" | custom-call | flops 1024 | bytes 1024 | tf_op jit(solution)/shard_map/serve_1/pallas_call | solution.py:724
  132.3 1.2 collective-permute-start.4
  133.5 0.8 collective-permute-start.5
  134.3 1.2 collective-permute-start.6
  135.5 0.8 collective-permute-start.7
  137.1 8.0 %attend_back.3 = (bf16[1,2304,256]{2,1,0:T(8,128)(2,1)}, f32[1,12,8,64]{3,2,1,0:T(8,128)}, f32[1,12,8,64]{3,2,1,0:T(8,128)}, bf16[8,112,768]{2,1,0:T(8,128)(2,1)}, f32[8,768]{1,0:T(8,128)}) custom-call(bf16[8,3,32,768]{3,2,1,0:T(8,128)(2,1)} %bitcast.1.hidden_ref, f32[3,256,768]{2,1,0:T(8,128)} %bitcast.105, ...), custom_call_target="tpu_custom_call", output_to_operand_aliasing={{3}: (12, {})} | custom-call | flops 1024 | bytes 1024 | tf_op jit(solution)/shard_map/attend_back/pallas_call | solution.py:1291
  145.1 3.3 %extra_back.1 = (bf16[2,24,768]{2,1,0:T(8,128)(2,1)}, bf16[24,768]{1,0:T(8,128)(2,1)}, f32[8,768]{1,0:T(8,128)}, bf16[8,112,768]{2,1,0:T(8,128)(2,1)}) custom-call(f32[24,768]{1,0:T(8,128)} %copy-done.21, bf16[768]{0:T(1024)(128)(2,1)} %gain_ref.7, bf16[768,2304]{1,0:T(8,128)(2,1)} %w_value_ref.1, ...), custom_call_target="tpu_custom_call", output_to_operand_aliasing={{3}: (12, {})} | custom-call | flops 1024 | bytes 1024 | tf_op jit(solution)/shard_map/extra_back/pallas_call | solution.py:1366
  148.4 11.4 %late_weight.1 = (bf16[10,16,24,384]{3,2,1,0:T(8,128)(2,1)}, bf16[10,16,24,384]{3,2,1,0:T(8,128)(2,1)}) custom-call(bf16[3,256,768]{2,1,0:T(8,128)(2,1)} %get-tuple-element.142.normed_ref, bf16[24,768]{1,0:T(8,128)(2,1)} %copy-done.25, bf16[2,24,768]{2,1,0:T(8,128)(2,1)} %get-tuple-element.143.pairs_ref, bf16[8,3,72,768]{3,2,1,0:T(8,128)(2,1)} %bitcast.103, ...), custom_call_target="tpu_custom_call" | custom-call | flops 1024 | bytes 1024 | tf_op jit(solution)/shard_map/late_weight/pallas_call | solution.py:1422
  161.1 3.7 %serve_2.1 = (bf16[5,2,2,1,1,1,1,24,384]{8,7,6,5,4,3,2,1,0:T(8,128)(2,1)}, bf16[5,2,2,1,1,1,1,24,384]{8,7,6,5,4,3,2,1,0:T(8,128)(2,1)}, bf16[8,2,1,1,1,1,1,24,384]{8,7,6,5,4,3,2,1,0:T(8,128)(2,1)}) custom-call(s32[8]{0:T(128)} %stack.35.places_ref, bf16[10,2,2,2,2,1,1,24,384]{8,7,6,5,4,3,2,1,0:T(8,128)(2,1)} %bitcast.83, ...), custom_call_target="tpu_custom_call" | custom-call | flops 1024 | bytes 1024 | tf_op jit(solution)/shard_map/serve_2/pallas_call | solution.py:724
  164.9 1.6 collective-permute-start.9
  167.0 2.0 collective-permute-start.11
  169.0 0.9 slice_reduce_fusion
  170.7 3.0 %pack.1 = (f32[25,768]{1,0:T(8,128)}, f32[8,128]{1,0:T(8,128)}) custom-call(f32[8,768]{1,0:T(8,128)} %get-tuple-element.154.sums_attend_ref, f32[8,768]{1,0:T(8,128)} %get-tuple-element.123.sums_in_ref.sums_up_ref, f32[8,768]{1,0:T(8,128)} %get-tuple-element.155.sums_final_ref, f32[3,48,768]{2,1,0:T(8,128)} %get-tuple-element.156.head_sum_ref, ...), custom_call_target="tpu_custom_call" | custom-call | flops 1024 | bytes 1024 | tf_op jit(solution)/shard_map/pack/pallas_call | solution.py:1470
  173.6 1.9 reshape.201
  175.6 1.2 copy.115
  176.7 0.8 copy.116
  178.2 1.0 concatenate.12
  180.6 0.9 copy-done.1
  181.6 4.7 %serve_5.1 = (bf16[5,2,2,2,1,1,1,24,384]{8,7,6,5,4,3,2,1,0:T(8,128)(2,1)}, bf16[5,2,2,1,2,1,1,24,384]{8,7,6,5,4,3,2,1,0:T(8,128)(2,1)}, bf16[10,2,1,1,1,1,1,24,3...) custom-call(s32[8]{0:T(128)} %stack.35.places_ref, ...), custom_call_target="tpu_custom_call" | custom-call | flops 1024 | bytes 1024 | tf_op jit(solution)/shard_map/serve_5/pallas_call | solution.py:724
  186.3 1.5 collective-permute-start.12
  188.3 0.8 copy.117
  189.2 5.5 %all-to-all-start.2 = ((f32[32,1,1280]{2,1,0:T(1,128)}), f32[32,1,1280]{2,1,0:T(1,128)S(1)}, u32[]{:S(2)}, u32[]{:S(2)}) async-start(f32[32,1,1280]{2,1,0:T(1,128)} %copy.117), calls=%async_computation.2 | async-start | bytes 327680 | tf_op jit(solution)/shard_map/all_to_all | solution.py:1510
  194.7 2.9 %collective-permute-start.15 = (bf16[8,1,1,1,1,1,1,24,384]{8,7,6,5,4,3,2,1,0:T(8,128)(2,1)}, bf16[8,1,1,1,1,1,1,24,384]{8,7,6,5,4,3,2,1,0:T(8,128)(2,1)S(1)}, u32[]{:S(2)}, u32[]{:S(2)}) collective-permute-start(bf16[8,1,1,1,1,1,1,24,384]{8,7,6,5,4,3,2,1,0:T(8,128)(2,1)} %get-tuple-element.166), channel_id=1, source_target_pairs={{0,16},{8,24},{16,0},{24,8},{1,17},{9,25},{17,1},{25,9},{2,18},{10... | collective-permute-start | bytes 442376 | tf_op jit(solution)/shard_map/ppermute | solution.py:686
  197.5 9.9 %all-to-all-done.2 = f32[32,1,1280]{2,1,0:T(1,128)S(1)} async-done(((f32[32,1,1280]{2,1,0:T(1,128)}), f32[32,1,1280]{2,1,0:T(1,128)S(1)}, u32[]{:S(2)}, u32[]{:S(2)}) %all-to-all-start.2) | async-done | bytes 163872 | tf_op jit(solution)/shard_map/all_to_all | solution.py:1510
  209.6 4.0 %serve_6.1 = (bf16[5,2,2,1,1,1,1,24,384]{8,7,6,5,4,3,2,1,0:T(8,128)(2,1)}, bf16[5,2,2,1,1,1,1,24,384]{8,7,6,5,4,3,2,1,0:T(8,128)(2,1)}, bf16[10,1,1,1,1,1,1,24,384]{8,7,6,5,4,3,2,1,0:T(8,128)(2,1)}, f32[96,768]{1,0:T(8,128)}) custom-call(s32[8]{0:T(128)} %stack.35.places_ref, bf16[10,2,2,2,2,1,1,24,384]{8,7,6,5,4,3,2,1,0:T(8,128)(2,1)} %bitcast.73, ...), custom_call_target="tpu_custom_call" | custom-call | flops 1024 | bytes 1024 | tf_op jit(solution)/shard_map/serve_6/pallas_call | solution.py:724
  213.6 1.5 collective-permute-start.16
  215.1 1.5 collective-permute-start.17
  216.6 1.2 collective-permute-start.18
  217.8 8.6 %collective-permute-done.18.refs_13_.refs_19_ = bf16[10,1,1,1,1,1,1,24,384]{8,7,6,5,4,3,2,1,0:T(8,128)(2,1)S(1)} collective-permute-done((bf16[10,1,1,1,1,1,1,24,384]{8,7,6,5,4,3,2,1,0:T(8,128)(2,1)}, bf16[10,1,1,1,1,1,1,24,384]{8,7,6,5,4,3,2,1,0:T(8,128)(2,1)S(1)}, u32[]{:S(2)}, u32[]{:S(2)}) %collective-permute-start.18) | collective-permute-done | bytes 184352 | tf_op jit(solution)/shard_map/ppermute | solution.py:686
  227.4 3.5 %serve_7.1 = (bf16[10,2,1,1,1,1,1,24,384]{8,7,6,5,4,3,2,1,0:T(8,128)(2,1)}, f32[24,3072]{1,0:T(8,128)}, f32[24,768]{1,0:T(8,128)}) custom-call(s32[8]{0:T(128)} %stack.35.places_ref, bf16[10,2,2,2,2,1,1,24,384]{8,7,6,5,4,3,2,1,0:T(8,128)(2,1)} %bitcast.75, bf16[10,2,2,2,2,1,1,24,384]{8,7,6,5,4,3,2,1,0:T(8,128)(2,1)} %copy-done.1, ...), custom_call_target="tpu_custom_call" | custom-call | flops 1024 | bytes 1024 | tf_op jit(solution)/shard_map/serve_7/pallas_call | solution.py:724
  230.9 3.6 %all-to-all-start.3 = ((bf16[8,112,768]{2,1,0:T(8,128)(2,1)}), bf16[8,112,768]{2,1,0:T(8,128)(2,1)S(1)}, u32[]{:S(2)}, u32[]{:S(2)}) async-start(bf16[8,112,768]{2,1,0:T(8,128)(2,1)} %get-tuple-element.175.grad_ref), calls=%async_computation.3 | async-start | bytes 2752512 | tf_op jit(solution)/shard_map/all_to_all | solution.py:949
  234.5 7.1 %collective-permute-done.19.refs_4_.refs_9_.refs_10_ = bf16[10,2,1,1,1,1,1,24,384]{8,7,6,5,4,3,2,1,0:T(8,128)(2,1)S(1)} collective-permute-done((bf16[10,2,1,1,1,1,1,24,384]{8,7,6,5,4,3,2,1,0:T(8,128)(2,1)}, bf16[10,2,1,1,1,1,1,24,384]{8,7,6,5,4,3,2,1,0:T(8,128)(2,1)S(1)}, u32[]{:S(2)}, u32[]{:S(2)}) %collective-permute-start.19) | collective-permute-done | bytes 368672 | tf_op jit(solution)/shard_map/ppermute | solution.py:686
  241.6 0.7 copy-done.11
  242.3 2.7 %serve_8.1 = bf16[10,1,1,1,1,1,1,24,384]{8,7,6,5,4,3,2,1,0:T(8,128)(2,1)} custom-call(s32[8]{0:T(128)} %stack.35.places_ref, bf16[10,2,2,2,2,1,1,24,384]{8,7,6,5,4,3,2,1,0:T(8,128)(2,1)} %bitcast.77, bf16[10,2,2,2,2,1,1,24,384]{8,7,6,5,4,3,2,1,0:T(8,128)(2,1)} %copy-done.1, bf16[5,2,2,2,1,1,1,24,384]{8,7,6,5,4,3,2,1,0:T(8,128)(2,1)} %copy-done.6, ...), custom_call_target="tpu_custom_call" | custom-call | flops 1024 | bytes 1024 | tf_op jit(solution)/shard_map/serve_8/pallas_call | solution.py:724
  249.7 3.6 %all-to-all-done.3.back_ref = bf16[8,112,768]{2,1,0:T(8,128)(2,1)S(1)} async-done(((bf16[8,112,768]{2,1,0:T(8,128)(2,1)}), bf16[8,112,768]{2,1,0:T(8,128)(2,1)S(1)}, u32[]{:S(2)}, u32[]{:S(2)}) %all-to-all-start.3) | async-done | bytes 1376288 | tf_op jit(solution)/shard_map/all_to_all | solution.py:949
  253.6 3.0 %copy.119 = bf16[8,3,8,2,4,2,4]{6,5,4,3,2,1,0:T(2,128)(2,1)S(1)} copy(bf16[8,3,8,2,4,2,4]{0,6,5,3,1,4,2:T(4,128)(2,1)S(1)} %bitcast.117) | data formatting | bytes 49152 | tf_op jit(solution)/shard_map/transpose | solution.py:1558
  256.6 1.7 copy.120
  258.3 5.6 %tokens.1 = (bf16[24,8,4,768]{3,2,1,0:T(4,128)(2,1)}, bf16[24,8,4,768]{3,2,1,0:T(4,128)(2,1)}, bf16[8,16,1536]{2,1,0:T(8,128)(2,1)}) custom-call(bf16[8,112,768]{2,1,0:T(8,128)(2,1)} %copy-done.12, bf16[1536,768]{1,0:T(8,128)(2,1)} %w_skip_ref.3), custom_call_target="tpu_custom_call" | custom-call | flops 1024 | bytes 1024 | tf_op jit(solution)/shard_map/tokens/pallas_call | solution.py:1529
  263.9 0.9 slice.94
  265.0 0.8 fusion.13
  266.4 2.8 %serve_9.1 = (f32[24,2304]{1,0:T(8,128)}, f32[48,768]{1,0:T(8,128)}) custom-call(s32[8]{0:T(128)} %stack.35.places_ref, bf16[10,2,2,2,2,1,1,24,384]{8,7,6,5,4,3,2,1,0:T(8,128)(2,1)} %bitcast.79, bf16[10,2,2,2,2,1,1,24,384]{8,7,6,5,4,3,2,1,0:T(8,128)(2,1)} %copy-done.1, bf16[5,2,2,2,1,1,1,24,384]{8,7,6,5,4,3,2,1,0:T(8,128)(2,1)} %copy-done.6, ...), custom_call_target="tpu_custom_call" | custom-call | flops 1024 | bytes 1024 | tf_op jit(solution)/shard_map/serve_9/pallas_call | solution.py:724
  (139 shorter events, 25.2 us)
Async XLA Ops:
  5.7 8.0 %copy-start.29 = (bf16[768]{0:T(1024)(128)(2,1)S(1)}, bf16[768]{0:T(1024)(128)(2,1)}, u32[]{:S(2)}) copy-start(bf16[768]{0:T(1024)(128)(2,1)} %gain_ref.7) | copy-start | bytes 4612
  5.8 8.6 %copy-start.32 = (bf16[3,3,4,4]{3,2,1,0:T(4,128)(2,1)S(1)}, bf16[3,3,4,4]{3,2,1,0:T(4,128)(2,1)}, u32[]{:S(2)}) copy-start(bf16[3,3,4,4]{3,2,1,0:T(4,128)(2,1)} %param.50) | copy-start | bytes 868
  5.8 13.0 %copy-start.2 = (bf16[768,2304]{1,0:T(8,128)(2,1)S(1)}, bf16[768,2304]{1,0:T(8,128)(2,1)}, u32[]{:S(2)}) copy-start(bf16[768,2304]{1,0:T(8,128)(2,1)} %w_value_ref.1) | copy-start | bytes 10616836
  5.8 22.4 %all-to-all-start = ((bf16[24,32,768]{2,1,0:T(8,128)(2,1)}), bf16[24,32,768]{2,1,0:T(8,128)(2,1)}, u32[]{:S(2)}, u32[]{:S(2)}) async-start(bf16[24,32,768]{2,1,0:T(8,128)(2,1)} %get-tuple-element.104), calls=%async_computation | async-start | bytes 2359296 | tf_op jit(solution)/shard_map/all_to_all | solution.py:949
  14.4 4.3 %copy-start.30 = (f32[768]{0:T(1024)S(1)}, f32[768]{0:T(1024)}, u32[]{:S(2)}) copy-start(f32[768]{0:T(1024)} %convert_element_type.48) | copy-start | bytes 9220
  15.0 3.6 %copy-start.31 = (f32[768]{0:T(1024)S(1)}, f32[768]{0:T(1024)}, u32[]{:S(2)}) copy-start(f32[768]{0:T(1024)} %convert_element_type.47) | copy-start | bytes 9220
  15.7 2.5 copy-start.26
  15.7 3.6 %copy-start.33 = (s32[24]{0:T(128)S(1)}, s32[24]{0:T(128)}, u32[]{:S(2)}) copy-start(s32[24]{0:T(128)} %param.31) | copy-start | bytes 292
  18.0 0.6 copy-start.21
  18.7 0.6 copy-start.25
  19.4 6.2 %copy-start.18 = (f32[9,9,48,48]{3,2,1,0:T(8,128)S(1)}, f32[9,9,48,48]{3,2,1,0:T(8,128)}, u32[]{:S(2)}) copy-start(f32[9,9,48,48]{3,2,1,0:T(8,128)} %constant.83.clone) | copy-start | bytes 2239492
  23.6 2.9 %copy-start.27 = (bf16[3,2,768]{2,1,0:T(2,128)(2,1)S(1)}, bf16[3,2,768]{2,1,0:T(2,128)(2,1)}, u32[]{:S(2)}) copy-start(bf16[3,2,768]{2,1,0:T(2,128)(2,1)} %copy-done.26) | copy-start | bytes 27652
  28.1 36.3 %all-to-all-start.1 = ((bf16[24,72,768]{2,1,0:T(8,128)(2,1)}), bf16[24,72,768]{2,1,0:T(8,128)(2,1)S(1)}, u32[]{:S(2)}, u32[]{:S(2)}) async-start(bf16[24,72,768]{2,1,0:T(8,128)(2,1)} %constant_dynamic-update-slice_fusion), calls=%async_computation.1 | async-start | bytes 5308416 | tf_op jit(solution)/shard_map/all_to_all | solution.py:949
  64.5 4.2 %copy-start.3 = (bf16[24,72,768]{2,1,0:T(8,128)(2,1)}, bf16[24,72,768]{2,1,0:T(8,128)(2,1)S(1)}, u32[]{:S(2)}) copy-start(bf16[24,72,768]{2,1,0:T(8,128)(2,1)S(1)} %all-to-all-done.1) | copy-start | bytes 7962628
  85.0 21.4 %collective-permute-start = (bf16[8,2,2,2,2,1,1,24,384]{8,7,6,5,4,3,2,1,0:T(8,128)(2,1)}, bf16[8,2,2,2,2,1,1,24,384]{8,7,6,5,4,3,2,1,0:T(8,128)(2,1)}, u32[]{:S(2)}, u32[]{:S(2)}) collective-permute-start(bf16[8,2,2,2,2,1,1,24,384]{8,7,6,5,4,3,2,1,0:T(8,128)(2,1)} %bitcast.115), channel_id=1, source_target_pairs={{0,1},{1,0},{2,3},{3,2},{4,5},{5,4},{6,7},{7,6},{8,9},{9,8},{10,11... | collective-permute-start | bytes 7077896 | tf_op jit(solution)/shard_map/ppermute | solution.py:686
  105.9 20.1 %collective-permute-start.1 = (bf16[10,2,2,2,2,1,1,24,384]{8,7,6,5,4,3,2,1,0:T(8,128)(2,1)}, bf16[10,2,2,2,2,1,1,24,384]{8,7,6,5,4,3,2,1,0:T(8,128)(2,1)S(1)}, u32[]{:S(2)}, u32[]{:S(2)}) collective-permute-start(bf16[10,2,2,2,2,1,1,24,384]{8,7,6,5,4,3,2,1,0:T(8,128)(2,1)} %bitcast.113), channel_id=1, source_target_pairs={{0,1},{1,0},{2,3},{3,2},{4,5},{5,4},{6,7},{7,6},{8,9},{9,8},{10,11... | collective-permute-start | bytes 8847368 | tf_op jit(solution)/shard_map/ppermute | solution.py:686
  109.9 15.7 %collective-permute-start.2 = (bf16[4,2,2,2,1,1,1,24,384]{8,7,6,5,4,3,2,1,0:T(8,128)(2,1)}, bf16[4,2,2,2,1,1,1,24,384]{8,7,6,5,4,3,2,1,0:T(8,128)(2,1)S(1)}, u32[]{:S(2)}, u32[]{:S(2)}) collective-permute-start(bf16[4,2,2,2,1,1,1,24,384]{8,7,6,5,4,3,2,1,0:T(8,128)(2,1)} %get-tuple-element.126.rest_0_), channel_id=1, source_target_pairs={{0,2},{1,3},{2,0},{3,1},{4,6},{5,7},{6,4},{7,5},{8,10},{9,11},{10,... | collective-permute-start | bytes 1769480 | tf_op jit(solution)/shard_map/ppermute | solution.py:686
  110.6 15.4 %collective-permute-start.3 = (bf16[4,2,2,1,2,1,1,24,384]{8,7,6,5,4,3,2,1,0:T(8,128)(2,1)}, bf16[4,2,2,1,2,1,1,24,384]{8,7,6,5,4,3,2,1,0:T(8,128)(2,1)}, u32[]{:S(2)}, u32[]{:S(2)}) collective-permute-start(bf16[4,2,2,1,2,1,1,24,384]{8,7,6,5,4,3,2,1,0:T(8,128)(2,1)} %get-tuple-element.127.rest_1_), channel_id=1, source_target_pairs={{0,4},{4,0},{1,5},{5,1},{2,6},{6,2},{3,7},{7,3},{8,12},{12,8},{9,1... | collective-permute-start | bytes 1769480 | tf_op jit(solution)/shard_map/ppermute | solution.py:686
  125.6 0.8 copy-start.8
  126.0 1.7 copy-start
  127.7 8.6 %copy-start.28 = (bf16[256,48]{1,0:T(8,128)(2,1)S(1)}, bf16[256,48]{1,0:T(8,128)(2,1)}, u32[]{:S(2)}) copy-start(bf16[256,48]{1,0:T(8,128)(2,1)} %get-tuple-element.109) | copy-start | bytes 73732
  132.3 27.6 %collective-permute-start.4 = (bf16[5,2,2,2,1,1,1,24,384]{8,7,6,5,4,3,2,1,0:T(8,128)(2,1)}, bf16[5,2,2,2,1,1,1,24,384]{8,7,6,5,4,3,2,1,0:T(8,128)(2,1)S(1)}, u32[]{:S(2)}, u32[]{:S(2)}) collective-permute-start(bf16[5,2,2,2,1,1,1,24,384]{8,7,6,5,4,3,2,1,0:T(8,128)(2,1)} %get-tuple-element.131.rest_1_), channel_id=1, source_target_pairs={{0,2},{1,3},{2,0},{3,1},{4,6},{5,7},{6,4},{7,5},{8,10},{9,11},{10,... | collective-permute-start | bytes 2211848 | tf_op jit(solution)/shard_map/ppermute | solution.py:686
  133.5 26.4 %collective-permute-start.5 = (bf16[5,2,2,1,2,1,1,24,384]{8,7,6,5,4,3,2,1,0:T(8,128)(2,1)}, bf16[5,2,2,1,2,1,1,24,384]{8,7,6,5,4,3,2,1,0:T(8,128)(2,1)S(1)}, u32[]{:S(2)}, u32[]{:S(2)}) collective-permute-start(bf16[5,2,2,1,2,1,1,24,384]{8,7,6,5,4,3,2,1,0:T(8,128)(2,1)} %get-tuple-element.132.rest_2_), channel_id=1, source_target_pairs={{0,4},{4,0},{1,5},{5,1},{2,6},{6,2},{3,7},{7,3},{8,12},{12,8},{9,1... | collective-permute-start | bytes 2211848 | tf_op jit(solution)/shard_map/ppermute | solution.py:686
  134.3 25.5 %collective-permute-start.6 = (bf16[4,2,2,1,1,1,1,24,384]{8,7,6,5,4,3,2,1,0:T(8,128)(2,1)}, bf16[4,2,2,1,1,1,1,24,384]{8,7,6,5,4,3,2,1,0:T(8,128)(2,1)S(1)}, u32[]{:S(2)}, u32[]{:S(2)}) collective-permute-start(bf16[4,2,2,1,1,1,1,24,384]{8,7,6,5,4,3,2,1,0:T(8,128)(2,1)} %get-tuple-element.133.rest_3_), channel_id=1, source_target_pairs={{0,4},{4,0},{1,5},{5,1},{2,6},{6,2},{3,7},{7,3},{8,12},{12,8},{9,1... | collective-permute-start | bytes 884744 | tf_op jit(solution)/shard_map/ppermute | solution.py:686
  135.5 24.4 %collective-permute-start.7 = (bf16[4,2,2,1,1,1,1,24,384]{8,7,6,5,4,3,2,1,0:T(8,128)(2,1)}, bf16[4,2,2,1,1,1,1,24,384]{8,7,6,5,4,3,2,1,0:T(8,128)(2,1)S(1)}, u32[]{:S(2)}, u32[]{:S(2)}) collective-permute-start(bf16[4,2,2,1,1,1,1,24,384]{8,7,6,5,4,3,2,1,0:T(8,128)(2,1)} %get-tuple-element.134.rest_4_), channel_id=1, source_target_pairs={{0,2},{1,3},{2,0},{3,1},{4,6},{5,7},{6,4},{7,5},{8,10},{9,11},{10,... | collective-permute-start | bytes 884744 | tf_op jit(solution)/shard_map/ppermute | solution.py:686
  159.8 0.7 copy-start.16
  159.9 0.8 copy-start.17
  159.9 1.0 copy-start.4
  159.9 1.2 copy-start.5
  164.9 15.0 %collective-permute-start.8 = (bf16[10,2,2,2,2,1,1,24,384]{8,7,6,5,4,3,2,1,0:T(8,128)(2,1)}, bf16[10,2,2,2,2,1,1,24,384]{8,7,6,5,4,3,2,1,0:T(8,128)(2,1)S(1)}, u32[]{:S(2)}, u32[]{:S(2)}) collective-permute-start(bf16[10,2,2,2,2,1,1,24,384]{8,7,6,5,4,3,2,1,0:T(8,128)(2,1)} %bitcast.134), channel_id=1, source_target_pairs={{0,1},{1,0},{2,3},{3,2},{4,5},{5,4},{6,7},{7,6},{8,9},{9,8},{10,11... | collective-permute-start | bytes 8847368 | tf_op jit(solution)/shard_map/ppermute | solution.py:686
  164.9 15.0 %collective-permute-start.9 = (bf16[5,2,2,1,1,1,1,24,384]{8,7,6,5,4,3,2,1,0:T(8,128)(2,1)}, bf16[5,2,2,1,1,1,1,24,384]{8,7,6,5,4,3,2,1,0:T(8,128)(2,1)}, u32[]{:S(2)}, u32[]{:S(2)}) collective-permute-start(bf16[5,2,2,1,1,1,1,24,384]{8,7,6,5,4,3,2,1,0:T(8,128)(2,1)} %get-tuple-element.150.rest_0_), channel_id=1, source_target_pairs={{0,4},{4,0},{1,5},{5,1},{2,6},{6,2},{3,7},{7,3},{8,12},{12,8},{9,1... | collective-permute-start | bytes 1105928 | tf_op jit(solution)/shard_map/ppermute | solution.py:686
  166.4 13.5 %collective-permute-start.10 = (bf16[5,2,2,1,1,1,1,24,384]{8,7,6,5,4,3,2,1,0:T(8,128)(2,1)}, bf16[5,2,2,1,1,1,1,24,384]{8,7,6,5,4,3,2,1,0:T(8,128)(2,1)}, u32[]{:S(2)}, u32[]{:S(2)}) collective-permute-start(bf16[5,2,2,1,1,1,1,24,384]{8,7,6,5,4,3,2,1,0:T(8,128)(2,1)} %get-tuple-element.151.rest_1_), channel_id=1, source_target_pairs={{0,2},{1,3},{2,0},{3,1},{4,6},{5,7},{6,4},{7,5},{8,10},{9,11},{10,... | collective-permute-start | bytes 1105928 | tf_op jit(solution)/shard_map/ppermute | solution.py:686
  167.0 12.9 %collective-permute-start.11 = (bf16[8,2,1,1,1,1,1,24,384]{8,7,6,5,4,3,2,1,0:T(8,128)(2,1)}, bf16[8,2,1,1,1,1,1,24,384]{8,7,6,5,4,3,2,1,0:T(8,128)(2,1)S(1)}, u32[]{:S(2)}, u32[]{:S(2)}) collective-permute-start(bf16[8,2,1,1,1,1,1,24,384]{8,7,6,5,4,3,2,1,0:T(8,128)(2,1)} %get-tuple-element.152.rest_2_), channel_id=1, source_target_pairs={{0,8},{8,0},{16,24},{24,16},{1,9},{9,1},{17,25},{25,17},{2,10},{10... | collective-permute-start | bytes 884744 | tf_op jit(solution)/shard_map/ppermute | solution.py:686
  179.9 0.7 copy-start.13
  179.9 1.6 copy-start.1
  181.6 6.8 %copy-start.20 = (f32[32,1280]{1,0:T(8,128)S(1)}, f32[32,1280]{1,0:T(8,128)}, u32[]{:S(2)}) copy-start(f32[32,1280]{1,0:T(8,128)} %pad.9.refs_22_) | copy-start | bytes 491524
  186.3 22.0 %collective-permute-start.12 = (bf16[5,2,2,2,1,1,1,24,384]{8,7,6,5,4,3,2,1,0:T(8,128)(2,1)}, bf16[5,2,2,2,1,1,1,24,384]{8,7,6,5,4,3,2,1,0:T(8,128)(2,1)S(1)}, u32[]{:S(2)}, u32[]{:S(2)}) collective-permute-start(bf16[5,2,2,2,1,1,1,24,384]{8,7,6,5,4,3,2,1,0:T(8,128)(2,1)} %get-tuple-element.163), channel_id=1, source_target_pairs={{0,2},{1,3},{2,0},{3,1},{4,6},{5,7},{6,4},{7,5},{8,10},{9,11},{10,... | collective-permute-start | bytes 2211848 | tf_op jit(solution)/shard_map/ppermute | solution.py:686
  187.8 20.5 %collective-permute-start.13 = (bf16[5,2,2,1,2,1,1,24,384]{8,7,6,5,4,3,2,1,0:T(8,128)(2,1)}, bf16[5,2,2,1,2,1,1,24,384]{8,7,6,5,4,3,2,1,0:T(8,128)(2,1)S(1)}, u32[]{:S(2)}, u32[]{:S(2)}) collective-permute-start(bf16[5,2,2,1,2,1,1,24,384]{8,7,6,5,4,3,2,1,0:T(8,128)(2,1)} %get-tuple-element.164), channel_id=1, source_target_pairs={{0,4},{4,0},{1,5},{5,1},{2,6},{6,2},{3,7},{7,3},{8,12},{12,8},{9,1... | collective-permute-start | bytes 2211848 | tf_op jit(solution)/shard_map/ppermute | solution.py:686
  188.3 20.0 %collective-permute-start.14 = (bf16[10,2,1,1,1,1,1,24,384]{8,7,6,5,4,3,2,1,0:T(8,128)(2,1)}, bf16[10,2,1,1,1,1,1,24,384]{8,7,6,5,4,3,2,1,0:T(8,128)(2,1)S(1)}, u32[]{:S(2)}, u32[]{:S(2)}) collective-permute-start(bf16[10,2,1,1,1,1,1,24,384]{8,7,6,5,4,3,2,1,0:T(8,128)(2,1)} %get-tuple-element.165), channel_id=1, source_target_pairs={{0,8},{8,0},{16,24},{24,16},{1,9},{9,1},{17,25},{25,17},{2,10},{10... | collective-permute-start | bytes 1105928 | tf_op jit(solution)/shard_map/ppermute | solution.py:686
  189.2 18.3 %all-to-all-start.2 = ((f32[32,1,1280]{2,1,0:T(1,128)}), f32[32,1,1280]{2,1,0:T(1,128)S(1)}, u32[]{:S(2)}, u32[]{:S(2)}) async-start(f32[32,1,1280]{2,1,0:T(1,128)} %copy.117), calls=%async_computation.2 | async-start | bytes 327680 | tf_op jit(solution)/shard_map/all_to_all | solution.py:1510
  194.7 13.6 %collective-permute-start.15 = (bf16[8,1,1,1,1,1,1,24,384]{8,7,6,5,4,3,2,1,0:T(8,128)(2,1)}, bf16[8,1,1,1,1,1,1,24,384]{8,7,6,5,4,3,2,1,0:T(8,128)(2,1)S(1)}, u32[]{:S(2)}, u32[]{:S(2)}) collective-permute-start(bf16[8,1,1,1,1,1,1,24,384]{8,7,6,5,4,3,2,1,0:T(8,128)(2,1)} %get-tuple-element.166), channel_id=1, source_target_pairs={{0,16},{8,24},{16,0},{24,8},{1,17},{9,25},{17,1},{25,9},{2,18},{10... | collective-permute-start | bytes 442376 | tf_op jit(solution)/shard_map/ppermute | solution.py:686
  208.3 0.7 copy-start.24
  208.3 0.8 copy-start.10
  208.3 1.1 copy-start.6
  208.3 1.2 copy-start.7
  213.6 12.8 %collective-permute-start.16 = (bf16[5,2,2,1,1,1,1,24,384]{8,7,6,5,4,3,2,1,0:T(8,128)(2,1)}, bf16[5,2,2,1,1,1,1,24,384]{8,7,6,5,4,3,2,1,0:T(8,128)(2,1)S(1)}, u32[]{:S(2)}, u32[]{:S(2)}) collective-permute-start(bf16[5,2,2,1,1,1,1,24,384]{8,7,6,5,4,3,2,1,0:T(8,128)(2,1)} %get-tuple-element.168.refs_20_), channel_id=1, source_target_pairs={{0,4},{4,0},{1,5},{5,1},{2,6},{6,2},{3,7},{7,3},{8,12},{12,8},{9,1... | collective-permute-start | bytes 1105928 | tf_op jit(solution)/shard_map/ppermute | solution.py:686
  215.1 11.3 %collective-permute-start.17 = (bf16[5,2,2,1,1,1,1,24,384]{8,7,6,5,4,3,2,1,0:T(8,128)(2,1)}, bf16[5,2,2,1,1,1,1,24,384]{8,7,6,5,4,3,2,1,0:T(8,128)(2,1)S(1)}, u32[]{:S(2)}, u32[]{:S(2)}) collective-permute-start(bf16[5,2,2,1,1,1,1,24,384]{8,7,6,5,4,3,2,1,0:T(8,128)(2,1)} %get-tuple-element.169.refs_21_), channel_id=1, source_target_pairs={{0,2},{1,3},{2,0},{3,1},{4,6},{5,7},{6,4},{7,5},{8,10},{9,11},{10,... | collective-permute-start | bytes 1105928 | tf_op jit(solution)/shard_map/ppermute | solution.py:686
  216.6 9.8 %collective-permute-start.18 = (bf16[10,1,1,1,1,1,1,24,384]{8,7,6,5,4,3,2,1,0:T(8,128)(2,1)}, bf16[10,1,1,1,1,1,1,24,384]{8,7,6,5,4,3,2,1,0:T(8,128)(2,1)S(1)}, u32[]{:S(2)}, u32[]{:S(2)}) collective-permute-start(bf16[10,1,1,1,1,1,1,24,384]{8,7,6,5,4,3,2,1,0:T(8,128)(2,1)} %get-tuple-element.170.refs_22_), channel_id=1, source_target_pairs={{0,16},{8,24},{16,0},{24,8},{1,17},{9,25},{17,1},{25,9},{2,18},{10... | collective-permute-start | bytes 552968 | tf_op jit(solution)/shard_map/ppermute | solution.py:686
  226.4 0.7 copy-start.23
  226.4 0.8 copy-start.14
  226.4 1.0 copy-start.15
  230.9 10.7 %collective-permute-start.19 = (bf16[10,2,1,1,1,1,1,24,384]{8,7,6,5,4,3,2,1,0:T(8,128)(2,1)}, bf16[10,2,1,1,1,1,1,24,384]{8,7,6,5,4,3,2,1,0:T(8,128)(2,1)S(1)}, u32[]{:S(2)}, u32[]{:S(2)}) collective-permute-start(bf16[10,2,1,1,1,1,1,24,384]{8,7,6,5,4,3,2,1,0:T(8,128)(2,1)} %get-tuple-element.172.refs_10_), channel_id=1, source_target_pairs={{0,8},{8,0},{16,24},{24,16},{1,9},{9,1},{17,25},{25,17},{2,10},{10... | collective-permute-start | bytes 1105928 | tf_op jit(solution)/shard_map/ppermute | solution.py:686
  230.9 22.4 %all-to-all-start.3 = ((bf16[8,112,768]{2,1,0:T(8,128)(2,1)}), bf16[8,112,768]{2,1,0:T(8,128)(2,1)S(1)}, u32[]{:S(2)}, u32[]{:S(2)}) async-start(bf16[8,112,768]{2,1,0:T(8,128)(2,1)} %get-tuple-element.175.grad_ref), calls=%async_computation.3 | async-start | bytes 2752512 | tf_op jit(solution)/shard_map/all_to_all | solution.py:949
  234.5 10.6 %copy-start.19 = (f32[32,1,1280]{2,0,1:T(8,128)S(1)}, f32[32,1,1280]{2,0,1:T(8,128)}, u32[]{:S(2)}) copy-start(f32[32,1,1280]{2,0,1:T(8,128)} %copy.126) | copy-start | bytes 491524
  241.6 0.7 copy-start.11
  245.7 20.0 %collective-permute-start.20 = (bf16[10,1,1,1,1,1,1,24,384]{8,7,6,5,4,3,2,1,0:T(8,128)(2,1)}, bf16[10,1,1,1,1,1,1,24,384]{8,7,6,5,4,3,2,1,0:T(8,128)(2,1)S(1)}, u32[]{:S(2)}, u32[]{:S(2)}) collective-permute-start(bf16[10,1,1,1,1,1,1,24,384]{8,7,6,5,4,3,2,1,0:T(8,128)(2,1)} %serve_8.1), channel_id=1, source_target_pairs={{0,16},{8,24},{16,0},{24,8},{1,17},{9,25},{17,1},{25,9},{2,18},{10... | collective-permute-start | bytes 552968 | tf_op jit(solution)/shard_map/ppermute | solution.py:686
  253.3 5.0 %copy-start.12 = (bf16[8,112,768]{2,1,0:T(8,128)(2,1)}, bf16[8,112,768]{2,1,0:T(8,128)(2,1)S(1)}, u32[]{:S(2)}) copy-start(bf16[8,112,768]{2,1,0:T(8,128)(2,1)S(1)} %all-to-all-done.3.back_ref) | copy-start | bytes 4128772
  256.6 8.2 %copy-start.9 = (bf16[8,3,8,2,4,2,4]{6,5,4,3,2,1,0:T(2,128)(2,1)}, bf16[8,3,8,2,4,2,4]{6,5,4,3,2,1,0:T(2,128)(2,1)S(1)}, u32[]{:S(2)}) copy-start(bf16[8,3,8,2,4,2,4]{6,5,4,3,2,1,0:T(2,128)(2,1)S(1)} %copy.119) | copy-start | bytes 73732
  265.8 0.7 copy-start.22
